TPU v7x, 32 devices: a whole 2x2x4 slice. The times are simulated.
32 devices in a mesh: seq: 8 (over y, x, core), fsdp: 4 (over z).
Axes of the slice: x: 2, y: 2, z: 4, core: 2. Of those that a mesh axis runs over, the one named last changes fastest.
Arguments:
- tokens: bfloat16 [4, 2048, 2048], P('fsdp', 'seq'), may hold values from -6 to 6
- w_in: bfloat16 [2048, 2304], P('fsdp'), may hold values from -0.125 to 0.125
- log_decay: float32 [4, 32, 2048], P('fsdp', None, 'seq'), may hold values from -2 to 0, as said below
- grad_out: bfloat16 [4, 2048, 2048], P('fsdp', 'seq'), may hold values from -6 to 6
Outputs:
- mixer_out: bfloat16 [4, 2048, 2048], P('fsdp', 'seq')
- grad_tokens: bfloat16 [4, 2048, 2048], P('fsdp', 'seq')
- grad_weights: float32 [2048, 2304], P(('seq', 'fsdp'))
Inputs may be any that keep to these rules, and one draw needn't show every extreme that they name: `log_decay`: each entry is the logarithm of a decay factor below one.
All inputs are finite; a program needn't handle non-finite values.
Results may differ from a plain program's by a relative error of at most 0.015.
Values may be sent and summed in bfloat16 or wider, within the bound.
No kernel may reach another device: no remote copies, remote signals or barrier semaphores. Data moves between devices by JAX's collectives and lax.ppermute only.
A program may use at most 192 MiB of HBM per device.

v0:
```python
import jax
import jax.numpy as jnp
from jax import lax
from jax.sharding import PartitionSpec as P

BLOCK = 256


highest = lax.Precision.HIGHEST
epsilon = 1e-05


def entering_2(shard, axis, join, neutral, backward):
    count = lax.axis_size(axis)
    place = lax.axis_index(axis)
    ahead = count - 1 - place if backward else place
    gathered = jax.tree.map(
        lambda a, kind: lax.all_gather(a.astype(kind), axis), shard, (jnp.bfloat16, jnp.bfloat16)
    )
    state = jax.tree.map(lambda a, e: jnp.zeros_like(a) + jnp.asarray(e, a.dtype), shard, neutral)

    def one(step, state):
        source = count - 1 - step if backward else step
        return join(
            state,
            jax.tree.map(
                lambda a, own: lax.dynamic_index_in_dim(a, source, 0, False).astype(own.dtype),
                gathered,
                shard,
            ),
        )

    return lax.fori_loop(0, ahead, one, state)


def combine_states(earlier, latter):
    return (earlier[0] + latter[0], jnp.exp(latter[0])[:, None, None] * earlier[1] + latter[1])


def block_chain(log_rates, terms, backward, start_state):

    def advance(carried, packed):
        log_k, term_k = packed
        return (jnp.exp(log_k)[:, None, None] * carried + term_k, carried)

    finish, inputs = lax.scan(advance, start_state, (log_rates, terms), reverse=backward)
    return (inputs, finish)


def decay_matrix(cumulative, log_rates):
    extent = cumulative.shape[-1]
    row_idx = lax.broadcasted_iota(jnp.int32, (extent, extent), 0)
    col_idx = lax.broadcasted_iota(jnp.int32, (extent, extent), 1)
    later_gap = cumulative[:, :, None] - cumulative[:, None, :]
    exclusive = cumulative - log_rates
    earlier_gap = exclusive[:, None, :] - exclusive[:, :, None]
    exponent = jnp.where(
        row_idx > col_idx, later_gap, jnp.where(row_idx < col_idx, earlier_gap, 0.0)
    )
    return jnp.exp(exponent) + (row_idx == col_idx).astype(jnp.float32)


def to_groups(array, axis, per_group):
    extents = array.shape
    grouped_shape = extents[:axis] + (extents[axis] // per_group, per_group) + extents[axis + 1 :]
    return jnp.moveaxis(array.reshape(grouped_shape), axis, 0)


def from_groups(array, axis):
    moved = jnp.moveaxis(array, 0, axis)
    extents = moved.shape
    return moved.reshape(
        extents[:axis] + (extents[axis] * extents[axis + 1],) + extents[axis + 2 :]
    )


def on_device(tokens, w_in, log_decay, grad_out):
    local_tokens = tokens[0]
    log_rates = log_decay[0]
    upstream_grad = grad_out[0]
    token_count = local_tokens.shape[0]
    hidden_width = local_tokens.shape[1]
    head_count = log_rates.shape[0]
    col_count = w_in.shape[1]
    inner_width = upstream_grad.shape[1]
    head_size = inner_width // head_count
    state_size = (col_count - inner_width) // 2
    block_count = token_count // BLOCK
    per_group = 8
    projected = jnp.dot(
        local_tokens,
        lax.all_gather(w_in, "fsdp", axis=0, tiled=True),
        preferred_element_type=jnp.float32,
    )
    xbc_rows = projected.astype(jnp.bfloat16)
    xbc_rows = lax.optimization_barrier(xbc_rows)
    xbc_float = xbc_rows.astype(jnp.float32)
    values = xbc_float[:, :inner_width].reshape(block_count, BLOCK, head_count, head_size)
    key_rows = xbc_float[:, inner_width : inner_width + state_size].reshape(
        block_count, BLOCK, state_size
    )
    queries = xbc_float[:, inner_width + state_size :].reshape(block_count, BLOCK, state_size)
    key_half = xbc_rows[:, inner_width : inner_width + state_size].reshape(
        block_count, BLOCK, state_size
    )
    query_half = xbc_rows[:, inner_width + state_size :].reshape(block_count, BLOCK, state_size)
    blocked = log_rates.reshape(head_count, block_count, BLOCK).transpose(1, 0, 2)
    cumulative = jnp.cumsum(blocked, axis=-1)
    totals = cumulative[:, :, -1]
    to_end = jnp.exp(totals[:, :, None] - cumulative)
    from_start = jnp.exp(cumulative - blocked)
    enter_weight = jnp.exp(cumulative)
    leave_weight = jnp.exp(totals[:, :, None] - (cumulative - blocked))
    end_terms = jnp.einsum("khq,kqhp,kqn->khpn", to_end, values, key_rows, precision=highest)
    start_terms = jnp.einsum("khq,kqhp,kqn->khpn", from_start, values, key_rows, precision=highest)
    zero_state = jnp.zeros((head_count, head_size, state_size), jnp.float32)
    none_log = jnp.zeros((head_count,), jnp.float32)
    device_log = jnp.sum(totals, axis=0)
    _, end_total = block_chain(totals, end_terms, False, zero_state)
    _, start_total = block_chain(totals, start_terms, True, zero_state)
    entering = entering_2(
        (device_log, end_total), "seq", combine_states, (none_log, zero_state), False
    )[1]
    arriving = entering_2(
        (device_log, start_total), "seq", combine_states, (none_log, zero_state), True
    )[1]
    fwd_in, _ = block_chain(totals, end_terms, False, entering)
    rev_next, _ = block_chain(totals, start_terms, True, arriving)

    def block_forward(packed):
        (
            block_vals,
            block_khalf,
            block_qhalf,
            block_queries,
            block_cumul,
            block_logs,
            block_enter,
            block_leave,
            state_in,
            state_next,
        ) = packed
        affinity = lax.dot_general(
            block_qhalf, block_khalf, (((1,), (1,)), ((), ())), preferred_element_type=jnp.float32
        )

        def group_forward(section):
            group_values, group_cumul, group_logs = section
            weighted = affinity[None] * decay_matrix(group_cumul, group_logs)
            return jnp.einsum("gij,jgp->igp", weighted, group_values, precision=highest)

        group_parts = lax.map(
            group_forward,
            (
                to_groups(block_vals, 1, per_group),
                to_groups(block_cumul, 0, per_group),
                to_groups(block_logs, 0, per_group),
            ),
        )
        inner_part = from_groups(group_parts, 1)
        carried_in = (
            jnp.einsum("qn,hpn->qhp", block_queries, state_in, precision=highest)
            * block_enter.T[:, :, None]
        )
        carried_back = (
            jnp.einsum("qn,hpn->qhp", block_queries, state_next, precision=highest)
            * block_leave.T[:, :, None]
        )
        return inner_part + carried_in + carried_back

    mixture = lax.map(
        block_forward,
        (
            values,
            key_half,
            query_half,
            queries,
            cumulative,
            blocked,
            enter_weight,
            leave_weight,
            fwd_in,
            rev_next,
        ),
    )
    row_scale = jnp.sqrt(jnp.mean(mixture * mixture, axis=-1) + epsilon)
    normed = mixture / row_scale[..., None]
    mixer_out = normed.astype(jnp.bfloat16).reshape(1, token_count, inner_width)
    upstream = upstream_grad.astype(jnp.float32).reshape(block_count, BLOCK, head_count, head_size)
    grad_mixture = (
        upstream - normed * jnp.mean(upstream * normed, axis=-1, keepdims=True)
    ) / row_scale[..., None]
    in_adjoint = jnp.einsum(
        "khq,kqhp,kqn->khpn", enter_weight, grad_mixture, queries, precision=highest
    )
    out_adjoint = jnp.einsum(
        "khq,kqhp,kqn->khpn", leave_weight, grad_mixture, queries, precision=highest
    )
    _, in_total = block_chain(totals, in_adjoint, True, zero_state)
    _, out_total = block_chain(totals, out_adjoint, False, zero_state)
    later_adjoint = entering_2(
        (device_log, in_total), "seq", combine_states, (none_log, zero_state), True
    )[1]
    earlier_adjoint = entering_2(
        (device_log, out_total), "seq", combine_states, (none_log, zero_state), False
    )[1]
    grad_ends, _ = block_chain(totals, in_adjoint, True, later_adjoint)
    grad_starts, _ = block_chain(totals, out_adjoint, False, earlier_adjoint)

    def block_backward(packed):
        (
            block_vals,
            block_keys,
            block_queries,
            block_khalf,
            block_qhalf,
            block_cumul,
            block_logs,
            block_enter,
            block_leave,
            block_end,
            block_start,
            state_in,
            state_next,
            block_grad,
            block_grad_end,
            block_grad_start,
        ) = packed
        affinity = lax.dot_general(
            block_qhalf, block_khalf, (((1,), (1,)), ((), ())), preferred_element_type=jnp.float32
        )

        def group_backward(section):
            group_values, group_cumul, group_logs, group_grad = section
            decays = decay_matrix(group_cumul, group_logs)
            weighted = affinity[None] * decays
            grad_vals = jnp.einsum("gij,igp->jgp", weighted, group_grad, precision=highest)
            grad_weighted = jnp.einsum("igp,jgp->gij", group_grad, group_values, precision=highest)
            return (grad_vals, jnp.sum(grad_weighted * decays, axis=0))

        group_vals, group_affinity = lax.map(
            group_backward,
            (
                to_groups(block_vals, 1, per_group),
                to_groups(block_cumul, 0, per_group),
                to_groups(block_logs, 0, per_group),
                to_groups(block_grad, 1, per_group),
            ),
        )
        grad_affinity = jnp.sum(group_affinity, axis=0)
        enter_cols = block_enter.T[:, :, None]
        leave_cols = block_leave.T[:, :, None]
        end_cols = block_end.T[:, :, None]
        start_cols = block_start.T[:, :, None]
        grad_queries = jnp.dot(grad_affinity, block_keys, precision=highest)
        grad_queries = grad_queries + jnp.einsum(
            "qhp,hpn->qn", block_grad * enter_cols, state_in, precision=highest
        )
        grad_queries = grad_queries + jnp.einsum(
            "qhp,hpn->qn", block_grad * leave_cols, state_next, precision=highest
        )
        grad_keys = jnp.dot(grad_affinity.T, block_queries, precision=highest)
        grad_keys = grad_keys + jnp.einsum(
            "qhp,hpn->qn", block_vals * end_cols, block_grad_end, precision=highest
        )
        grad_keys = grad_keys + jnp.einsum(
            "qhp,hpn->qn", block_vals * start_cols, block_grad_start, precision=highest
        )
        grad_values = from_groups(group_vals, 1)
        grad_values = grad_values + end_cols * jnp.einsum(
            "qn,hpn->qhp", block_keys, block_grad_end, precision=highest
        )
        grad_values = grad_values + start_cols * jnp.einsum(
            "qn,hpn->qhp", block_keys, block_grad_start, precision=highest
        )
        return (grad_values, grad_keys, grad_queries)

    grad_values, grad_keys, grad_queries = lax.map(
        block_backward,
        (
            values,
            key_rows,
            queries,
            key_half,
            query_half,
            cumulative,
            blocked,
            enter_weight,
            leave_weight,
            to_end,
            from_start,
            fwd_in,
            rev_next,
            grad_mixture,
            grad_ends,
            grad_starts,
        ),
    )
    grad_proj = jnp.concatenate(
        [
            grad_values.reshape(token_count, inner_width),
            grad_keys.reshape(token_count, state_size),
            grad_queries.reshape(token_count, state_size),
        ],
        axis=1,
    ).astype(jnp.bfloat16)
    grad_local = lax.dot_general(
        grad_proj,
        lax.all_gather(w_in, "fsdp", axis=0, tiled=True),
        (((1,), (1,)), ((), ())),
        preferred_element_type=jnp.float32,
    )
    grad_tokens = grad_local.astype(jnp.bfloat16).reshape(1, token_count, hidden_width)
    partial_rows = lax.psum_scatter(
        lax.dot_general(
            local_tokens, grad_proj, (((0,), (0,)), ((), ())), preferred_element_type=jnp.float32
        ).astype(jnp.bfloat16),
        "seq",
        scatter_dimension=0,
        tiled=True,
    )
    grad_weights = lax.psum_scatter(partial_rows, "fsdp", scatter_dimension=0, tiled=True).astype(
        jnp.float32
    )
    return (mixer_out, grad_tokens, grad_weights)


def solution(mesh):
    return jax.shard_map(
        on_device,
        mesh=mesh,
        in_specs=(
            P("fsdp", "seq", None),
            P("fsdp", None),
            P("fsdp", None, "seq"),
            P("fsdp", "seq", None),
        ),
        out_specs=(P("fsdp", "seq", None), P("fsdp", "seq", None), P(("seq", "fsdp"), None)),
        check_vma=False,
    )
```

profile of v0, /device:TPU:0, one launch (start us, length us, event | category | flops | bytes accessed | tf_op | source)
XLA Modules:
  0.0 504.9 jit_solution(16805960647515836634)
XLA Ops:
  9.2 169.9 %all-gather.11.cloned.1.call-done = bf16[2048,2304]{1,0:T(8,128)(2,1)} async-done(((bf16[512,2304]{1,0:T(8,128)(2,1)}), bf16[2048,2304]{1,0:T(8,128)(2,1)}) %all-gather.11.cloned.1.call-update) | async-done | bytes 9437200 | tf_op jit(solution)/shard_map/all_gather | solution.py:92
  179.1 6.3 %convolution_convert_fusion.1 = bf16[256,2304]{1,0:T(8,128)(2,1)S(1)} fusion(bf16[2048,2304]{1,0:T(8,128)(2,1)} %all-gather.11.cloned.1.call-done, bf16[1,256,2048]{2,1,0:T(8,128)(2,1)S(1)} %copy-done), kind=kOutput, calls=%fused_computation.70 | convolution fusion | flops 2416508928 | bytes 11665408 | tf_op jit(solution)/shard_map/dot_general | solution.py:90
  204.2 8.6 %all-gather = bf16[8,32,1]{1,2,0:T(2,128)(2,1)S(1)} all-gather(bf16[1,32,1]{1,2,0:T(2,128)(2,1)S(1)} %slice.83), channel_id=2, replica_groups=mesh['seq'=8,'fsdp'=4] {'seq'}, dimensions={0}, use_global_device_ids=true | all-gather | bytes 576 | tf_op jit(solution)/shard_map/all_gather | solution.py:18
  216.4 18.4 %while.56 = (s32[]{:T(128)}, f32[4,256,8,64]{1,3,2,0:T(8,128)}, f32[4,256,8,64]{1,3,2,0:T(8,128)S(1)}, f32[256,256]{1,0:T(8,128)}, f32[4,8,256]{2,1,0:T(8,128)S(1)}, /*index=5*/f32[4,8,256]{2,1,0:T(8,128)S(1)}, s32[]{:T(128)}) while((s32[]{:T(128)}, f32[4,256,8,64]{1,3,2,0:T(8,128)}, f32[4,256,8,64]{1,3,2,0:T(8,128)S(1)}, ...), condition=%wide.region_3.4_spmd, body=%wide.region_2.3_spmd.sunk | while | flops 406063104 | bytes 2171997 | solution.py:152
  216.5 4.5 fusion.178
  221.1 4.5 fusion.178
  225.7 4.5 fusion.178
  230.3 4.5 fusion.178
  236.2 9.5 %while.58 = (s32[]{:T(128)}, f32[32,64,128]{2,1,0:T(8,128)S(1)}, s32[]{:T(128)}, bf16[8,32]{1,0:T(8,128)(2,1)S(1)}, bf16[8,32,64,128]{3,2,1,0:T(8,128)(2,1)}, /*index=5*/s32[]{:T(128)}, s32[]{:T(128)}, s32[]{:T(128)}, s32[]{:T(128)}) while((s32[]{:T(128)}, f32[32,64,128]{2,1,0:T(8,128)S(1)}, s32[]{:T(128)}, bf16[8,32]{1,0:T(8,128)(2,1)S(1)}, ...), condition=%wide.region_7.8_spmd, body=%wide.region_6.7_spmd.sunk | while | flops 786470 | bytes 2621915 | solution.py:33
  245.7 21.5 %all-gather.13.cloned.1.call-done = bf16[256,64,128]{2,1,0:T(8,128)(2,1)} async-done(((bf16[32,64,128]{2,1,0:T(8,128)(2,1)}), bf16[256,64,128]{2,1,0:T(8,128)(2,1)}) %all-gather.13.cloned.1.call-update) | async-done | bytes 4194320 | tf_op jit(solution)/shard_map/all_gather | solution.py:18
  284.0 35.4 %while.59 = (s32[]{:T(128)}, f32[4,256,8,64]{1,3,2,0:T(8,128)}, f32[4,256,256]{2,1,0:T(8,128)}, f32[4,256,8,64]{1,3,2,0:T(8,128)}, f32[256,256]{1,0:T(8,128)}, /...) while((s32[]{:T(128)}, f32[4,256,8,64]{1,3,2,0:T(8,128)}, ...), condition=%wide.region_12.13_spmd, body=%wide.region_10.12_spmd.sunk | while | flops 812320768 | bytes 4434033 | solution.py:241
  284.1 4.1 fusion.184
  288.2 3.9 multiply_reduce_fusion.4
  293.0 4.1 fusion.184
  297.0 3.9 multiply_reduce_fusion.4
  301.8 4.1 fusion.184
  305.9 3.9 multiply_reduce_fusion.4
  310.6 4.1 fusion.184
  328.4 9.7 %while.60 = (s32[]{:T(128)}, f32[32,64,128]{2,1,0:T(8,128)S(1)}, s32[]{:T(128)}, bf16[8,32]{1,0:T(8,128)(2,1)S(1)}, bf16[8,32,64,128]{3,2,1,0:T(8,128)(2,1)}, /*index=5*/s32[]{:T(128)}, s32[]{:T(128)}, s32[]{:T(128)}, s32[]{:T(128)}) while((s32[]{:T(128)}, f32[32,64,128]{2,1,0:T(8,128)S(1)}, s32[]{:T(128)}, bf16[8,32]{1,0:T(8,128)(2,1)S(1)}, ...), condition=%wide.region_14.15_spmd, body=%wide.region_13.14_spmd.sunk | while | flops 786470 | bytes 2621915 | solution.py:33
  344.8 18.4 %all-gather.19.cloned.1.call-done = bf16[256,64,128]{2,1,0:T(8,128)(2,1)} async-done(((bf16[32,64,128]{2,1,0:T(8,128)(2,1)}), bf16[256,64,128]{2,1,0:T(8,128)(2,1)}) %all-gather.19.cloned.1.call-update) | async-done | bytes 4194320 | tf_op jit(solution)/shard_map/all_gather | solution.py:18
  371.0 6.6 %fusion.55 = bf16[2048,2304]{0,1:T(8,128)(2,1)} fusion(bf16[1,256,2048]{2,1,0:T(8,128)(2,1)S(1)} %copy-done, bf16[256,128]{0,1:T(8,128)(2,1)S(1)} %copy-done.11, bf16[256,128]{0,1:T(8,128)(2,1)S(1)} %fusion.114, bf16[256,2048]{0,1:T(8,128)(2,1)S(1)} %bitcast.229), kind=kOutput, calls=%fused_computation.69 | convolution fusion | flops 2424176640 | bytes 11665408 | tf_op jit(solution)/shard_map/dot_general | solution.py:315
  378.0 85.6 %reduce-scatter.5.cloned.1.call-done = bf16[256,2304]{0,1:T(8,128)(2,1)} async-done(((bf16[2048,2304]{0,1:T(8,128)(2,1)}), bf16[256,2304]{0,1:T(8,128)(2,1)}) %reduce-scatter.5.cloned.1.call-update) | async-done | bytes 1179664 | tf_op jit(solution)/shard_map/reduce_scatter | solution.py:314
  467.5 7.3 %fusion.56 = bf16[1,256,2048]{2,1,0:T(8,128)(2,1)} fusion(bf16[2048,2304]{1,0:T(8,128)(2,1)} %all-gather.11.cloned.1.call-done, bf16[256,128]{0,1:T(8,128)(2,1)S(1)} %copy-done.11, bf16[256,128]{0,1:T(8,128)(2,1)S(1)} %copy-done.13, bf16[256,2048]{0,1:T(8,128)(2,1)S(1)} %bitcast.230), kind=kOutput, calls=%fused_computation.72 | convolution fusion | flops 2419982336 | bytes 11665408 | tf_op jit(solution)/shard_map/dot_general | solution.py:307
  474.8 20.6 %reduce-scatter.7.cloned.1.call-done = bf16[64,2304]{1,0:T(8,128)(2,1)} async-done(((bf16[256,2304]{1,0:T(8,128)(2,1)}), bf16[64,2304]{1,0:T(8,128)(2,1)}) %reduce-scatter.7.cloned.1.call-update) | async-done | bytes 294928
  (170 shorter events, 98.3 us)
Async XLA Ops:
  7.2 171.9 %copy-start = (bf16[1,256,2048]{2,1,0:T(8,128)(2,1)S(1)}, bf16[1,256,2048]{2,1,0:T(8,128)(2,1)}, u32[]{:S(2)}) copy-start(bf16[1,256,2048]{2,1,0:T(8,128)(2,1)} %param.16) | copy-start | bytes 3145732
  7.2 0.8 copy-start.9
  7.2 171.9 %all-gather.11.cloned.1.call-start = ((), (), s32[]{:S(2)}) async-start(), calls=%async_computation.2 | async-start | bytes 11796480 | tf_op jit(solution)/shard_map/all_gather | solution.py:92
  7.9 226.8 %all-gather.15.cloned.1.call-start = ((), (), s32[]{:S(2)}) async-start(), calls=%async_computation.5 | async-start | bytes 4718592 | tf_op jit(solution)/shard_map/all_gather | solution.py:18
  9.1 176.3 %copy-start.10 = (f32[1,32,256]{1,2,0:T(8,128)}, f32[1,32,256]{1,2,0:T(8,128)S(1)}, u32[]{:S(2)}) copy-start(f32[1,32,256]{1,2,0:T(8,128)S(1)} %get-tuple-element.649) | copy-start | bytes 98308
  185.4 1.1 copy-start.8
  192.8 74.3 %all-gather.13.cloned.1.call-start = ((), (), s32[]{:S(2)}) async-start(), calls=%async_computation.4 | async-start | bytes 4718592 | tf_op jit(solution)/shard_map/all_gather | solution.py:18
  198.1 130.2 %all-gather.17.cloned.1.call-start = ((), (), s32[]{:S(2)}) async-start(), calls=%async_computation.6 | async-start | bytes 4718592 | tf_op jit(solution)/shard_map/all_gather | solution.py:18
  234.8 1.3 copy-start.1
  267.8 2.0 copy-start.6
  269.8 2.3 copy-start.4
  274.4 1.4 copy-start.2
  278.5 84.7 %all-gather.19.cloned.1.call-start = ((), (), s32[]{:S(2)}) async-start(), calls=%async_computation.7 | async-start | bytes 4718592 | tf_op jit(solution)/shard_map/all_gather | solution.py:18
  282.2 181.5 %reduce-scatter.5.cloned.1.call-start = ((), (), s32[]{:S(2)}) async-start(), calls=%async_computation.3 | async-start | bytes 10616832 | tf_op jit(solution)/shard_map/reduce_scatter | solution.py:314
  320.7 3.8 copy-start.3
  363.3 4.9 copy-start.5
  368.2 2.8 copy-start.12
  368.2 2.8 copy-start.11
  377.7 88.4 %copy-start.7 = (bf16[256,32,64]{0,2,1:T(8,128)(2,1)S(1)}, bf16[256,32,64]{0,2,1:T(8,128)(2,1)}, u32[]{:S(2)}) copy-start(bf16[256,32,64]{0,2,1:T(8,128)(2,1)} %get-tuple-element.655) | copy-start | bytes 3145732
  377.7 117.7 %reduce-scatter.7.cloned.1.call-start = ((), (), s32[]{:S(2)}) async-start(), calls=%async_computation.8 | async-start | bytes 1474560
  466.1 1.5 copy-start.13
Sparse Core Ops, SparseCore 0:
  9.6 169.4 all-gather.10
  192.9 34.9 all-gather.14
  230.3 36.7 all-gather.12
  278.7 46.0 all-gather.16
  326.5 36.7 all-gather.18
  377.8 85.7 reduce-scatter.4
  466.2 29.1 reduce-scatter.6
where the time goes:
time: 514 us; the launch traced here: 505 us
  waiting for transfers between devices  317 us (62%)
  matrix products  110 us (21%)
  other arithmetic  26.6 us (5%)
  local copies, waits for them, and re-layouts  26 us (5%)
  between operations  14.8 us (3%)
  blocking collectives  8.63 us (2%)
    all_gather x1, waiting for transfers between devices, on_device(): lax.all_gather(w_in, 'fsdp', axis=0, tiled=True)  170 us
    reduce_scatter x1, waiting for transfers between devices, on_device(): lax.psum_scatter(lax.dot_general(local_tokens, grad_proj, (((0,), (0,)),...  85.6 us
    all_gather x4, waiting for transfers between devices, entering_2(): lax.all_gather(a.astype(kind), axis)  39.9 us
    unnamed x8, waiting for transfers between devices  21.4 us
    add x14, other arithmetic, combine_states(): jnp.exp(latter[0])[:, None, None] * earlier[1] + latter[1]  18.3 us
    dot_general x4, matrix products, group_forward(): return jnp.einsum('gij,jgp->igp', weighted, group_values, precision=highest)  18 us
    dot_general x4, matrix products, group_backward(): jnp.einsum('gij,igp->jgp', weighted, group_grad, precision=highest)  16.3 us
    dot_general x4, matrix products, group_backward(): jnp.einsum('igp,jgp->gij', group_grad, group_values, precision=highest)  15.7 us
  transfers between devices with their start and end apart: 7, of which 5 were waited for; matrix products, arithmetic and copies ran while one was open for 23% of the time, Pallas kernels for 0%

commit v1 on v0

v1 whole, which is shorter than its diff:
```python
import functools

import jax
import jax.numpy as jnp
from jax import lax
from jax.experimental import pallas as pl
from jax.experimental.pallas import tpu as pltpu
from jax.sharding import PartitionSpec as P

CHUNK = 128
EPSILON = 1e-05
VMEM_LIMIT = 50 * 1024 * 1024

f32 = jnp.float32
bf16 = jnp.bfloat16


def dot_nn(a, b):
    return lax.dot_general(a, b, (((1,), (0,)), ((), ())), preferred_element_type=f32)


def dot_nt(a, b):
    return lax.dot_general(a, b, (((1,), (1,)), ((), ())), preferred_element_type=f32)


def dot_tn(a, b):
    return lax.dot_general(a, b, (((0,), (0,)), ((), ())), preferred_element_type=f32)


def by_head(rows, heads, head_size):
    if heads == 1:
        return rows
    lane = lax.broadcasted_iota(jnp.int32, rows.shape, 1)
    parts = []
    for h in range(heads):
        inside = (lane >= h * head_size) & (lane < (h + 1) * head_size)
        parts.append(jnp.where(inside, rows, jnp.zeros_like(rows)))
    return jnp.concatenate(parts, axis=0)


def decayed(affinity, decays, heads):
    tiled = jnp.concatenate([affinity] * heads, axis=1) if heads > 1 else affinity
    return (tiled * decays.astype(f32)).astype(bf16)


def forward_kernel(
    heads, head_size,
    x_ref, b_ref, c_ref, m_ref, te_ref, fs_ref, en_ref, lv_ref, dt_ref, mean_ref,
    z_ref, rs_ref, sf_ref, rn_ref,
    carry,
):
    chunks = dt_ref.shape[0]
    state_size = b_ref.shape[1]
    carry[...] = jnp.zeros_like(carry)

    def reverse_states(i, _):
        k = chunks - 1 - i
        rows = pl.ds(pl.multiple_of(k * CHUNK, CHUNK), CHUNK)
        state = pl.ds(pl.multiple_of(k * state_size, state_size), state_size)
        rn_ref[state, :] = carry[...].astype(bf16)
        term = dot_tn(b_ref[rows, :], x_ref[rows, :] * fs_ref[rows, :])
        carry[...] = dt_ref[k] * carry[...] + term
        return 0

    lax.fori_loop(0, chunks, reverse_states, 0, unroll=2)
    carry[...] = jnp.zeros_like(carry)

    def outputs(k, _):
        rows = pl.ds(pl.multiple_of(k * CHUNK, CHUNK), CHUNK)
        state = pl.ds(pl.multiple_of(k * state_size, state_size), state_size)
        x, b, c = x_ref[rows, :], b_ref[rows, :], c_ref[rows, :]
        state_in = carry[...].astype(bf16)
        sf_ref[state, :] = state_in
        weights = decayed(dot_nt(c, b), m_ref[rows, :], heads)
        y = dot_nn(weights, by_head(x, heads, head_size))
        y = y + en_ref[rows, :].astype(f32) * dot_nn(c, state_in)
        y = y + lv_ref[rows, :].astype(f32) * dot_nn(c, rn_ref[state, :])
        mean_square = dot_nn((y * y).astype(bf16), mean_ref[...])
        inverse = lax.rsqrt(mean_square + EPSILON)
        z_ref[rows, :] = (y * inverse).astype(bf16)
        rs_ref[rows, :] = inverse.astype(bf16)
        carry[...] = dt_ref[k] * carry[...] + dot_tn(b, x * te_ref[rows, :])
        return 0

    lax.fori_loop(0, chunks, outputs, 0, unroll=2)


def backward_kernel(
    heads, head_size,
    x_ref, b_ref, c_ref, m_ref, mt_ref, te_ref, fs_ref, en_ref, lv_ref, dt_ref, mean_ref,
    z_ref, rs_ref, sf_ref, rn_ref, g_ref,
    dx_ref, db_ref, dc_ref,
    carry, dy_ref, ge_ref,
):
    chunks = dt_ref.shape[0]
    state_size = b_ref.shape[1]
    carry[...] = jnp.zeros_like(carry)

    def end_adjoints(i, _):
        k = chunks - 1 - i
        rows = pl.ds(pl.multiple_of(k * CHUNK, CHUNK), CHUNK)
        state = pl.ds(pl.multiple_of(k * state_size, state_size), state_size)
        g, z = g_ref[rows, :].astype(f32), z_ref[rows, :].astype(f32)
        mean_gz = dot_nn((g * z).astype(bf16), mean_ref[...])
        dy = ((g - z * mean_gz) * rs_ref[rows, :].astype(f32)).astype(bf16)
        dy_ref[rows, :] = dy
        ge_ref[state, :] = carry[...].astype(bf16)
        carry[...] = dt_ref[k] * carry[...] + dot_tn(c_ref[rows, :], dy * en_ref[rows, :])
        return 0

    lax.fori_loop(0, chunks, end_adjoints, 0, unroll=2)
    carry[...] = jnp.zeros_like(carry)

    def gradients(k, _):
        rows = pl.ds(pl.multiple_of(k * CHUNK, CHUNK), CHUNK)
        state = pl.ds(pl.multiple_of(k * state_size, state_size), state_size)
        x, b, c, dy = x_ref[rows, :], b_ref[rows, :], c_ref[rows, :], dy_ref[rows, :]
        te, fs, en, lv = te_ref[rows, :], fs_ref[rows, :], en_ref[rows, :], lv_ref[rows, :]
        ge, gs = ge_ref[state, :], carry[...].astype(bf16)
        m = m_ref[rows, :]
        grad_weights = dot_nt(dy, by_head(x, heads, head_size)) * m.astype(f32)
        da = grad_weights[:, :CHUNK]
        for h in range(1, heads):
            da = da + grad_weights[:, h * CHUNK : (h + 1) * CHUNK]
        da = da.astype(bf16)
        turned = decayed(dot_nt(b, c), mt_ref[rows, :], heads)
        dx = dot_nn(turned, by_head(dy, heads, head_size))
        dx = dx + te.astype(f32) * dot_nn(b, ge)
        dx = dx + fs.astype(f32) * dot_nn(b, gs)
        dx_ref[rows, :] = dx.astype(bf16)
        dy_lv = dy * lv
        dc = dot_nn(da, b) + dot_nt(dy * en, sf_ref[state, :]) + dot_nt(dy_lv, rn_ref[state, :])
        dc_ref[rows, :] = dc.astype(bf16)
        db = dot_tn(da, c) + dot_nt(x * te, ge) + dot_nt(x * fs, gs)
        db_ref[rows, :] = db.astype(bf16)
        carry[...] = dt_ref[k] * carry[...] + dot_tn(c, dy_lv)
        return 0

    lax.fori_loop(0, chunks, gradients, 0, unroll=2)


def whole(count):
    return [pl.BlockSpec(memory_space=pltpu.VMEM)] * count


def decay_tables(log_rates, head_size):
    heads, length = log_rates.shape
    chunks = length // CHUNK
    logs = log_rates.reshape(heads, chunks, CHUNK)
    cumulative = jnp.cumsum(logs, axis=-1)
    totals = cumulative[:, :, -1:]
    exclusive = cumulative - logs

    def spread(a):
        rows = a.reshape(heads, length).T
        return jnp.repeat(jnp.exp(rows), head_size, axis=1).astype(bf16)

    to_end = spread(totals - cumulative)
    from_start = spread(exclusive)
    enter = spread(cumulative)
    leave = spread(totals - exclusive)
    chunk_decay = jnp.repeat(jnp.exp(totals[:, :, 0].T), head_size, axis=1)[:, None, :]
    row = lax.broadcasted_iota(jnp.int32, (1, CHUNK, 1, CHUNK), 1)
    col = lax.broadcasted_iota(jnp.int32, (1, CHUNK, 1, CHUNK), 3)
    by_row = lambda a: a.transpose(1, 2, 0)[:, :, :, None]
    by_col = lambda a: a.transpose(1, 0, 2)[:, None, :, :]
    below = by_row(cumulative) - by_col(cumulative)
    above = by_col(exclusive) - by_row(exclusive)
    diagonal = (row == col).astype(f32)
    decays = jnp.exp(jnp.where(row > col, below, jnp.where(row < col, above, 0.0))) + diagonal
    turned = jnp.exp(jnp.where(col > row, -below, jnp.where(col < row, -above, 0.0))) + diagonal
    decays = decays.astype(bf16).reshape(length, heads * CHUNK)
    turned = turned.astype(bf16).reshape(length, heads * CHUNK)
    return to_end, from_start, enter, leave, chunk_decay, decays, turned


def on_device(tokens, w_in, log_decay, grad_out):
    local_tokens = tokens[0]
    upstream = grad_out[0]
    token_count, hidden_width = local_tokens.shape
    head_count = log_decay.shape[1]
    inner_width = upstream.shape[1]
    head_size = inner_width // head_count
    state_size = (w_in.shape[1] - inner_width) // 2
    seq_count = lax.axis_size("seq")
    fsdp_count = lax.axis_size("fsdp")
    place = lax.axis_index("seq")
    heads = head_count // seq_count
    width = heads * head_size
    length = token_count * seq_count
    shared = 2 * state_size
    shared_part = shared // seq_count

    all_tokens = lax.all_gather(local_tokens, "seq", axis=0, tiled=True)
    own_columns = jnp.concatenate(
        [lax.dynamic_slice_in_dim(w_in, place * width, width, 1), w_in[:, inner_width:]], axis=1
    )
    w_columns = lax.all_gather(own_columns, "fsdp", axis=0, tiled=True)
    log_rates = lax.all_to_all(log_decay[0], "seq", 0, 1, tiled=True)
    g = lax.all_to_all(upstream, "seq", 1, 0, tiled=True)
    to_end, from_start, enter, leave, chunk_decay, decays, turned = decay_tables(
        log_rates, head_size
    )
    head_row = lax.broadcasted_iota(jnp.int32, (width, width), 0) // head_size
    head_col = lax.broadcasted_iota(jnp.int32, (width, width), 1) // head_size
    mean_over_head = jnp.where(head_row == head_col, 1.0 / head_size, 0.0).astype(bf16)

    xbc = jnp.dot(all_tokens, w_columns, preferred_element_type=f32).astype(bf16)
    x = xbc[:, :width]
    b = xbc[:, width : width + state_size]
    c = xbc[:, width + state_size :]

    chunks = length // CHUNK
    shape = jax.ShapeDtypeStruct
    params = pltpu.CompilerParams(vmem_limit_bytes=VMEM_LIMIT)
    z, inverse, states_in, states_next = pl.pallas_call(
        functools.partial(forward_kernel, heads, head_size),
        out_shape=[
            shape((length, width), bf16),
            shape((length, width), bf16),
            shape((chunks * state_size, width), bf16),
            shape((chunks * state_size, width), bf16),
        ],
        in_specs=whole(10),
        out_specs=whole(4),
        scratch_shapes=[pltpu.VMEM((state_size, width), f32)],
        compiler_params=params,
    )(x, b, c, decays, to_end, from_start, enter, leave, chunk_decay, mean_over_head)
    mixer_out = lax.all_to_all(z, "seq", 0, 1, tiled=True)

    dx, db, dc = pl.pallas_call(
        functools.partial(backward_kernel, heads, head_size),
        out_shape=[
            shape((length, width), bf16),
            shape((length, state_size), bf16),
            shape((length, state_size), bf16),
        ],
        in_specs=whole(16),
        out_specs=whole(3),
        scratch_shapes=[
            pltpu.VMEM((state_size, width), f32),
            pltpu.VMEM((length, width), bf16),
            pltpu.VMEM((chunks * state_size, width), bf16),
        ],
        compiler_params=params,
    )(
        x, b, c, decays, turned, to_end, from_start, enter, leave, chunk_decay, mean_over_head,
        z, inverse, states_in, states_next, g,
    )

    packed = jnp.concatenate([dx, db, dc], axis=1).reshape(seq_count, token_count, width + shared)
    arrived = lax.all_to_all(packed, "seq", 0, 0)
    grad_heads = arrived[:, :, :width]
    grad_shared = jnp.sum(arrived[:, :, width:].astype(f32), axis=0).astype(bf16)
    w_heads = lax.all_gather(w_columns[:, :width], "seq")
    grad_tokens = lax.dot_general(
        grad_heads, w_heads, (((0, 2), (0, 2)), ((), ())), preferred_element_type=f32
    ) + dot_nt(grad_shared, w_columns[:, width:])

    shared_columns = lax.all_to_all(grad_shared, "seq", 1, 0, tiled=True)
    grad_columns = jnp.concatenate([dx, shared_columns], axis=1)
    partial = dot_tn(all_tokens, grad_columns).astype(bf16)
    rows_each = hidden_width // (seq_count * fsdp_count)
    partial = partial.reshape(seq_count, fsdp_count, rows_each, width + shared_part)
    summed = lax.psum_scatter(partial, "fsdp", scatter_dimension=1, tiled=False)
    owned = lax.all_to_all(summed, "seq", 0, 0).astype(f32)
    grad_weights = jnp.concatenate(
        [
            owned[:, :, :width].transpose(1, 0, 2).reshape(rows_each, inner_width),
            owned[:, :, width:].transpose(1, 0, 2).reshape(rows_each, shared),
        ],
        axis=1,
    )
    return mixer_out[None], grad_tokens.astype(bf16)[None], grad_weights


def solution(mesh):
    return jax.shard_map(
        on_device,
        mesh=mesh,
        in_specs=(
            P("fsdp", "seq", None),
            P("fsdp", None),
            P("fsdp", None, "seq"),
            P("fsdp", "seq", None),
        ),
        out_specs=(P("fsdp", "seq", None), P("fsdp", "seq", None), P(("seq", "fsdp"), None)),
        check_vma=False,
    )
```

time: 514 us -> 343 us (0.67); the launches traced: 505 us -> 342 us
  waiting for transfers between devices: 317 us -> 172 us
  matrix products: 110 us -> 23.1 us
  Pallas kernels: 0 us -> 29.2 us
  blocking collectives: 8.63 us -> 37.1 us
  other arithmetic: 26.6 us -> 11 us
  starting transfers between devices: 0.71 us -> 16.1 us
  local copies, waits for them, and re-layouts: 26 us -> 39.4 us
    all_gather x5 -> x3, waiting for transfers between devices: 210 us -> 110 us  [the longest x1 55 us: on_device(): all_tokens = lax.all_gather(local_tokens, 'seq', axis=0, tiled=True)]
    dot_general x30 -> x4, matrix products: 110 us -> 23.1 us  [the longest x1 8.5 us: on_device(): jnp.dot(all_tokens, w_columns, preferred_element_type=f32).astype(bf16)]
    reduce_scatter x1 -> x0, waiting for transfers between devices: 85.6 us -> none  [on_device(): lax.psum_scatter(lax.dot_general(local_tokens, grad_proj, (((0,), (0,)),...]
    all_to_all x0 -> x2, blocking collectives: none -> 37.1 us  [the longest x1 29.1 us: on_device(): arrived = lax.all_to_all(packed, 'seq', 0, 0)]
    pallas_call x0 -> x2, Pallas kernels: none -> 29.2 us  [the longest x1 16.2 us: on_device(): pl.pallas_call(functools.partial(backward_kernel, heads, head_size), out_...]
    unnamed x8 -> x5, waiting for transfers between devices: 21.4 us -> 43.9 us
    add x14 -> x0, other arithmetic: 18.3 us -> none  [combine_states(): jnp.exp(latter[0])[:, None, None] * earlier[1] + latter[1]]
    all_to_all x0 -> x4, waiting for transfers between devices: none -> 17.8 us  [the longest x1 14.7 us: on_device(): mixer_out = lax.all_to_all(z, 'seq', 0, 1, tiled=True)]
  transfers between devices with their start and end apart: 7 -> 8, of which waited for: 5 -> 6; matrix products, arithmetic and copies ran while one was open for 23% -> 17% of each run, Pallas kernels for 0% -> 4%
where the time goes in v1:
time: 343 us; the launch traced here: 342 us
  waiting for transfers between devices  172 us (50%)
  local copies, waits for them, and re-layouts  39.4 us (11%)
  blocking collectives  37.1 us (11%)
  Pallas kernels  29.2 us (9%)
  matrix products  23.1 us (7%)
  starting transfers between devices  16.1 us (5%)
  between operations  14 us (4%)
  other arithmetic  11 us (3%)
    all_gather x1, waiting for transfers between devices, on_device(): all_tokens = lax.all_gather(local_tokens, 'seq', axis=0, tiled=True)  55 us
    all_gather x1, waiting for transfers between devices, on_device(): w_heads = lax.all_gather(w_columns[:, :width], 'seq')  49.2 us
    unnamed x5, waiting for transfers between devices  43.9 us
    all_to_all x1, blocking collectives, on_device(): arrived = lax.all_to_all(packed, 'seq', 0, 0)  29.1 us
    pallas_call x1, Pallas kernels, on_device(): pl.pallas_call(functools.partial(backward_kernel, heads, head_size), out_...  16.2 us
    all_to_all x1, waiting for transfers between devices, on_device(): mixer_out = lax.all_to_all(z, 'seq', 0, 1, tiled=True)  14.7 us
    pallas_call x1, Pallas kernels, on_device(): pl.pallas_call(functools.partial(forward_kernel, heads, head_size), out_s...  13 us
    convert_element_type x4, local copies, waits for them, and re-layouts, spread(): return jnp.repeat(jnp.exp(rows), head_size, axis=1).astype(bf16)  9.04 us
  transfers between devices with their start and end apart: 8, of which 6 were waited for; matrix products, arithmetic and copies ran while one was open for 17% of the time, Pallas kernels for 4%

profile of v1, /device:TPU:0, one launch (start us, length us, event | category | flops | bytes accessed | tf_op | source)
XLA Modules:
  0.0 341.7 jit_solution(7251946156004573332)
XLA Ops:
  10.6 5.2 %all-to-all-start = ((f32[8,4,256]{2,1,0:T(4,128)}), f32[8,4,256]{2,1,0:T(4,128)S(1)}, u32[]{:S(2)}, u32[]{:S(2)}) async-start(f32[8,4,256]{2,1,0:T(4,128)} %all_to_all.58), calls=%async_computation | async-start | bytes 65536 | tf_op jit(solution)/shard_map/all_to_all | solution.py:199
  17.6 3.1 all-to-all-done
  20.7 3.6 %all-to-all-start.2 = ((bf16[256,8,256]{2,0,1:T(8,128)(2,1)}), bf16[256,8,256]{2,0,1:T(8,128)(2,1)S(1)}, u32[]{:S(2)}, u32[]{:S(2)}) async-start(bf16[256,8,256]{2,0,1:T(8,128)(2,1)} %copy.77), calls=%async_computation.2 | async-start | bytes 2097152 | tf_op jit(solution)/shard_map/all_to_all | solution.py:200
  28.2 7.5 %fusion.10 = (bf16[16,128,4,128]{3,2,1,0:T(4,128)(2,1)S(1)}, bf16[16,128,4,128]{3,2,1,0:T(4,128)(2,1)S(1)}) fusion(f32[128,128]{1,0:T(8,128)S(1)} %fusion.31, f32[16,128,4]{2,1,0:T(8,128)} %copy.70, f32[16,4,128]{2,1,0:T(4,128)S(1)} %copy.69, f32[16,4,128]{2,1,0:T(4,128)S(1)} %copy.68, f32[16,128,4]{2,1,0:T(8,128)} %copy.67, ...), kind=kLoop, calls=%fused_computation.14 | loop fusion | flops 12582912 | bytes 4456448 | tf_op jit(solution)/shard_map/convert_element_type | solution.py:173
  38.8 2.3 copy.72.te_ref
  45.4 2.3 copy.74.en_ref
  53.0 5.8 %all-gather.6.cloned.1.call-done = bf16[2048,512]{1,0:T(8,128)(2,1)} async-done(((bf16[512,512]{1,0:T(8,128)(2,1)}), bf16[2048,512]{1,0:T(8,128)(2,1)}) %all-gather.6.cloned.1.call-update) | async-done | bytes 2097168 | tf_op jit(solution)/shard_map/all_gather | solution.py:198
  58.8 55.0 %all-gather.8.cloned.1.call-done = bf16[1,2048,2048]{2,1,0:T(8,128)(2,1)} async-done(((bf16[1,256,2048]{2,1,0:T(8,128)(2,1)}), bf16[1,2048,2048]{2,1,0:T(8,128)(2,1)}) %all-gather.8.cloned.1.call-update) | async-done | bytes 8388624 | tf_op jit(solution)/shard_map/all_gather | solution.py:194
  113.9 8.5 %fusion.15 = bf16[2048,512]{1,0:T(8,128)(2,1)S(1)} fusion(bf16[2048,512]{1,0:T(8,128)(2,1)} %all-gather.6.cloned.1.call-done, bf16[1,2048,2048]{2,1,0:T(8,128)(2,1)} %all-gather.8.cloned.1.call-done), kind=kOutput, calls=%fused_computation.17 | convolution fusion | flops 4296015872 | bytes 12582912 | tf_op jit(solution)/shard_map/dot_general | solution.py:208
  123.5 13.0 %shard_map.67 = (bf16[2048,256]{1,0:T(8,128)(2,1)}, bf16[2048,256]{1,0:T(8,128)(2,1)S(1)}, bf16[2048,256]{1,0:T(8,128)(2,1)}, bf16[2048,256]{1,0:T(8,128)(2,1)}) custom-call(bf16[2048,256]{1,0:T(8,128)(2,1)} %slice.44.x_ref, bf16[2048,128]{1,0:T(8,128)(2,1)S(1)} %get-tuple-element.22.b_ref, bf16[2048,128]{1,0:T(8,128)(2,1)S(1)} %get-tuple-element.21.c_ref, ...), custom_call_target="tpu_custom_call" | custom-call | tf_op jit(solution)/shard_map/pallas_call | solution.py:216
  138.5 16.2 %shard_map.68 = (bf16[2048,256]{1,0:T(8,128)(2,1)S(1)}, bf16[2048,128]{1,0:T(8,128)(2,1)S(1)}, bf16[2048,128]{1,0:T(8,128)(2,1)S(1)}) custom-call(bf16[2048,256]{1,0:T(8,128)(2,1)} %slice.44.x_ref, bf16[2048,128]{1,0:T(8,128)(2,1)S(1)} %get-tuple-element.22.b_ref, bf16[2048,128]{1,0:T(8,128)(2,1)S(1)} %get-tuple-element.21.c_ref, ...), custom_call_target="tpu_custom_call" | custom-call | tf_op jit(solution)/shard_map/pallas_call | solution.py:231
  154.8 29.1 %all_to_all.80 = bf16[8,256,512]{2,1,0:T(8,128)(2,1)S(1)} all-to-all(bf16[8,256,512]{2,1,0:T(8,128)(2,1)S(1)} %bitcast.122), channel_id=1, replica_groups=mesh['seq'=8,'fsdp'=4] {'seq'}, dimensions={0} | all-to-all | bytes 4194304 | tf_op jit(solution)/shard_map/all_to_all | solution.py:252
  184.2 7.9 %all_to_all.81 = bf16[256,8,32]{0,2,1:T(8,128)(2,1)S(1)} all-to-all(bf16[256,8,32]{0,2,1:T(8,128)(2,1)S(1)} %bitcast.139), channel_id=1, replica_groups=mesh['seq'=8,'fsdp'=4] {'seq'}, dimensions={1} | all-to-all | bytes 262144 | tf_op jit(solution)/shard_map/all_to_all | solution.py:260
  193.1 7.3 %fusion.22 = bf16[2048,288]{0,1:T(8,128)(2,1)} fusion(bf16[1,2048,2048]{2,1,0:T(8,128)(2,1)} %all-gather.8.cloned.1.call-done, bf16[2048,32]{1,0:T(8,128)(2,1)} %bitcast.136, bf16[2048,256]{1,0:T(8,128)(2,1)S(1)} %get-tuple-element.14), kind=kOutput, calls=%fused_computation.22 | convolution fusion | flops 2418868224 | bytes 10747904 | tf_op jit(solution)/shard_map/dot_general | solution.py:27
  200.4 2.5 copy.84
  203.0 2.3 slice.49
  205.4 3.6 %all-to-all-start.1 = ((bf16[8,256,256]{2,1,0:T(8,128)(2,1)}), bf16[8,256,256]{2,1,0:T(8,128)(2,1)S(1)}, u32[]{:S(2)}, u32[]{:S(2)}) async-start(bf16[8,256,256]{2,1,0:T(8,128)(2,1)} %bitcast.17), calls=%async_computation.1 | async-start | bytes 2097152 | tf_op jit(solution)/shard_map/all_to_all | solution.py:229
  209.5 14.7 %all-to-all-done.1 = bf16[8,256,256]{2,1,0:T(8,128)(2,1)S(1)} async-done(((bf16[8,256,256]{2,1,0:T(8,128)(2,1)}), bf16[8,256,256]{2,1,0:T(8,128)(2,1)S(1)}, u32[]{:S(2)}, u32[]{:S(2)}) %all-to-all-start.1) | async-done | bytes 1048608 | tf_op jit(solution)/shard_map/all_to_all | solution.py:229
  225.8 2.3 broadcast_in_dim.74
  228.2 43.2 %all-reduce.3.cloned.1.call-done = bf16[8,4,64,288]{3,2,1,0:T(8,128)(2,1)} async-done(((bf16[8,4,64,288]{3,2,1,0:T(8,128)(2,1)}), bf16[8,4,64,288]{3,2,1,0:T(8,128)(2,1)}) %all-reduce.3.cloned.1.call-update) | async-done | bytes 1179664
  271.4 2.3 dynamic-slice_bitcast_fusion
  273.7 3.6 %all-to-all-start.5 = ((bf16[8,64,288]{2,1,0:T(8,128)(2,1)}), bf16[8,64,288]{2,1,0:T(8,128)(2,1)S(1)}, u32[]{:S(2)}, u32[]{:S(2)}) async-start(bf16[8,64,288]{2,1,0:T(8,128)(2,1)} %dynamic-slice_bitcast_fusion), calls=%async_computation.5 | async-start | bytes 786432 | tf_op jit(solution)/shard_map/all_to_all | solution.py:266
  277.4 49.2 %all-gather.10.cloned.1.call-done = bf16[16384,256]{1,0:T(8,128)(2,1)} async-done(((bf16[2048,256]{1,0:T(8,128)(2,1)}), bf16[16384,256]{1,0:T(8,128)(2,1)}) %all-gather.10.cloned.1.call-update) | async-done | bytes 8388624 | tf_op jit(solution)/shard_map/all_gather | solution.py:255
  326.6 5.9 %convolution_bitcast_fusion = f32[256,2048]{1,0:T(8,128)S(1)} fusion(bf16[8,2048,256]{2,1,0:T(8,128)(2,1)} %bitcast.142, bf16[8,256,512]{2,1,0:T(8,128)(2,1)S(1)} %all_to_all.80), kind=kOutput, calls=%fused_computation.18 | convolution fusion | flops 2147483648 | bytes 11534336 | tf_op jit(solution)/shard_map/dot_general | solution.py:256
  (72 shorter events, 31.3 us)
Async XLA Ops:
  7.2 2.8 copy-start.4
  7.2 8.9 %copy-start.3 = (bf16[1,256,2048]{2,1,0:T(8,128)(2,1)S(1)}, bf16[1,256,2048]{2,1,0:T(8,128)(2,1)}, u32[]{:S(2)}) copy-start(bf16[1,256,2048]{2,1,0:T(8,128)(2,1)} %param.7) | copy-start | bytes 3145732
  7.2 51.6 %all-gather.6.cloned.1.call-start = ((), (), s32[]{:S(2)}) async-start(), calls=%async_computation.6 | async-start | bytes 2621440 | tf_op jit(solution)/shard_map/all_gather | solution.py:198
  9.2 104.6 %all-gather.8.cloned.1.call-start = ((), (), s32[]{:S(2)}) async-start(), calls=%async_computation.7 | async-start | bytes 9437184 | tf_op jit(solution)/shard_map/all_gather | solution.py:194
  10.6 10.0 %all-to-all-start = ((f32[8,4,256]{2,1,0:T(4,128)}), f32[8,4,256]{2,1,0:T(4,128)S(1)}, u32[]{:S(2)}, u32[]{:S(2)}) async-start(f32[8,4,256]{2,1,0:T(4,128)} %all_to_all.58), calls=%async_computation | async-start | bytes 65536 | tf_op jit(solution)/shard_map/all_to_all | solution.py:199
  20.7 116.8 %all-to-all-start.2 = ((bf16[256,8,256]{2,0,1:T(8,128)(2,1)}), bf16[256,8,256]{2,0,1:T(8,128)(2,1)S(1)}, u32[]{:S(2)}, u32[]{:S(2)}) async-start(bf16[256,8,256]{2,0,1:T(8,128)(2,1)} %copy.77), calls=%async_computation.2 | async-start | bytes 2097152 | tf_op jit(solution)/shard_map/all_to_all | solution.py:200
  24.2 247.1 %all-reduce.3.cloned.1.call-start = ((), (), s32[]{:S(2)}) async-start(), calls=%async_computation.9 | async-start | bytes 3145728
  136.5 1.0 copy-start
  137.5 1.0 copy-start.1
  203.0 6.0 %copy-start.5 = (u32[32]{0:T(128)S(1)}, u32[32]{0:T(128)}, u32[]{:S(2)}) copy-start(u32[32]{0:T(128)} %constant.56) | copy-start | bytes 388
  203.0 123.6 %all-gather.10.cloned.1.call-start = ((), (), s32[]{:S(2)}) async-start(), calls=%async_computation.8 | async-start | bytes 9437184 | tf_op jit(solution)/shard_map/all_gather | solution.py:255
  205.4 18.9 %all-to-all-start.1 = ((bf16[8,256,256]{2,1,0:T(8,128)(2,1)}), bf16[8,256,256]{2,1,0:T(8,128)(2,1)S(1)}, u32[]{:S(2)}, u32[]{:S(2)}) async-start(bf16[8,256,256]{2,1,0:T(8,128)(2,1)} %bitcast.17), calls=%async_computation.1 | async-start | bytes 2097152 | tf_op jit(solution)/shard_map/all_to_all | solution.py:229
  273.7 60.2 %all-to-all-start.5 = ((bf16[8,64,288]{2,1,0:T(8,128)(2,1)}), bf16[8,64,288]{2,1,0:T(8,128)(2,1)S(1)}, u32[]{:S(2)}, u32[]{:S(2)}) async-start(bf16[8,64,288]{2,1,0:T(8,128)(2,1)} %dynamic-slice_bitcast_fusion), calls=%async_computation.5 | async-start | bytes 786432 | tf_op jit(solution)/shard_map/all_to_all | solution.py:266
  326.6 5.9 %copy-start.2 = (bf16[2048,512]{1,0:T(8,128)(2,1)S(1)}, bf16[2048,512]{1,0:T(8,128)(2,1)}, u32[]{:S(2)}) copy-start(bf16[2048,512]{1,0:T(8,128)(2,1)} %all-gather.6.cloned.1.call-done) | copy-start | bytes 6291460
Sparse Core Ops, SparseCore 0:
  10.2 48.6 all-gather.5
  60.7 53.0 all-gather.7
  203.1 68.2 all-reduce.2
  273.1 53.4 all-gather.9

commit v2 on v1

--- a/solution.py
+++ b/solution.py
@@ -43,9 +43,13 @@
     return (tiled * decays.astype(f32)).astype(bf16)
 
 
+def relative_chunk(k, place_ref, per_block):
+    return lax.bitwise_xor(k // per_block, place_ref[0]) * per_block + k % per_block
+
+
 def forward_kernel(
-    heads, head_size,
-    x_ref, b_ref, c_ref, m_ref, te_ref, fs_ref, en_ref, lv_ref, dt_ref, mean_ref,
+    heads, head_size, per_block,
+    place_ref, x_ref, b_ref, c_ref, m_ref, te_ref, fs_ref, en_ref, lv_ref, dt_ref, mean_ref,
     z_ref, rs_ref, sf_ref, rn_ref,
     carry,
 ):
@@ -54,7 +58,7 @@
     carry[...] = jnp.zeros_like(carry)
 
     def reverse_states(i, _):
-        k = chunks - 1 - i
+        k = relative_chunk(chunks - 1 - i, place_ref, per_block)
         rows = pl.ds(pl.multiple_of(k * CHUNK, CHUNK), CHUNK)
         state = pl.ds(pl.multiple_of(k * state_size, state_size), state_size)
         rn_ref[state, :] = carry[...].astype(bf16)
@@ -65,7 +69,8 @@
     lax.fori_loop(0, chunks, reverse_states, 0, unroll=2)
     carry[...] = jnp.zeros_like(carry)
 
-    def outputs(k, _):
+    def outputs(i, _):
+        k = relative_chunk(i, place_ref, per_block)
         rows = pl.ds(pl.multiple_of(k * CHUNK, CHUNK), CHUNK)
         state = pl.ds(pl.multiple_of(k * state_size, state_size), state_size)
         x, b, c = x_ref[rows, :], b_ref[rows, :], c_ref[rows, :]
@@ -86,8 +91,8 @@
 
 
 def backward_kernel(
-    heads, head_size,
-    x_ref, b_ref, c_ref, m_ref, mt_ref, te_ref, fs_ref, en_ref, lv_ref, dt_ref, mean_ref,
+    heads, head_size, per_block,
+    place_ref, x_ref, b_ref, c_ref, m_ref, mt_ref, te_ref, fs_ref, en_ref, lv_ref, dt_ref, mean_ref,
     z_ref, rs_ref, sf_ref, rn_ref, g_ref,
     dx_ref, db_ref, dc_ref,
     carry, dy_ref, ge_ref,
@@ -97,7 +102,7 @@
     carry[...] = jnp.zeros_like(carry)
 
     def end_adjoints(i, _):
-        k = chunks - 1 - i
+        k = relative_chunk(chunks - 1 - i, place_ref, per_block)
         rows = pl.ds(pl.multiple_of(k * CHUNK, CHUNK), CHUNK)
         state = pl.ds(pl.multiple_of(k * state_size, state_size), state_size)
         g, z = g_ref[rows, :].astype(f32), z_ref[rows, :].astype(f32)
@@ -111,7 +116,8 @@
     lax.fori_loop(0, chunks, end_adjoints, 0, unroll=2)
     carry[...] = jnp.zeros_like(carry)
 
-    def gradients(k, _):
+    def gradients(i, _):
+        k = relative_chunk(i, place_ref, per_block)
         rows = pl.ds(pl.multiple_of(k * CHUNK, CHUNK), CHUNK)
         state = pl.ds(pl.multiple_of(k * state_size, state_size), state_size)
         x, b, c, dy = x_ref[rows, :], b_ref[rows, :], c_ref[rows, :], dy_ref[rows, :]
@@ -139,8 +145,101 @@
     lax.fori_loop(0, chunks, gradients, 0, unroll=2)
 
 
+def project_kernel(pieces, slots, *refs):
+    piece_refs, (w_ref, x_ref, b_ref, c_ref, held, sems) = refs[:pieces], refs[pieces:]
+    rows = held.shape[1]
+    width, state_size = x_ref.shape[1], b_ref.shape[1]
+
+    def fetch(i):
+        return pltpu.make_async_copy(piece_refs[i], held.at[i % slots], sems.at[i % slots])
+
+    for i in range(min(slots, pieces)):
+        fetch(i).start()
+    for i in range(pieces):
+        fetch(i).wait()
+        result = dot_nn(held[i % slots], w_ref[...]).astype(bf16)
+        if i + slots < pieces:
+            fetch(i + slots).start()
+        x_ref[i * rows : (i + 1) * rows, :] = result[:, :width]
+        b_ref[i * rows : (i + 1) * rows, :] = result[:, width : width + state_size]
+        c_ref[i * rows : (i + 1) * rows, :] = result[:, width + state_size :]
+
+
+def weight_kernel(pieces, slots, *refs):
+    piece_refs, (grad_ref, out_ref, held, total, sems) = refs[:pieces], refs[pieces:]
+    rows = held.shape[1]
+    hidden = held.shape[2]
+    tile = 256 if hidden % 256 == 0 else hidden
+
+    def fetch(i):
+        return pltpu.make_async_copy(piece_refs[i], held.at[i % slots], sems.at[i % slots])
+
+    for i in range(slots):
+        fetch(i).start()
+    for first in range(0, pieces, slots):
+        for i in range(first, first + slots):
+            fetch(i).wait()
+        grad = grad_ref[:, first * rows : (first + slots) * rows]
+        for t in range(0, hidden, tile):
+            block = held[:, :, t : t + tile].reshape(slots * rows, tile)
+            term = dot_nn(grad, block)
+            if first > 0:
+                term = term + total[:, t : t + tile]
+            if first + slots < pieces:
+                total[:, t : t + tile] = term
+            else:
+                out_ref[t : t + tile, :] = term.T.astype(bf16)
+        for i in range(first + slots, min(first + 2 * slots, pieces)):
+            fetch(i).start()
+
+
 def whole(count):
     return [pl.BlockSpec(memory_space=pltpu.VMEM)] * count
+
+
+def permute_xor(a, axis, mask):
+    count = lax.axis_size(axis)
+    return lax.ppermute(a, axis, [(i, i ^ mask) for i in range(count)])
+
+
+def gather_halves(rows, axis):
+    count = lax.axis_size(axis)
+    bits = count.bit_length() - 1
+    half = rows.shape[0] // 2
+    upper = list(range(1, bits))
+    orders = (upper + [0], upper[1:] + upper[:1] + [0])
+    held = ({0: rows[:half]}, {0: rows[half:]})
+    for step in range(bits):
+        for part in range(2):
+            mask = 1 << orders[part][step]
+            for r in list(held[part]):
+                held[part][r ^ mask] = permute_xor(held[part][r], axis, mask)
+    return [held[part][r] for r in range(count) for part in range(2)]
+
+
+def gather_line(rows, axis):
+    count = lax.axis_size(axis)
+    extent = rows.shape[0]
+    up, down = [rows], [rows]
+    for d in range(1, count):
+        up.append(lax.ppermute(up[-1], axis, [(i, i + 1) for i in range(d - 1, count - 1)]))
+        down.append(lax.ppermute(down[-1], axis, [(i, i - 1) for i in range(1, count - d + 1)]))
+    line = jnp.concatenate(up[:0:-1] + [rows] + down[1:], axis=0)
+    start = (count - 1 - lax.axis_index(axis)) * extent
+    return lax.dynamic_slice_in_dim(line, start, count * extent, 0)
+
+
+def exchange_xor(pieces, axis):
+    return [pieces[0]] + [permute_xor(p, axis, r) for r, p in enumerate(pieces) if r > 0]
+
+
+def in_order(pieces, place, axis):
+    stacked = jnp.stack(pieces)
+    ordered = [
+        lax.dynamic_index_in_dim(stacked, lax.bitwise_xor(place, j), 0, False)
+        for j in range(len(pieces))
+    ]
+    return jnp.concatenate(ordered, axis=axis)
 
 
 def decay_tables(log_rates, head_size):
@@ -185,19 +284,40 @@
     seq_count = lax.axis_size("seq")
     fsdp_count = lax.axis_size("fsdp")
     place = lax.axis_index("seq")
+    row_place = lax.axis_index("fsdp")
     heads = head_count // seq_count
     width = heads * head_size
     length = token_count * seq_count
     shared = 2 * state_size
     shared_part = shared // seq_count
-
-    all_tokens = lax.all_gather(local_tokens, "seq", axis=0, tiled=True)
-    own_columns = jnp.concatenate(
-        [lax.dynamic_slice_in_dim(w_in, place * width, width, 1), w_in[:, inner_width:]], axis=1
-    )
-    w_columns = lax.all_gather(own_columns, "fsdp", axis=0, tiled=True)
-    log_rates = lax.all_to_all(log_decay[0], "seq", 0, 1, tiled=True)
-    g = lax.all_to_all(upstream, "seq", 1, 0, tiled=True)
+    chunks = length // CHUNK
+    per_block = token_count // CHUNK
+    relative = range(seq_count)
+    shape = jax.ShapeDtypeStruct
+    params = pltpu.CompilerParams(vmem_limit_bytes=VMEM_LIMIT)
+
+    def columns_of(array, r):
+        return lax.dynamic_slice_in_dim(array, lax.bitwise_xor(place, r) * width, width, 1)
+
+    pieces = gather_halves(local_tokens, "seq")
+    parity = place % 2
+    shared_half = lax.dynamic_slice_in_dim(w_in, inner_width + parity * state_size, state_size, 1)
+    first_columns = gather_line(
+        jnp.concatenate([columns_of(w_in, 0), shared_half], axis=1), "fsdp"
+    )
+    w_own, w_half = first_columns[:, :width], first_columns[:, width:]
+    w_other = permute_xor(w_half, "seq", 1)
+    w_shared = jnp.where(
+        parity == 0,
+        jnp.concatenate([w_half, w_other], axis=1),
+        jnp.concatenate([w_other, w_half], axis=1),
+    )
+    w_columns = jnp.concatenate([w_own, w_shared], axis=1)
+
+    log_pieces = lax.all_to_all(log_decay[0], "seq", 0, 0, tiled=True)
+    log_pieces = log_pieces.reshape(seq_count, heads, token_count)
+    log_rates = in_order([log_pieces[r] for r in relative], place, 1)
+    g = jnp.concatenate(exchange_xor([columns_of(upstream, r) for r in relative], "seq"), axis=0)
     to_end, from_start, enter, leave, chunk_decay, decays, turned = decay_tables(
         log_rates, head_size
     )
@@ -205,37 +325,66 @@
     head_col = lax.broadcasted_iota(jnp.int32, (width, width), 1) // head_size
     mean_over_head = jnp.where(head_row == head_col, 1.0 / head_size, 0.0).astype(bf16)
 
-    xbc = jnp.dot(all_tokens, w_columns, preferred_element_type=f32).astype(bf16)
-    x = xbc[:, :width]
-    b = xbc[:, width : width + state_size]
-    c = xbc[:, width + state_size :]
-
-    chunks = length // CHUNK
-    shape = jax.ShapeDtypeStruct
-    params = pltpu.CompilerParams(vmem_limit_bytes=VMEM_LIMIT)
+    count = len(pieces)
+    slots = min(count, 16)
+    streamed = [pl.BlockSpec(memory_space=pl.ANY)] * count
+    x, b, c = pl.pallas_call(
+        functools.partial(project_kernel, count, slots),
+        out_shape=[
+            shape((length, width), bf16),
+            shape((length, state_size), bf16),
+            shape((length, state_size), bf16),
+        ],
+        in_specs=streamed + whole(1),
+        out_specs=whole(3),
+        scratch_shapes=[
+            pltpu.VMEM((slots,) + pieces[0].shape, bf16),
+            pltpu.SemaphoreType.DMA((slots,)),
+        ],
+        compiler_params=params,
+        cost_estimate=pl.CostEstimate(
+            flops=2 * length * hidden_width * (width + shared),
+            bytes_accessed=2 * length * hidden_width,
+            transcendentals=0,
+        ),
+    )(*pieces, w_columns)
+
+    scalar = [pl.BlockSpec(memory_space=pltpu.SMEM)]
+    place_word = place.astype(jnp.int32).reshape(1)
+    mixer_cost = pl.CostEstimate(
+        flops=60 * length * width * CHUNK, bytes_accessed=40 * length * width, transcendentals=0
+    )
     z, inverse, states_in, states_next = pl.pallas_call(
-        functools.partial(forward_kernel, heads, head_size),
+        functools.partial(forward_kernel, heads, head_size, per_block),
         out_shape=[
             shape((length, width), bf16),
             shape((length, width), bf16),
             shape((chunks * state_size, width), bf16),
             shape((chunks * state_size, width), bf16),
         ],
-        in_specs=whole(10),
+        in_specs=scalar + whole(10),
         out_specs=whole(4),
         scratch_shapes=[pltpu.VMEM((state_size, width), f32)],
         compiler_params=params,
-    )(x, b, c, decays, to_end, from_start, enter, leave, chunk_decay, mean_over_head)
-    mixer_out = lax.all_to_all(z, "seq", 0, 1, tiled=True)
+        cost_estimate=mixer_cost,
+    )(place_word, x, b, c, decays, to_end, from_start, enter, leave, chunk_decay, mean_over_head)
+    blocks = lambda a: [a[r * token_count : (r + 1) * token_count] for r in relative]
+    mixer_out = in_order(exchange_xor(blocks(z), "seq"), place, 1)
+
+    rest = jnp.concatenate([columns_of(w_in, r) for r in relative if r % 2 == 0 and r > 0], axis=1)
+    rest, first_columns = lax.optimization_barrier((rest, first_columns))
+    w_even = gather_line(rest, "fsdp")
+    w_even = jnp.concatenate([w_own, w_even], axis=1)
+    w_odd = permute_xor(w_even, "seq", 1)
 
     dx, db, dc = pl.pallas_call(
-        functools.partial(backward_kernel, heads, head_size),
+        functools.partial(backward_kernel, heads, head_size, per_block),
         out_shape=[
             shape((length, width), bf16),
             shape((length, state_size), bf16),
             shape((length, state_size), bf16),
         ],
-        in_specs=whole(16),
+        in_specs=scalar + whole(16),
         out_specs=whole(3),
         scratch_shapes=[
             pltpu.VMEM((state_size, width), f32),
@@ -243,34 +392,59 @@
             pltpu.VMEM((chunks * state_size, width), bf16),
         ],
         compiler_params=params,
+        cost_estimate=mixer_cost,
     )(
-        x, b, c, decays, turned, to_end, from_start, enter, leave, chunk_decay, mean_over_head,
-        z, inverse, states_in, states_next, g,
-    )
-
-    packed = jnp.concatenate([dx, db, dc], axis=1).reshape(seq_count, token_count, width + shared)
-    arrived = lax.all_to_all(packed, "seq", 0, 0)
-    grad_heads = arrived[:, :, :width]
-    grad_shared = jnp.sum(arrived[:, :, width:].astype(f32), axis=0).astype(bf16)
-    w_heads = lax.all_gather(w_columns[:, :width], "seq")
-    grad_tokens = lax.dot_general(
-        grad_heads, w_heads, (((0, 2), (0, 2)), ((), ())), preferred_element_type=f32
-    ) + dot_nt(grad_shared, w_columns[:, width:])
-
-    shared_columns = lax.all_to_all(grad_shared, "seq", 1, 0, tiled=True)
-    grad_columns = jnp.concatenate([dx, shared_columns], axis=1)
-    partial = dot_tn(all_tokens, grad_columns).astype(bf16)
+        place_word, x, b, c, decays, turned, to_end, from_start, enter, leave, chunk_decay,
+        mean_over_head, z, inverse, states_in, states_next, g,
+    )
+
+    shared_grads = exchange_xor(blocks(jnp.concatenate([db, dc], axis=1)), "seq")
+    head_grads = exchange_xor(blocks(dx), "seq")
+    grad_shared = sum(a.astype(f32) for a in shared_grads).astype(bf16)
+    even_grads = jnp.concatenate([head_grads[r] for r in relative if r % 2 == 0], axis=1)
+    odd_grads = jnp.concatenate([head_grads[r] for r in relative if r % 2 == 1], axis=1)
+    grad_tokens = dot_nt(even_grads, w_even) + dot_nt(odd_grads, w_odd)
+    grad_tokens = grad_tokens + dot_nt(grad_shared, w_shared)
+
     rows_each = hidden_width // (seq_count * fsdp_count)
-    partial = partial.reshape(seq_count, fsdp_count, rows_each, width + shared_part)
-    summed = lax.psum_scatter(partial, "fsdp", scatter_dimension=1, tiled=False)
-    owned = lax.all_to_all(summed, "seq", 0, 0).astype(f32)
-    grad_weights = jnp.concatenate(
-        [
-            owned[:, :, :width].transpose(1, 0, 2).reshape(rows_each, inner_width),
-            owned[:, :, width:].transpose(1, 0, 2).reshape(rows_each, shared),
-        ],
-        axis=1,
-    )
+
+    def weight_columns(grad_t):
+        columns = grad_t.shape[0]
+        partial = pl.pallas_call(
+            functools.partial(weight_kernel, count, slots),
+            out_shape=shape((hidden_width, columns), bf16),
+            in_specs=streamed + whole(1),
+            out_specs=whole(1)[0],
+            scratch_shapes=[
+                pltpu.VMEM((slots,) + pieces[0].shape, bf16),
+                pltpu.VMEM((columns, hidden_width), f32),
+                pltpu.SemaphoreType.DMA((slots,)),
+            ],
+            compiler_params=params,
+            cost_estimate=pl.CostEstimate(
+                flops=2 * length * hidden_width * columns,
+                bytes_accessed=2 * length * hidden_width,
+                transcendentals=0,
+            ),
+        )(*pieces, grad_t)
+        partial = partial.reshape(seq_count, fsdp_count, rows_each, columns)
+        parts = [
+            lax.dynamic_index_in_dim(partial, lax.bitwise_xor(row_place, k), 1, False)
+            for k in range(fsdp_count)
+        ]
+        arrived = exchange_xor(parts, "fsdp")
+        summed = sum(a.astype(f32) for a in arrived).astype(bf16)
+        owned = lax.all_to_all(summed, "seq", 0, 0).astype(f32)
+        return owned.transpose(1, 0, 2).reshape(rows_each, seq_count * columns)
+
+    head_part = weight_columns(dx.T)
+    turned_shared = grad_shared.T.reshape(seq_count, shared_part, token_count)
+    sent = [
+        lax.dynamic_index_in_dim(turned_shared, lax.bitwise_xor(place, r), 0, False)
+        for r in relative
+    ]
+    shared_t = jnp.concatenate(exchange_xor(sent, "seq"), axis=1)
+    grad_weights = jnp.concatenate([head_part, weight_columns(shared_t)], axis=1)
     return mixer_out[None], grad_tokens.astype(bf16)[None], grad_weights
 
 

time: 343 us -> 334 us (0.974)
  waiting for transfers between devices: 172 us -> 94.7 us
  starting transfers between devices: 16.1 us -> 89.6 us
  blocking collectives: 37.1 us -> 0 us
  local copies, waits for them, and re-layouts: 39.4 us -> 71.3 us
  Pallas kernels: 29.2 us -> 50.6 us
  matrix products: 23.1 us -> 6.6 us
  between operations: 14 us -> 1.86 us
  other arithmetic: 11 us -> 17.4 us
    all_gather x3 -> x0, waiting for transfers between devices: 110 us -> none  [the longest x1 55 us: on_device(): all_tokens = lax.all_gather(local_tokens, 'seq', axis=0, tiled=True)]
    ppermute x0 -> x69, waiting for transfers between devices: none -> 89.2 us  [the longest x57 54.1 us: permute_xor(): return lax.ppermute(a, axis, [(i, i ^ mask) for i in range(count)])]
    ppermute x0 -> x69, starting transfers between devices: none -> 78.7 us  [the longest x57 54.8 us: permute_xor(): return lax.ppermute(a, axis, [(i, i ^ mask) for i in range(count)])]
    unnamed x5 -> x0, waiting for transfers between devices: 43.9 us -> none
    unnamed x18 -> x148, local copies, waits for them, and re-layouts: 6.39 us -> 44.7 us
    all_to_all x2 -> x0, blocking collectives: 37.1 us -> none  [the longest x1 29.1 us: on_device(): arrived = lax.all_to_all(packed, 'seq', 0, 0)]
    dot_general x3 -> x0, matrix products: 21.7 us -> none  [the longest x1 8.5 us: on_device(): jnp.dot(all_tokens, w_columns, preferred_element_type=f32).astype(bf16)]
    pallas_call x2 -> x5, Pallas kernels: 29.2 us -> 50.6 us  [the longest x1 16.2 us: on_device(): pl.pallas_call(functools.partial(backward_kernel, heads, head_size, per_b...]
  transfers between devices with their start and end apart: 8 -> 72, of which waited for: 6 -> 21; matrix products, arithmetic and copies ran while one was open for 17% -> 25% of each run, Pallas kernels for 4% -> 15%
where the time goes in v2:
time: 334 us; the launch traced here: 332 us
  waiting for transfers between devices  94.7 us (28%)
  starting transfers between devices  89.6 us (27%)
  local copies, waits for them, and re-layouts  71.3 us (21%)
  Pallas kernels  50.6 us (15%)
  other arithmetic  17.4 us (5%)
  matrix products  6.6 us (2%)
    ppermute x57, starting transfers between devices, permute_xor(): return lax.ppermute(a, axis, [(i, i ^ mask) for i in range(count)])  54.8 us
    ppermute x57, waiting for transfers between devices, permute_xor(): return lax.ppermute(a, axis, [(i, i ^ mask) for i in range(count)])  54.1 us
    unnamed x148, local copies, waits for them, and re-layouts  44.7 us
    ppermute x6, waiting for transfers between devices, gather_line(): lax.ppermute(down[-1], axis, [(i, i - 1) for i in range(1, count - d + 1)])  35 us
    pallas_call x1, Pallas kernels, on_device(): pl.pallas_call(functools.partial(backward_kernel, heads, head_size, per_b...  16.2 us
    ppermute x6, starting transfers between devices, gather_line(): lax.ppermute(up[-1], axis, [(i, i + 1) for i in range(d - 1, count - 1)])  15.9 us
    pallas_call x1, Pallas kernels, on_device(): pl.pallas_call(functools.partial(forward_kernel, heads, head_size, per_bl...  12.5 us
    pallas_call x2, Pallas kernels, weight_columns(): pl.pallas_call(functools.partial(weight_kernel, count, slots), out_shape=...  11.8 us
  transfers between devices with their start and end apart: 72, of which 21 were waited for; matrix products, arithmetic and copies ran while one was open for 25% of the time, Pallas kernels for 15%

profile of v2, /device:TPU:0, one launch (start us, length us, event | category | flops | bytes accessed | tf_op | source)
XLA Modules:
  0.0 332.0 jit_solution(9367086026417612218)
XLA Ops:
  3.8 5.7 %collective-permute-start.14 = (bf16[512,384]{1,0:T(8,128)(2,1)}, bf16[512,384]{1,0:T(8,128)(2,1)}, u32[]{:S(2)}, u32[]{:S(2)}) collective-permute-start(bf16[512,384]{1,0:T(8,128)(2,1)} %pad_maximum_fusion.3), channel_id=1, source_target_pairs={{0,1},{1,2},{2,3},{4,5},{5,6},{6,7},{8,9},{9,10},{10,11},{12,13},{... | collective-permute-start | bytes 1179656 | tf_op jit(solution)/shard_map/ppermute | solution.py:225
  10.9 3.7 %all-to-all-start = ((f32[8,4,256]{2,1,0:T(4,128)}), f32[8,4,256]{2,1,0:T(4,128)S(1)}, u32[]{:S(2)}, u32[]{:S(2)}) async-start(f32[8,4,256]{2,1,0:T(4,128)} %all_to_all.12), calls=%async_computation | async-start | bytes 65536 | tf_op jit(solution)/shard_map/all_to_all | solution.py:317
  25.9 6.4 %fusion.6 = (bf16[16,128,4,128]{3,2,1,0:T(4,128)(2,1)}, bf16[16,128,4,128]{3,2,1,0:T(4,128)(2,1)S(1)}) fusion(f32[128,128]{1,0:T(8,128)S(1)} %fusion.32, f32[16,128,4]{2,1,0:T(8,128)S(1)} %copy.30, f32[16,4,128]{2,1,0:T(4,128)S(1)} %copy.29, f32[16,4,128]{2,1,0:T(4,128)S(1)} %copy.28, f32[16,128,4]{2,1,0:T(8,128)S(1)} %copy.27, ...), kind=kLoop, calls=%fused_computation.10 | loop fusion | flops 12582912 | bytes 4456448 | tf_op jit(solution)/shard_map/convert_element_type | solution.py:272
  38.3 2.7 collective-permute-done.32
  41.6 8.9 %collective-permute-done.33 = bf16[256,256]{1,0:T(8,128)(2,1)S(1)} collective-permute-done((bf16[256,256]{1,0:T(8,128)(2,1)S(1)}, bf16[256,256]{1,0:T(8,128)(2,1)S(1)}, u32[]{:S(2)}, u32[]{:S(2)}) %collective-permute-start.33) | collective-permute-done | bytes 131104 | tf_op jit(solution)/shard_map/ppermute | solution.py:202
  60.9 3.3 %copy.79 = bf16[256,8,4,128]{3,1,2,0:T(8,128)(2,1)} copy(bf16[256,8,4,128]{3,2,1,0:T(4,128)(2,1)} %bitcast.179) | data formatting | bytes 4194304
  74.4 4.9 %collective-permute-start.38 = (bf16[512,768]{1,0:T(8,128)(2,1)S(1)}, bf16[512,768]{1,0:T(8,128)(2,1)S(1)}, u32[]{:S(2)}, u32[]{:S(2)}) collective-permute-start(bf16[512,768]{1,0:T(8,128)(2,1)S(1)} %copy-done.23), channel_id=1, source_target_pairs={{0,1},{1,2},{2,3},{4,5},{5,6},{6,7},{8,9},{9,10},{10,11},{12,13},{... | collective-permute-start | bytes 2359304 | tf_op jit(solution)/shard_map/ppermute | solution.py:225
  84.8 25.0 %collective-permute-done.19 = bf16[512,384]{1,0:T(8,128)(2,1)S(1)} collective-permute-done((bf16[512,384]{1,0:T(8,128)(2,1)S(1)}, bf16[512,384]{1,0:T(8,128)(2,1)S(1)}, u32[]{:S(2)}, u32[]{:S(2)}) %collective-permute-start.19) | collective-permute-done | bytes 393248 | tf_op jit(solution)/shard_map/ppermute | solution.py:226
  116.2 7.1 %collective-permute-done.10.refs_12_ = bf16[128,2048]{1,0:T(8,128)(2,1)S(1)} collective-permute-done((bf16[128,2048]{1,0:T(8,128)(2,1)S(1)}, bf16[128,2048]{1,0:T(8,128)(2,1)S(1)}, u32[]{:S(2)}, u32[]{:S(2)}) %collective-permute-start.10) | collective-permute-done | bytes 524320 | tf_op jit(solution)/shard_map/ppermute | solution.py:202
  135.2 10.1 %shard_map.67 = (bf16[2048,256]{1,0:T(8,128)(2,1)}, bf16[2048,128]{1,0:T(8,128)(2,1)S(1)}, bf16[2048,128]{1,0:T(8,128)(2,1)S(1)}) custom-call(bf16[128,2048]{1,0:T(8,128)(2,1)S(1)} %get-tuple-element.64.refs_0_, bf16[128,2048]{1,0:T(8,128)(2,1)S(1)} %get-tuple-element.63.refs_1_, bf16[128,2048]{1,0:T(8,128)(2,1)S(1)} %collective-permute-done.refs_2_, ...), custom_call_target="tpu_custom_call" | custom-call | flops 4294967296 | bytes 8388608 | tf_op jit(solution)/shard_map/pallas_call | solution.py:331
  145.3 12.5 %shard_map.68 = (bf16[2048,256]{1,0:T(8,128)(2,1)S(1)}, bf16[2048,256]{1,0:T(8,128)(2,1)S(1)}, bf16[2048,256]{1,0:T(8,128)(2,1)}, bf16[2048,256]{1,0:T(8,128)(2,1)}) custom-call(s32[1]{0:T(128)} %bitcast.place_ref, bf16[2048,256]{1,0:T(8,128)(2,1)} %get-tuple-element.14.x_ref, bf16[2048,128]{1,0:T(8,128)(2,1)S(1)} %get-tuple-element.15.b_ref, ...), custom_call_target="tpu_custom_call" | custom-call | flops 4026531840 | bytes 20971520 | tf_op jit(solution)/shard_map/pallas_call | solution.py:357
  160.0 16.2 %shard_map.69 = (bf16[2048,256]{1,0:T(8,128)(2,1)S(1)}, bf16[2048,128]{1,0:T(8,128)(2,1)S(1)}, bf16[2048,128]{1,0:T(8,128)(2,1)S(1)}) custom-call(s32[1]{0:T(128)} %bitcast.place_ref, bf16[2048,256]{1,0:T(8,128)(2,1)} %get-tuple-element.14.x_ref, bf16[2048,128]{1,0:T(8,128)(2,1)S(1)} %get-tuple-element.15.b_ref, ...), custom_call_target="tpu_custom_call" | custom-call | flops 4026531840 | bytes 20971520 | tf_op jit(solution)/shard_map/pallas_call | solution.py:380
  183.5 7.3 %shard_map.70 = bf16[2048,256]{1,0:T(8,128)(2,1)} custom-call(bf16[128,2048]{1,0:T(8,128)(2,1)S(1)} %get-tuple-element.64.refs_0_, bf16[128,2048]{1,0:T(8,128)(2,1)S(1)} %get-tuple-element.63.refs_1_, bf16[128,2048]{1,0:T(8,128)(2,1)S(1)} %copy-done.6, bf16[128,2048]{1,0:T(8,128)(2,1)S(1)} %copy-done.9, bf16[128,2048]{1,0:T(8,128)(2,1)S(1)} %copy-done.2, ...), custom_call_target="tpu_custom_call" | custom-call | flops 2147483648 | bytes 8388608 | tf_op jit(solution)/shard_map/pallas_call | solution.py:413
  206.7 3.9 %collective-permute-done.53 = bf16[256,256]{1,0:T(8,128)(2,1)S(1)} collective-permute-done((bf16[256,256]{1,0:T(8,128)(2,1)S(1)}, bf16[256,256]{1,0:T(8,128)(2,1)S(1)}, u32[]{:S(2)}, u32[]{:S(2)}) %collective-permute-start.53) | collective-permute-done | bytes 131104 | tf_op jit(solution)/shard_map/ppermute | solution.py:202
  210.6 9.4 %collective-permute-start.56 = (bf16[8,64,256]{2,1,0:T(8,128)(2,1)}, bf16[8,64,256]{2,1,0:T(8,128)(2,1)}, u32[]{:S(2)}, u32[]{:S(2)}) collective-permute-start(bf16[8,64,256]{2,1,0:T(8,128)(2,1)} %get-tuple-element.31), channel_id=1, source_target_pairs={{0,1},{1,0},{2,3},{3,2},{4,5},{5,4},{6,7},{7,6},{8,9},{9,8},{10,11... | collective-permute-start | bytes 786440 | tf_op jit(solution)/shard_map/ppermute | solution.py:202
  229.7 10.0 %collective-permute-done.43 = bf16[512,768]{1,0:T(8,128)(2,1)S(1)} collective-permute-done((bf16[512,768]{1,0:T(8,128)(2,1)}, bf16[512,768]{1,0:T(8,128)(2,1)S(1)}, u32[]{:S(2)}, u32[]{:S(2)}) %collective-permute-start.43) | collective-permute-done | bytes 786464 | tf_op jit(solution)/shard_map/ppermute | solution.py:226
  248.5 2.9 collective-permute-done.26
  275.3 4.5 %shard_map.71 = bf16[2048,32]{1,0:T(8,128)(2,1)S(1)} custom-call(bf16[128,2048]{1,0:T(8,128)(2,1)S(1)} %get-tuple-element.64.refs_0_, bf16[128,2048]{1,0:T(8,128)(2,1)S(1)} %get-tuple-element.63.refs_1_, bf16[128,2048]{1,0:T(8,128)(2,1)S(1)} %copy-done.7, bf16[128,2048]{1,0:T(8,128)(2,1)S(1)} %copy-done.10, bf16[128,2048]{1,0:T(8,128)(2,1)S(1)} %copy-done.2, ...), custom_call_target="tpu_custom_call" | custom-call | flops 268435456 | bytes 8388608 | tf_op jit(solution)/shard_map/pallas_call | solution.py:413
  286.4 6.7 %collective-permute-done.67 = bf16[8,64,32]{1,2,0:T(8,128)(2,1)S(1)} collective-permute-done((bf16[8,64,32]{1,2,0:T(8,128)(2,1)S(1)}, bf16[8,64,32]{1,2,0:T(8,128)(2,1)S(1)}, u32[]{:S(2)}, u32[]{:S(2)}) %collective-permute-start.67) | collective-permute-done | bytes 32800 | tf_op jit(solution)/shard_map/ppermute | solution.py:202
  294.8 4.5 %collective-permute-done.68 = bf16[8,64,32]{1,2,0:T(8,128)(2,1)S(1)} collective-permute-done((bf16[8,64,32]{1,2,0:T(8,128)(2,1)S(1)}, bf16[8,64,32]{1,2,0:T(8,128)(2,1)S(1)}, u32[]{:S(2)}, u32[]{:S(2)}) %collective-permute-start.68) | collective-permute-done | bytes 32800 | tf_op jit(solution)/shard_map/ppermute | solution.py:202
  300.1 3.3 %all-to-all-start.2 = ((bf16[8,2,1024]{2,1,0:T(2,128)(2,1)}), bf16[8,2,1024]{2,1,0:T(2,128)(2,1)S(1)}, u32[]{:S(2)}, u32[]{:S(2)}) async-start(bf16[8,2,1024]{2,1,0:T(2,128)(2,1)} %reshape.191), calls=%async_computation.2 | async-start | bytes 65536 | tf_op jit(solution)/shard_map/all_to_all | solution.py:437
  309.3 3.8 %all-to-all-start.1 = ((bf16[8,64,256]{2,1,0:T(8,128)(2,1)}), bf16[8,64,256]{2,1,0:T(8,128)(2,1)S(1)}, u32[]{:S(2)}, u32[]{:S(2)}) async-start(bf16[8,64,256]{2,1,0:T(8,128)(2,1)} %fusion.28), calls=%async_computation.1 | async-start | bytes 524288 | tf_op jit(solution)/shard_map/all_to_all | solution.py:437
  314.5 5.5 %all-to-all-done.1 = bf16[8,64,256]{2,1,0:T(8,128)(2,1)S(1)} async-done(((bf16[8,64,256]{2,1,0:T(8,128)(2,1)}), bf16[8,64,256]{2,1,0:T(8,128)(2,1)S(1)}, u32[]{:S(2)}, u32[]{:S(2)}) %all-to-all-start.1) | async-done | bytes 262176 | tf_op jit(solution)/shard_map/all_to_all | solution.py:437
  324.4 3.8 %fusion.18 = f32[256,2048]{1,0:T(8,128)S(1)} fusion(bf16[2048,1024]{1,0:T(8,128)(2,1)} %collective-permute-done.48, bf16[256,256]{1,0:T(8,128)(2,1)} %collective-permute-done.47, bf16[256,256]{1,0:T(8,128)(2,1)} %collective-permute-done.46, bf16[256,256]{1,0:T(8,128)(2,1)} %collective-permute-done.45, bf16[256,256]{1,0:T(8,128)(2,1)} %collective-permute-done.44), kind=kOutput, calls=%fused_computation.29 | convolution fusion | flops 1075838976 | bytes 6815744 | tf_op jit(solution)/shard_map/dot_general | solution.py:23
  (351 shorter events, 157.8 us)
Async XLA Ops:
  3.8 33.0 %collective-permute-start.14 = (bf16[512,384]{1,0:T(8,128)(2,1)}, bf16[512,384]{1,0:T(8,128)(2,1)}, u32[]{:S(2)}, u32[]{:S(2)}) collective-permute-start(bf16[512,384]{1,0:T(8,128)(2,1)} %pad_maximum_fusion.3), channel_id=1, source_target_pairs={{0,1},{1,2},{2,3},{4,5},{5,6},{6,7},{8,9},{9,10},{10,11},{12,13},{... | collective-permute-start | bytes 1179656 | tf_op jit(solution)/shard_map/ppermute | solution.py:225
  32.5 31.8 %collective-permute-start.17 = (bf16[512,384]{1,0:T(8,128)(2,1)}, bf16[512,384]{1,0:T(8,128)(2,1)}, u32[]{:S(2)}, u32[]{:S(2)}) collective-permute-start(bf16[512,384]{1,0:T(8,128)(2,1)} %pad_maximum_fusion.3), channel_id=1, source_target_pairs={{1,0},{2,1},{3,2},{5,4},{6,5},{7,6},{9,8},{10,9},{11,10},{13,12},{... | collective-permute-start | bytes 1179656 | tf_op jit(solution)/shard_map/ppermute | solution.py:226
  33.8 34.7 %collective-permute-start.2 = (bf16[128,2048]{1,0:T(8,128)(2,1)S(1)}, bf16[128,2048]{1,0:T(8,128)(2,1)S(1)}, u32[]{:S(2)}, u32[]{:S(2)}) collective-permute-start(bf16[128,2048]{1,0:T(8,128)(2,1)S(1)} %get-tuple-element.64.refs_0_), channel_id=1, source_target_pairs={{0,8},{4,12},{8,0},{12,4},{16,24},{20,28},{24,16},{28,20},{1,9},{5... | collective-permute-start | bytes 1572872 | tf_op jit(solution)/shard_map/ppermute | solution.py:202
  36.9 28.8 %collective-permute-start.15 = (bf16[512,384]{1,0:T(8,128)(2,1)}, bf16[512,384]{1,0:T(8,128)(2,1)}, u32[]{:S(2)}, u32[]{:S(2)}) collective-permute-start(bf16[512,384]{1,0:T(8,128)(2,1)} %collective-permute-done.14), channel_id=1, source_target_pairs={{1,2},{2,3},{5,6},{6,7},{9,10},{10,11},{13,14},{14,15},{17,18},{18... | collective-permute-start | bytes 1179656 | tf_op jit(solution)/shard_map/ppermute | solution.py:225
  41.1 33.3 %collective-permute-start.7 = (bf16[128,2048]{1,0:T(8,128)(2,1)S(1)}, bf16[128,2048]{1,0:T(8,128)(2,1)}, u32[]{:S(2)}, u32[]{:S(2)}) collective-permute-start(bf16[128,2048]{1,0:T(8,128)(2,1)S(1)} %get-tuple-element.63.refs_1_), channel_id=1, source_target_pairs={{0,16},{4,20},{8,24},{12,28},{16,0},{20,4},{24,8},{28,12},{1,17},{... | collective-permute-start | bytes 1572872 | tf_op jit(solution)/shard_map/ppermute | solution.py:202
  74.4 39.9 %collective-permute-start.38 = (bf16[512,768]{1,0:T(8,128)(2,1)S(1)}, bf16[512,768]{1,0:T(8,128)(2,1)S(1)}, u32[]{:S(2)}, u32[]{:S(2)}) collective-permute-start(bf16[512,768]{1,0:T(8,128)(2,1)S(1)} %copy-done.23), channel_id=1, source_target_pairs={{0,1},{1,2},{2,3},{4,5},{5,6},{6,7},{8,9},{9,10},{10,11},{12,13},{... | collective-permute-start | bytes 2359304 | tf_op jit(solution)/shard_map/ppermute | solution.py:225
  79.3 35.1 %collective-permute-start.41 = (bf16[512,768]{1,0:T(8,128)(2,1)S(1)}, bf16[512,768]{1,0:T(8,128)(2,1)}, u32[]{:S(2)}, u32[]{:S(2)}) collective-permute-start(bf16[512,768]{1,0:T(8,128)(2,1)S(1)} %copy-done.23), channel_id=1, source_target_pairs={{1,0},{2,1},{3,2},{5,4},{6,5},{7,6},{9,8},{10,9},{11,10},{13,12},{... | collective-permute-start | bytes 2359304 | tf_op jit(solution)/shard_map/ppermute | solution.py:226
  80.6 29.2 %collective-permute-start.19 = (bf16[512,384]{1,0:T(8,128)(2,1)S(1)}, bf16[512,384]{1,0:T(8,128)(2,1)S(1)}, u32[]{:S(2)}, u32[]{:S(2)}) collective-permute-start(bf16[512,384]{1,0:T(8,128)(2,1)S(1)} %collective-permute-done.18), channel_id=1, source_target_pairs={{1,0},{5,4},{9,8},{13,12},{17,16},{21,20},{25,24},{29,28}} | collective-permute-start | bytes 1179656 | tf_op jit(solution)/shard_map/ppermute | solution.py:226
  83.1 29.6 %collective-permute-start = (bf16[128,2048]{1,0:T(8,128)(2,1)S(1)}, bf16[128,2048]{1,0:T(8,128)(2,1)S(1)}, u32[]{:S(2)}, u32[]{:S(2)}) collective-permute-start(bf16[128,2048]{1,0:T(8,128)(2,1)S(1)} %get-tuple-element.64.refs_0_), channel_id=1, source_target_pairs={{0,4},{4,0},{8,12},{12,8},{16,20},{20,16},{24,28},{28,24},{1,5},{5... | collective-permute-start | bytes 1572872 | tf_op jit(solution)/shard_map/ppermute | solution.py:202
  83.3 29.4 %collective-permute-start.1 = (bf16[128,2048]{1,0:T(8,128)(2,1)S(1)}, bf16[128,2048]{1,0:T(8,128)(2,1)S(1)}, u32[]{:S(2)}, u32[]{:S(2)}) collective-permute-start(bf16[128,2048]{1,0:T(8,128)(2,1)S(1)} %get-tuple-element.63.refs_1_), channel_id=1, source_target_pairs={{0,4},{4,0},{8,12},{12,8},{16,20},{20,16},{24,28},{28,24},{1,5},{5... | collective-permute-start | bytes 1572872 | tf_op jit(solution)/shard_map/ppermute | solution.py:202
  130.5 65.1 %collective-permute-start.42 = (bf16[512,768]{1,0:T(8,128)(2,1)}, bf16[512,768]{1,0:T(8,128)(2,1)}, u32[]{:S(2)}, u32[]{:S(2)}) collective-permute-start(bf16[512,768]{1,0:T(8,128)(2,1)} %collective-permute-done.41), channel_id=1, source_target_pairs={{1,0},{2,1},{5,4},{6,5},{9,8},{10,9},{13,12},{14,13},{17,16},{18,1... | collective-permute-start | bytes 2359304 | tf_op jit(solution)/shard_map/ppermute | solution.py:226
  131.8 91.2 %collective-permute-start.40 = (bf16[512,768]{1,0:T(8,128)(2,1)}, bf16[512,768]{1,0:T(8,128)(2,1)}, u32[]{:S(2)}, u32[]{:S(2)}) collective-permute-start(bf16[512,768]{1,0:T(8,128)(2,1)} %collective-permute-done.39), channel_id=1, source_target_pairs={{2,3},{6,7},{10,11},{14,15},{18,19},{22,23},{26,27},{30,31}} | collective-permute-start | bytes 2359304 | tf_op jit(solution)/shard_map/ppermute | solution.py:225
  200.9 19.2 %collective-permute-start.54 = (bf16[256,256]{1,0:T(8,128)(2,1)S(1)}, bf16[256,256]{1,0:T(8,128)(2,1)S(1)}, u32[]{:S(2)}, u32[]{:S(2)}) collective-permute-start(bf16[256,256]{1,0:T(8,128)(2,1)S(1)} %get-tuple-element.44), channel_id=1, source_target_pairs={{0,24},{4,28},{8,16},{12,20},{16,8},{20,12},{24,0},{28,4},{1,25},{... | collective-permute-start | bytes 393224 | tf_op jit(solution)/shard_map/ppermute | solution.py:202
  204.2 18.5 %collective-permute-start.55 = (bf16[256,256]{1,0:T(8,128)(2,1)S(1)}, bf16[256,256]{1,0:T(8,128)(2,1)S(1)}, u32[]{:S(2)}, u32[]{:S(2)}) collective-permute-start(bf16[256,256]{1,0:T(8,128)(2,1)S(1)} %get-tuple-element.43), channel_id=1, source_target_pairs={{0,28},{4,24},{8,20},{12,16},{16,12},{20,8},{24,4},{28,0},{1,29},{... | collective-permute-start | bytes 393224 | tf_op jit(solution)/shard_map/ppermute | solution.py:202
  205.2 34.5 %collective-permute-start.43 = (bf16[512,768]{1,0:T(8,128)(2,1)}, bf16[512,768]{1,0:T(8,128)(2,1)S(1)}, u32[]{:S(2)}, u32[]{:S(2)}) collective-permute-start(bf16[512,768]{1,0:T(8,128)(2,1)} %collective-permute-done.42), channel_id=1, source_target_pairs={{1,0},{5,4},{9,8},{13,12},{17,16},{21,20},{25,24},{29,28}} | collective-permute-start | bytes 2359304 | tf_op jit(solution)/shard_map/ppermute | solution.py:226
  210.6 92.8 %collective-permute-start.56 = (bf16[8,64,256]{2,1,0:T(8,128)(2,1)}, bf16[8,64,256]{2,1,0:T(8,128)(2,1)}, u32[]{:S(2)}, u32[]{:S(2)}) collective-permute-start(bf16[8,64,256]{2,1,0:T(8,128)(2,1)} %get-tuple-element.31), channel_id=1, source_target_pairs={{0,1},{1,0},{2,3},{3,2},{4,5},{5,4},{6,7},{7,6},{8,9},{9,8},{10,11... | collective-permute-start | bytes 786440 | tf_op jit(solution)/shard_map/ppermute | solution.py:202
  220.1 85.0 %collective-permute-start.57 = (bf16[8,64,256]{2,1,0:T(8,128)(2,1)}, bf16[8,64,256]{2,1,0:T(8,128)(2,1)}, u32[]{:S(2)}, u32[]{:S(2)}) collective-permute-start(bf16[8,64,256]{2,1,0:T(8,128)(2,1)} %get-tuple-element.33), channel_id=1, source_target_pairs={{0,2},{1,3},{2,0},{3,1},{4,6},{5,7},{6,4},{7,5},{8,10},{9,11},{10,... | collective-permute-start | bytes 786440 | tf_op jit(solution)/shard_map/ppermute | solution.py:202
  222.7 20.3 %collective-permute-start.23 = (bf16[256,256]{1,0:T(8,128)(2,1)}, bf16[256,256]{1,0:T(8,128)(2,1)S(1)}, u32[]{:S(2)}, u32[]{:S(2)}) collective-permute-start(bf16[256,256]{1,0:T(8,128)(2,1)} %get-tuple-element.60), channel_id=1, source_target_pairs={{0,12},{4,8},{8,4},{12,0},{16,28},{20,24},{24,20},{28,16},{1,13},{... | collective-permute-start | bytes 393224 | tf_op jit(solution)/shard_map/ppermute | solution.py:202
  223.0 21.8 %collective-permute-start.24 = (bf16[256,256]{1,0:T(8,128)(2,1)S(1)}, bf16[256,256]{1,0:T(8,128)(2,1)S(1)}, u32[]{:S(2)}, u32[]{:S(2)}) collective-permute-start(bf16[256,256]{1,0:T(8,128)(2,1)S(1)} %copy-done.41), channel_id=1, source_target_pairs={{0,16},{4,20},{8,24},{12,28},{16,0},{20,4},{24,8},{28,12},{1,17},{... | collective-permute-start | bytes 393224 | tf_op jit(solution)/shard_map/ppermute | solution.py:202
  243.0 81.4 %collective-permute-start.48 = (bf16[2048,1024]{1,0:T(8,128)(2,1)}, bf16[2048,1024]{1,0:T(8,128)(2,1)}, u32[]{:S(2)}, u32[]{:S(2)}) collective-permute-start(bf16[2048,1024]{1,0:T(8,128)(2,1)} %pad_maximum_fusion), channel_id=1, source_target_pairs={{0,4},{4,0},{8,12},{12,8},{16,20},{20,16},{24,28},{28,24},{1,5},{5... | collective-permute-start | bytes 12582920 | tf_op jit(solution)/shard_map/ppermute | solution.py:202
  284.3 22.2 %collective-permute-start.58 = (bf16[8,64,256]{2,1,0:T(8,128)(2,1)S(1)}, bf16[8,64,256]{2,1,0:T(8,128)(2,1)S(1)}, u32[]{:S(2)}, u32[]{:S(2)}) collective-permute-start(bf16[8,64,256]{2,1,0:T(8,128)(2,1)S(1)} %copy-done.40), channel_id=1, source_target_pairs={{0,3},{1,2},{2,1},{3,0},{4,7},{5,6},{6,5},{7,4},{8,11},{9,10},{10,... | collective-permute-start | bytes 786440 | tf_op jit(solution)/shard_map/ppermute | solution.py:202
  299.3 21.7 %collective-permute-start.44 = (bf16[256,256]{1,0:T(8,128)(2,1)}, bf16[256,256]{1,0:T(8,128)(2,1)}, u32[]{:S(2)}, u32[]{:S(2)}) collective-permute-start(bf16[256,256]{1,0:T(8,128)(2,1)} %get-tuple-element.38), channel_id=1, source_target_pairs={{0,4},{4,0},{8,12},{12,8},{16,20},{20,16},{24,28},{28,24},{1,5},{5... | collective-permute-start | bytes 393224 | tf_op jit(solution)/shard_map/ppermute | solution.py:202
  303.4 18.1 %collective-permute-start.45 = (bf16[256,256]{1,0:T(8,128)(2,1)}, bf16[256,256]{1,0:T(8,128)(2,1)}, u32[]{:S(2)}, u32[]{:S(2)}) collective-permute-start(bf16[256,256]{1,0:T(8,128)(2,1)} %get-tuple-element.37), channel_id=1, source_target_pairs={{0,12},{4,8},{8,4},{12,0},{16,28},{20,24},{24,20},{28,16},{1,13},{... | collective-permute-start | bytes 393224 | tf_op jit(solution)/shard_map/ppermute | solution.py:202
  306.5 17.9 %collective-permute-start.47 = (bf16[256,256]{1,0:T(8,128)(2,1)}, bf16[256,256]{1,0:T(8,128)(2,1)}, u32[]{:S(2)}, u32[]{:S(2)}) collective-permute-start(bf16[256,256]{1,0:T(8,128)(2,1)} %get-tuple-element.35), channel_id=1, source_target_pairs={{0,28},{4,24},{8,20},{12,16},{16,12},{20,8},{24,4},{28,0},{1,29},{... | collective-permute-start | bytes 393224 | tf_op jit(solution)/shard_map/ppermute | solution.py:202
  (99 other events, 1318.4 us)

commit v3 on v1

v3 whole, which is shorter than its diff:
```python
import functools

import jax
import jax.numpy as jnp
from jax import lax
from jax.experimental import pallas as pl
from jax.experimental.pallas import tpu as pltpu
from jax.sharding import PartitionSpec as P

CHUNK = 128
EPSILON = 1e-05
VMEM_LIMIT = 60 * 1024 * 1024

f32 = jnp.float32
bf16 = jnp.bfloat16


def dot_nn(a, b):
    return lax.dot_general(a, b, (((1,), (0,)), ((), ())), preferred_element_type=f32)


def dot_nt(a, b):
    return lax.dot_general(a, b, (((1,), (1,)), ((), ())), preferred_element_type=f32)


def dot_tn(a, b):
    return lax.dot_general(a, b, (((0,), (0,)), ((), ())), preferred_element_type=f32)


def by_head(rows, heads, head_size):
    if heads == 1:
        return rows
    lane = lax.broadcasted_iota(jnp.int32, rows.shape, 1)
    parts = []
    for h in range(heads):
        inside = (lane >= h * head_size) & (lane < (h + 1) * head_size)
        parts.append(jnp.where(inside, rows, jnp.zeros_like(rows)))
    return jnp.concatenate(parts, axis=0)


def decayed(affinity, decays, heads):
    tiled = jnp.concatenate([affinity] * heads, axis=1) if heads > 1 else affinity
    return (tiled * decays.astype(f32)).astype(bf16)


def mixer_kernel(
    sources, arrays, slots, group, blocks, heads, head_size, places_ref, *refs
):
    array_refs, refs = refs[:arrays], refs[arrays:]
    w_hbm, refs = refs[:blocks], refs[blocks:]
    table_hbm, g_hbm, refs = refs[:7], refs[7], refs[8:]
    z_hbm, grads_hbm, refs = refs[0], refs[1], refs[2:]
    te_ref, fs_ref, en_ref, lv_ref, dt_ref, m_ref, mt_ref, refs = *refs[:7], refs[7:]
    g_ref, z_ref, grads_ref, held, w_ref, x_ref, b_ref, c_ref, refs = *refs[:8], refs[8:]
    rs_ref, sf_ref, rn_ref, dy_ref, ge_ref, mean_ref, carry, sems, loads, stores = refs
    pieces = len(sources)
    rows_each = held.shape[1]
    width = x_ref.shape[1]
    state_size = b_ref.shape[1]
    extent = w_ref.shape[0] // blocks
    chunks = dt_ref.shape[0]
    place, row_place = places_ref[0], places_ref[1]

    def fetch(i):
        array, start = sources[i]
        source = array_refs[array].at[pl.ds(start, rows_each)]
        return pltpu.make_async_copy(source, held.at[i % slots], sems.at[i % slots])

    w_loads = []
    for k in range(blocks):
        offset = pl.multiple_of(lax.bitwise_xor(row_place, k) * extent, extent)
        target = w_ref.at[pl.ds(offset, extent)]
        w_loads.append(pltpu.make_async_copy(w_hbm[k], target, loads.at[8 + k]))
    table_refs = (te_ref, fs_ref, en_ref, lv_ref, dt_ref, m_ref, mt_ref)
    table_loads = [
        pltpu.make_async_copy(source, target, loads.at[n])
        for n, (source, target) in enumerate(zip(table_hbm, table_refs))
    ]
    g_load = pltpu.make_async_copy(g_hbm, g_ref, loads.at[7])
    for load in w_loads:
        load.start()
    for i in range(slots):
        fetch(i).start()
    for load in table_loads:
        load.start()
    g_load.start()

    head_row = lax.broadcasted_iota(jnp.int32, (width, width), 0)
    head_col = lax.broadcasted_iota(jnp.int32, (width, width), 1)
    same = jnp.zeros((width, width), jnp.bool_)
    for h in range(heads):
        low, high = h * head_size, (h + 1) * head_size
        same |= (head_row >= low) & (head_row < high) & (head_col >= low) & (head_col < high)
    mean_ref[...] = jnp.where(same, 1.0 / head_size, 0.0).astype(bf16)

    for load in w_loads:
        load.wait()
    for first in range(0, pieces, group):
        for i in range(first, first + group):
            fetch(i).wait()
        slot = first % slots
        block = held[slot : slot + group].reshape(group * rows_each, held.shape[2])
        result = dot_nn(block, w_ref[...]).astype(bf16)
        for i in range(first, first + group):
            if i + slots < pieces:
                fetch(i + slots).start()
            offset = (2 * lax.bitwise_xor(place, i // 2) + i % 2) * rows_each
            target = pl.ds(pl.multiple_of(offset, rows_each), rows_each)
            part = result[(i - first) * rows_each : (i - first + 1) * rows_each]
            x_ref[target, :] = part[:, :width]
            b_ref[target, :] = part[:, width : width + state_size]
            c_ref[target, :] = part[:, width + state_size :]
    for load in table_loads:
        load.wait()

    def spans(k):
        rows = pl.ds(pl.multiple_of(k * CHUNK, CHUNK), CHUNK)
        return rows, pl.ds(pl.multiple_of(k * state_size, state_size), state_size)

    carry[...] = jnp.zeros_like(carry)

    def reverse_states(i, _):
        k = chunks - 1 - i
        rows, state = spans(k)
        rn_ref[state, :] = carry[...].astype(bf16)
        term = dot_tn(b_ref[rows, :], x_ref[rows, :] * fs_ref[rows, :])
        carry[...] = dt_ref[k] * carry[...] + term
        return 0

    lax.fori_loop(0, chunks, reverse_states, 0, unroll=2)
    carry[...] = jnp.zeros_like(carry)

    def outputs(k, _):
        rows, state = spans(k)
        x, b, c = x_ref[rows, :], b_ref[rows, :], c_ref[rows, :]
        state_in = carry[...].astype(bf16)
        sf_ref[state, :] = state_in
        weights = decayed(dot_nt(c, b), m_ref[rows, :], heads)
        y = dot_nn(weights, by_head(x, heads, head_size))
        y = y + en_ref[rows, :].astype(f32) * dot_nn(c, state_in)
        y = y + lv_ref[rows, :].astype(f32) * dot_nn(c, rn_ref[state, :])
        mean_square = dot_nn((y * y).astype(bf16), mean_ref[...])
        inverse = lax.rsqrt(mean_square + EPSILON)
        z_ref[rows, :] = (y * inverse).astype(bf16)
        rs_ref[rows, :] = inverse.astype(bf16)
        carry[...] = dt_ref[k] * carry[...] + dot_tn(b, x * te_ref[rows, :])
        return 0

    lax.fori_loop(0, chunks, outputs, 0, unroll=2)
    z_store = pltpu.make_async_copy(z_ref, z_hbm, stores.at[0])
    z_store.start()
    g_load.wait()
    carry[...] = jnp.zeros_like(carry)

    def end_adjoints(i, _):
        k = chunks - 1 - i
        rows, state = spans(k)
        g, z = g_ref[rows, :].astype(f32), z_ref[rows, :].astype(f32)
        mean_gz = dot_nn((g * z).astype(bf16), mean_ref[...])
        dy = ((g - z * mean_gz) * rs_ref[rows, :].astype(f32)).astype(bf16)
        dy_ref[rows, :] = dy
        ge_ref[state, :] = carry[...].astype(bf16)
        carry[...] = dt_ref[k] * carry[...] + dot_tn(c_ref[rows, :], dy * en_ref[rows, :])
        return 0

    lax.fori_loop(0, chunks, end_adjoints, 0, unroll=2)
    carry[...] = jnp.zeros_like(carry)

    def gradients(k, _):
        rows, state = spans(k)
        x, b, c, dy = x_ref[rows, :], b_ref[rows, :], c_ref[rows, :], dy_ref[rows, :]
        te, fs, en, lv = te_ref[rows, :], fs_ref[rows, :], en_ref[rows, :], lv_ref[rows, :]
        ge, gs = ge_ref[state, :], carry[...].astype(bf16)
        grad_weights = dot_nt(dy, by_head(x, heads, head_size)) * m_ref[rows, :].astype(f32)
        da = grad_weights[:, :CHUNK]
        for h in range(1, heads):
            da = da + grad_weights[:, h * CHUNK : (h + 1) * CHUNK]
        da = da.astype(bf16)
        turned = decayed(dot_nt(b, c), mt_ref[rows, :], heads)
        dx = dot_nn(turned, by_head(dy, heads, head_size))
        dx = dx + te.astype(f32) * dot_nn(b, ge)
        dx = dx + fs.astype(f32) * dot_nn(b, gs)
        grads_ref[rows, :width] = dx.astype(bf16)
        dy_lv = dy * lv
        dc = dot_nn(da, b) + dot_nt(dy * en, sf_ref[state, :]) + dot_nt(dy_lv, rn_ref[state, :])
        db = dot_tn(da, c) + dot_nt(x * te, ge) + dot_nt(x * fs, gs)
        grads_ref[rows, width : width + state_size] = db.astype(bf16)
        grads_ref[rows, width + state_size :] = dc.astype(bf16)
        carry[...] = dt_ref[k] * carry[...] + dot_tn(c, dy_lv)
        return 0

    lax.fori_loop(0, chunks, gradients, 0, unroll=2)
    grads_store = pltpu.make_async_copy(grads_ref, grads_hbm, stores.at[1])
    grads_store.start()
    z_store.wait()
    grads_store.wait()


def tokens_kernel(places_ref, grads_ref, shared_ref, w_shared_ref, *refs):
    columns, (out_ref, lhs_ref, w_ref) = refs[:-3], refs[-3:]
    count = grads_ref.shape[0]
    extent, width = columns[0].shape[1:]
    k = pl.program_id(0)

    @pl.when(k == 0)
    def _():
        for r in range(count):
            source = grads_ref[lax.bitwise_xor(places_ref[0], r)]
            lhs_ref[:, r * width : (r + 1) * width] = source[:, :width]
        lhs_ref[:, count * width :] = shared_ref[...]

    for r in range(count):
        w_ref[:, r * width : (r + 1) * width] = columns[r][0]
    w_ref[:, count * width :] = w_shared_ref[0]
    offset = pl.multiple_of(lax.bitwise_xor(places_ref[1], k) * extent, extent)
    out_ref[0, :, pl.ds(offset, extent)] = dot_nt(lhs_ref[...], w_ref[...]).astype(bf16)


def sum_kernel(parts_ref, sum_ref, turned_ref):
    start = parts_ref.shape[2] - sum_ref.shape[1]
    total = parts_ref[0, :, start:].astype(f32)
    for n in range(1, parts_ref.shape[0]):
        total = total + parts_ref[n, :, start:].astype(f32)
    sum_ref[...] = total.astype(bf16)
    turned_ref[...] = total.T.astype(bf16).reshape(turned_ref.shape)


def add_kernel(*refs):
    out_ref, refs = refs[-1], refs[:-1]
    head_refs, shared_refs = refs[: len(refs) // 2], refs[len(refs) // 2 :]
    rows = head_refs[0].shape[1]
    total = head_refs[0][...].astype(f32)
    for ref in head_refs[1:]:
        total = total + ref[...].astype(f32)
    out_ref[:, :rows, :] = total.astype(bf16)
    total = shared_refs[0][...].astype(f32)
    for ref in shared_refs[1:]:
        total = total + ref[...].astype(f32)
    total = total.astype(bf16)
    extra = out_ref.shape[1] - rows
    part = total.shape[2]
    out_ref[:, rows:, :] = jnp.zeros((out_ref.shape[0], extra, out_ref.shape[2]), bf16)
    for q in range(rows // extra):
        out_ref[:, rows:, q * part : (q + 1) * part] = total[:, q * extra : (q + 1) * extra]


def spread_kernel(blocks_ref, out_ref):
    width = blocks_ref.shape[2]
    for n in range(blocks_ref.shape[0]):
        out_ref[0, :, n * width : (n + 1) * width] = blocks_ref[n]


def weight_kernel(sources, arrays, slots, group, parts, places_ref, *refs):
    array_refs, grad_ref = refs[:arrays], refs[arrays]
    out_refs = refs[arrays + 1 : arrays + 1 + parts]
    held, total, result, sems = refs[arrays + 1 + parts :]
    pieces = len(sources)
    rows = held.shape[1]
    hidden = held.shape[2]

    def fetch(i):
        array, start = sources[i]
        source = array_refs[array].at[pl.ds(start, rows)]
        return pltpu.make_async_copy(source, held.at[i % slots], sems.at[i % slots])

    for i in range(slots):
        fetch(i).start()
    for first in range(0, pieces, group):
        turned = []
        for i in range(first, first + group):
            offset = (2 * lax.bitwise_xor(places_ref[0], i // 2) + i % 2) * rows
            if len(grad_ref.shape) == 3:
                block = grad_ref[lax.bitwise_xor(places_ref[0], i // 2)]
                turned.append(block[:, i % 2 * rows : (i % 2 + 1) * rows])
            else:
                block = grad_ref[pl.ds(pl.multiple_of(offset, rows), rows), :]
                turned.append(block[:, : total.shape[0]].T)
        for i in range(first, first + group):
            fetch(i).wait()
        slot = first % slots
        block = held[slot : slot + group].reshape(group * rows, hidden)
        term = dot_nn(jnp.concatenate(turned, axis=1), block)
        if first > 0:
            term = term + total[...]
        if first + group < pieces:
            total[...] = term
        else:
            result[...] = term.T.astype(bf16)
        for i in range(first, first + group):
            if i + slots < pieces:
                fetch(i + slots).start()
    each = out_refs[0].shape[1]
    for k in range(parts):
        mine = lax.bitwise_xor(places_ref[1], k) * each
        for j in range(out_refs[0].shape[0]):
            source = pl.ds(pl.multiple_of(j * parts * each + mine, each), each)
            out_refs[k][j] = result[source, :]


def finish_kernel(packed_ref, out_ref):
    count, _, width = packed_ref.shape
    rows = out_ref.shape[0]
    extra = packed_ref.shape[1] - rows
    part = (out_ref.shape[1] - count * width) // count
    for n in range(count):
        out_ref[:, n * width : (n + 1) * width] = packed_ref[n, :rows].astype(f32)
        start = count * width + n * part
        for q in range(rows // extra):
            block = packed_ref[n, rows:, q * part : (q + 1) * part]
            out_ref[q * extra : (q + 1) * extra, start : start + part] = block.astype(f32)


def resident(array):
    return pl.BlockSpec(array.shape, lambda k: (0,) * len(array.shape))


def after(value, *earlier):
    return lax.optimization_barrier((value,) + earlier)[0]


def permute_xor(a, axis, mask):
    count = lax.axis_size(axis)
    return lax.ppermute(a, axis, [(i, i ^ mask) for i in range(count)])


def gather_rows(rows, axis, beside, work):
    count = lax.axis_size(axis)
    bits = count.bit_length() - 1
    half = rows.shape[0] // 2
    if bits == 3:
        first = [permute_xor(rows, axis, mask) for mask in (2, 4)]
        *first, beside = lax.optimization_barrier((*first, beside))
        across = {2: first[0], 4: first[1]}
        done = work(beside)
        corner = [
            permute_xor(across[2][:half], axis, 4),
            permute_xor(across[4][half:], axis, 2),
        ]
        own = {0: [rows], 2: [across[2]], 4: [across[4]], 6: corner}
        held = {}
        for r, parts in own.items():
            held[r] = parts
            held[r ^ 1] = [permute_xor(after(a, done[0]), axis, 1) for a in parts]
    else:
        done = work(beside)
        upper = list(range(1, bits))
        orders = (upper + [0], upper[1:] + upper[:1] + [0])
        both = ({0: rows[:half]}, {0: rows[half:]})
        for step in range(bits):
            for part in range(2):
                mask = 1 << orders[part][step]
                for r in list(both[part]):
                    both[part][r ^ mask] = permute_xor(both[part][r], axis, mask)
        held = {r: [both[0][r], both[1][r]] for r in range(count)}
    arrays, sources = [], []
    for r in range(count):
        for part in range(2):
            whole_block = len(held[r]) == 1
            if part == 0 or not whole_block:
                arrays.append(held[r][part])
            sources.append((len(arrays) - 1, half * part if whole_block else 0))
    return arrays, tuple(sources), done


def exchange_xor(pieces, axis):
    return [pieces[0]] + [permute_xor(p, axis, r) for r, p in enumerate(pieces) if r > 0]


def tables_kernel(log_ref, *refs):
    out_refs, table_refs, sems = refs[:7], refs[7:14], refs[14]
    te_ref, fs_ref, en_ref, lv_ref, dt_ref, m_ref, mt_ref = table_refs
    heads = log_ref.shape[0]
    chunks = dt_ref.shape[0]
    head_size = te_ref.shape[1] // heads
    row = lax.broadcasted_iota(jnp.int32, (CHUNK, CHUNK), 0)
    col = lax.broadcasted_iota(jnp.int32, (CHUNK, CHUNK), 1)
    logs = jnp.concatenate(
        [log_ref[:, k * CHUNK : (k + 1) * CHUNK] for k in range(chunks)], axis=0
    )
    cumulative = lax.dot_general(
        logs, (row <= col).astype(f32), (((1,), (0,)), ((), ())),
        precision=lax.Precision.HIGHEST, preferred_element_type=f32,
    )
    exclusive = cumulative - logs
    cum_t, exc_t = cumulative.T, exclusive.T
    total = cum_t[CHUNK - 1 : CHUNK, :]
    spreads = (
        (te_ref, jnp.exp(total - cum_t)),
        (fs_ref, jnp.exp(exc_t)),
        (en_ref, jnp.exp(cum_t)),
        (lv_ref, jnp.exp(total - exc_t)),
    )
    chunk_decay = jnp.exp(total)
    diagonal = (row == col).astype(f32)
    for k in range(chunks):
        rows = slice(k * CHUNK, (k + 1) * CHUNK)
        picked = range(k * heads, (k + 1) * heads)
        for ref, source in spreads:
            ref[rows, :] = jnp.concatenate(
                [jnp.broadcast_to(source[:, n : n + 1], (CHUNK, head_size)) for n in picked], axis=1
            ).astype(bf16)
        dt_ref[k] = jnp.concatenate(
            [jnp.broadcast_to(chunk_decay[:, n : n + 1], (1, head_size)) for n in picked], axis=1
        )
        for h, n in enumerate(picked):
            cum_col, exc_col = cum_t[:, n : n + 1], exc_t[:, n : n + 1]
            cum_row, exc_row = cumulative[n : n + 1, :], exclusive[n : n + 1, :]
            below, above = cum_col - cum_row, exc_row - exc_col
            exponent = jnp.where(row > col, below, jnp.where(row < col, above, 0.0))
            turned = jnp.where(row < col, -below, jnp.where(row > col, -above, 0.0))
            columns = slice(h * CHUNK, (h + 1) * CHUNK)
            m_ref[rows, columns] = (jnp.exp(exponent) + diagonal).astype(bf16)
            mt_ref[rows, columns] = (jnp.exp(turned) + diagonal).astype(bf16)
    stores = [
        pltpu.make_async_copy(source, target, sems.at[n])
        for n, (source, target) in enumerate(zip(table_refs, out_refs))
    ]
    for store in stores:
        store.start()
    for store in stores:
        store.wait()


def on_device(tokens, w_in, log_decay, grad_out):
    local_tokens = tokens[0]
    upstream = grad_out[0]
    token_count, hidden_width = local_tokens.shape
    head_count = log_decay.shape[1]
    inner_width = upstream.shape[1]
    head_size = inner_width // head_count
    state_size = (w_in.shape[1] - inner_width) // 2
    seq_count = lax.axis_size("seq")
    fsdp_count = lax.axis_size("fsdp")
    place = lax.axis_index("seq")
    row_place = lax.axis_index("fsdp")
    heads = head_count // seq_count
    width = heads * head_size
    length = token_count * seq_count
    shared = 2 * state_size
    chunks = length // CHUNK
    extent = hidden_width // fsdp_count
    shape = jax.ShapeDtypeStruct
    params = pltpu.CompilerParams(vmem_limit_bytes=VMEM_LIMIT)
    scalar = [pl.BlockSpec(memory_space=pltpu.SMEM)]
    places = jnp.stack([place, row_place]).astype(jnp.int32)

    def cost(flops, moved):
        return pl.CostEstimate(flops=flops, bytes_accessed=moved, transcendentals=0)

    def from_all(block):
        return exchange_xor([block] * fsdp_count, "fsdp")

    def columns(r):
        return lax.dynamic_slice_in_dim(w_in, lax.bitwise_xor(place, r) * width, width, 1)

    log_rates = lax.all_to_all(log_decay[0], "seq", 0, 1, tiled=True)
    w_own = from_all(jnp.concatenate([columns(0), w_in[:, inner_width:]], axis=1))
    table_shapes = (
        [shape((length, width), bf16)] * 4
        + [shape((chunks, 1, width), f32)]
        + [shape((length, heads * CHUNK), bf16)] * 2
    )
    in_hbm = [pl.BlockSpec(memory_space=pltpu.HBM)]
    scratch = lambda *buffers: [pltpu.VMEM(a.shape, a.dtype) for a in buffers]
    make_tables = pl.pallas_call(
        tables_kernel,
        grid=(1,),
        out_shape=table_shapes,
        in_specs=[resident(log_rates)],
        out_specs=in_hbm * 7,
        scratch_shapes=scratch(*table_shapes) + [pltpu.SemaphoreType.DMA((7,))],
        compiler_params=params,
        cost_estimate=cost(0, 8 * length * width),
    )
    arrays, sources, tables = gather_rows(local_tokens, "seq", log_rates, make_tables)
    g = lax.all_to_all(after(upstream, tables[0]), "seq", 1, 0, tiled=True)

    w_stack = jnp.stack(w_own)
    w_shared = w_stack[:, :, width:]
    w_sides = {0: w_stack[:, :, :width]}
    for r in range(2, seq_count, 2):
        if r & (r - 1):
            w_sides[r] = from_all(after(columns(r), *w_own))
        else:
            w_sides[r] = permute_xor(after(w_sides[0], *arrays[-2:]), "seq", r)


    count = len(sources)
    slots = min(count, 16)
    group = min(slots, 4)
    held = shape((slots, token_count // 2, hidden_width), bf16)
    by_position = shape((length, width), bf16)
    by_state = shape((chunks * state_size, width), bf16)
    state_rows = shape((length, state_size), bf16)
    buffers = [
        *table_shapes, by_position, by_position, shape((length, width + shared), bf16),
        held, shape((hidden_width, width + shared), bf16),
        by_position, state_rows, state_rows,
        by_position, by_state, by_state, by_position, by_state,
        shape((width, width), bf16), shape((state_size, width), f32),
    ]
    z, grads = pl.pallas_call(
        functools.partial(
            mixer_kernel, sources, len(arrays), slots, group, fsdp_count, heads, head_size
        ),
        out_shape=[by_position, shape((length, width + shared), bf16)],
        in_specs=scalar + in_hbm * (len(arrays) + fsdp_count + 8),
        out_specs=in_hbm * 2,
        scratch_shapes=scratch(*buffers)
        + [
            pltpu.SemaphoreType.DMA((slots,)),
            pltpu.SemaphoreType.DMA((8 + fsdp_count,)),
            pltpu.SemaphoreType.DMA((2,)),
        ],
        compiler_params=params,
        cost_estimate=cost(
            2 * length * hidden_width * (width + shared) + 120 * length * width * CHUNK,
            4 * length * hidden_width,
        ),
    )(places, *arrays, *w_own, *tables, g)

    rows_each = hidden_width // (seq_count * fsdp_count)

    def weight_columns(grad, columns):
        total = shape((columns, hidden_width), f32)
        result = shape((hidden_width, columns), bf16)
        parts = [shape((seq_count, rows_each, columns), bf16)] * fsdp_count
        parts = pl.pallas_call(
            functools.partial(weight_kernel, sources, len(arrays), slots, group, fsdp_count),
            out_shape=parts,
            grid=(1,),
            in_specs=scalar + in_hbm * len(arrays) + [resident(grad)],
            out_specs=[resident(a) for a in parts],
            scratch_shapes=scratch(held, total, result) + [pltpu.SemaphoreType.DMA((slots,))],
            compiler_params=params,
            cost_estimate=cost(2 * length * hidden_width * columns, 2 * length * hidden_width),
        )(places, *arrays, grad)
        return parts

    for r in range(0, seq_count, 2):
        if isinstance(w_sides[r], list):
            w_sides[r] = jnp.stack(w_sides[r])
        w_sides[r + 1] = permute_xor(after(w_sides[r], grads), "seq", 1)
    arrived = lax.all_to_all(
        grads.reshape(seq_count, token_count, width + shared), "seq", 0, 0
    )
    head_weights = weight_columns(grads, width)
    head_arrived = exchange_xor(head_weights, "fsdp")
    arrived, z, w_sides, _ = lax.optimization_barrier((arrived, z, w_sides, head_weights[0]))
    sums = [
        shape((token_count, shared), bf16),
        shape((seq_count, shared // seq_count, token_count), bf16),
    ]
    grad_shared, turned_shared = pl.pallas_call(
        sum_kernel,
        grid=(1,),
        out_shape=sums,
        in_specs=[resident(arrived)],
        out_specs=[resident(a) for a in sums],
        compiler_params=params,
    )(arrived)
    shared_columns = lax.all_to_all(turned_shared, "seq", 0, 0)
    mixed_blocks = lax.all_to_all(
        after(z, shared_columns).reshape(seq_count, token_count, width), "seq", 0, 0
    )
    shared_weights = weight_columns(shared_columns, shared // seq_count)
    shared_arrived = exchange_xor(shared_weights, "fsdp")

    def by_block(a):
        return pl.BlockSpec((1,) + a.shape[1:], lambda k: (k, 0, 0))

    w_blocks = [w_shared] + [w_sides[r] for r in range(seq_count)]
    grad_tokens_shape = shape((1, token_count, hidden_width), bf16)
    lhs = shape((token_count, inner_width + shared), bf16)
    w_block = shape((extent, inner_width + shared), bf16)
    grad_tokens = pl.pallas_call(
        tokens_kernel,
        grid=(fsdp_count,),
        out_shape=grad_tokens_shape,
        in_specs=scalar
        + [resident(arrived), resident(grad_shared)]
        + [by_block(a) for a in w_blocks],
        out_specs=resident(grad_tokens_shape),
        scratch_shapes=scratch(lhs, w_block),
        compiler_params=params,
        cost_estimate=cost(
            2 * token_count * hidden_width * (inner_width + shared),
            2 * hidden_width * (inner_width + shared),
        ),
    )(places, arrived, grad_shared, *w_blocks)

    mixer_out_shape = shape((1, token_count, inner_width), bf16)
    mixer_out = pl.pallas_call(
        spread_kernel,
        grid=(1,),
        out_shape=mixer_out_shape,
        in_specs=[resident(mixed_blocks)],
        out_specs=resident(mixer_out_shape),
        compiler_params=params,
    )(mixed_blocks)
    extra = 16
    packed = shape((seq_count, rows_each + extra, width), bf16)
    packed_sums = pl.pallas_call(
        add_kernel,
        grid=(1,),
        out_shape=packed,
        in_specs=[resident(a) for a in head_arrived + shared_arrived],
        out_specs=resident(packed),
        compiler_params=params,
    )(*head_arrived, *shared_arrived)
    owned = lax.all_to_all(packed_sums, "seq", 0, 0)
    finished = shape((rows_each, inner_width + shared), f32)
    grad_weights = pl.pallas_call(
        finish_kernel,
        grid=(1,),
        out_shape=finished,
        in_specs=[resident(owned)],
        out_specs=resident(finished),
        compiler_params=params,
    )(owned)
    return mixer_out, grad_tokens, grad_weights


def solution(mesh):
    return jax.shard_map(
        on_device,
        mesh=mesh,
        in_specs=(
            P("fsdp", "seq", None),
            P("fsdp", None),
            P("fsdp", None, "seq"),
            P("fsdp", "seq", None),
        ),
        out_specs=(P("fsdp", "seq", None), P("fsdp", "seq", None), P(("seq", "fsdp"), None)),
        check_vma=False,
    )
```

time: 343 us -> 223 us (0.65)
  waiting for transfers between devices: 172 us -> 71.5 us
  starting transfers between devices: 16.1 us -> 56.8 us
  Pallas kernels: 29.2 us -> 68.1 us
  local copies, waits for them, and re-layouts: 39.4 us -> 11.5 us
  blocking collectives: 37.1 us -> 9.51 us
  matrix products: 23.1 us -> 0 us
  between operations: 14 us -> 0.92 us
  other arithmetic: 11 us -> 3.53 us
    all_gather x3 -> x0, waiting for transfers between devices: 110 us -> none  [the longest x1 55 us: on_device(): all_tokens = lax.all_gather(local_tokens, 'seq', axis=0, tiled=True)]
    unnamed x5 -> x0, waiting for transfers between devices: 43.9 us -> none
    ppermute x0 -> x27, waiting for transfers between devices: none -> 43.4 us  [permute_xor(): return lax.ppermute(a, axis, [(i, i ^ mask) for i in range(count)])]
    pallas_call x2 -> x9, Pallas kernels: 29.2 us -> 68.1 us  [the longest x1 29.1 us: on_device(): pl.pallas_call(functools.partial(mixer_kernel, sources, len(arrays), slot...]
    ppermute x0 -> x27, starting transfers between devices: none -> 38.4 us  [permute_xor(): return lax.ppermute(a, axis, [(i, i ^ mask) for i in range(count)])]
    all_to_all x2 -> x1, blocking collectives: 37.1 us -> 9.51 us  [on_device(): shared_columns = lax.all_to_all(turned_shared, 'seq', 0, 0)]
    dot_general x4 -> x0, matrix products: 23.1 us -> none  [the longest x1 8.5 us: on_device(): jnp.dot(all_tokens, w_columns, preferred_element_type=f32).astype(bf16)]
    all_to_all x1, waiting for transfers between devices: 3.06 us -> 15.1 us  [on_device(): log_rates = lax.all_to_all(log_decay[0], 'seq', 0, 1, tiled=True)]
  transfers between devices with their start and end apart: 8 -> 32, of which waited for: 6 -> 7; matrix products, arithmetic and copies ran while one was open for 17% -> 5% of each run, Pallas kernels for 4% -> 29%
where the time goes in v3:
time: 223 us; the launch traced here: 222 us
  waiting for transfers between devices  71.5 us (32%)
  Pallas kernels  68.1 us (31%)
  starting transfers between devices  56.8 us (25%)
  local copies, waits for them, and re-layouts  11.5 us (5%)
  blocking collectives  9.51 us (4%)
  other arithmetic  3.53 us (2%)
    ppermute x27, waiting for transfers between devices, permute_xor(): return lax.ppermute(a, axis, [(i, i ^ mask) for i in range(count)])  43.4 us
    ppermute x27, starting transfers between devices, permute_xor(): return lax.ppermute(a, axis, [(i, i ^ mask) for i in range(count)])  38.4 us
    pallas_call x1, Pallas kernels, on_device(): pl.pallas_call(functools.partial(mixer_kernel, sources, len(arrays), slot...  29.1 us
    all_to_all x1, waiting for transfers between devices, on_device(): log_rates = lax.all_to_all(log_decay[0], 'seq', 0, 1, tiled=True)  15.1 us
    pallas_call x2, Pallas kernels, weight_columns(): pl.pallas_call(functools.partial(weight_kernel, sources, len(arrays), slo...  12.7 us
    all_to_all x1, blocking collectives, on_device(): shared_columns = lax.all_to_all(turned_shared, 'seq', 0, 0)  9.51 us
    pallas_call x1, Pallas kernels, gather_rows(): done = work(beside)  9.22 us
    pallas_call x1, Pallas kernels, on_device(): pl.pallas_call(tokens_kernel, grid=(fsdp_count,), out_shape=grad_tokens_s...  7.99 us
  transfers between devices with their start and end apart: 32, of which 7 were waited for; matrix products, arithmetic and copies ran while one was open for 5% of the time, Pallas kernels for 29%

profile of v3, /device:TPU:0, one launch (start us, length us, event | category | flops | bytes accessed | tf_op | source)
XLA Modules:
  0.0 221.8 jit_solution(3238869654713633273)
XLA Ops:
  0.6 3.0 %collective-permute-start = (bf16[256,2048]{1,0:T(8,128)(2,1)}, bf16[256,2048]{1,0:T(8,128)(2,1)S(1)}, u32[]{:S(2)}, u32[]{:S(2)}) collective-permute-start(bf16[256,2048]{1,0:T(8,128)(2,1)} %bitcast.26), channel_id=1, source_target_pairs={{0,8},{4,12},{8,0},{12,4},{16,24},{20,28},{24,16},{28,20},{1,9},{5... | collective-permute-start | bytes 3145736 | tf_op jit(solution)/shard_map/ppermute | solution.py:323
  6.5 3.3 %all-to-all-start = ((f32[8,4,256]{2,1,0:T(4,128)}), f32[8,4,256]{2,1,0:T(4,128)S(1)}, u32[]{:S(2)}, u32[]{:S(2)}) async-start(f32[8,4,256]{2,1,0:T(4,128)} %all_to_all.40), calls=%async_computation | async-start | bytes 65536 | tf_op jit(solution)/shard_map/all_to_all | solution.py:456
  13.7 15.1 %all-to-all-done = f32[8,4,256]{2,1,0:T(4,128)S(1)} async-done(((f32[8,4,256]{2,1,0:T(4,128)}), f32[8,4,256]{2,1,0:T(4,128)S(1)}, u32[]{:S(2)}, u32[]{:S(2)}) %all-to-all-start) | async-done | bytes 32800 | tf_op jit(solution)/shard_map/all_to_all | solution.py:456
  32.6 2.6 %collective-permute-start.10 = (bf16[512,512]{1,0:T(8,128)(2,1)}, bf16[512,512]{1,0:T(8,128)(2,1)}, u32[]{:S(2)}, u32[]{:S(2)}) collective-permute-start(bf16[512,512]{1,0:T(8,128)(2,1)} %get-tuple-element.99.refs_10_), channel_id=1, source_target_pairs={{0,2},{1,3},{2,0},{3,1},{4,6},{5,7},{6,4},{7,5},{8,10},{9,11},{10,... | collective-permute-start | bytes 1572872 | tf_op jit(solution)/shard_map/ppermute | solution.py:323
  36.6 9.2 %shard_map.67 = (bf16[2048,256]{1,0:T(8,128)(2,1)}, bf16[2048,256]{1,0:T(8,128)(2,1)}, bf16[2048,256]{1,0:T(8,128)(2,1)}, bf16[2048,256]{1,0:T(8,128)(2,1)}, f32...) custom-call(f32[4,2048]{1,0:T(4,128)} %bitcast.37), custom_call_target="tpu_custom_call" | custom-call | bytes 4194304 | tf_op jit(solution)/shard_map/pallas_call | solution.py:334
  49.5 4.4 %all-to-all-start.1 = ((bf16[256,8,256]{2,0,1:T(8,128)(2,1)}), bf16[256,8,256]{2,0,1:T(8,128)(2,1)}, u32[]{:S(2)}, u32[]{:S(2)}) async-start(bf16[256,8,256]{2,0,1:T(8,128)(2,1)} %bitcast.24), calls=%async_computation.1 | async-start | bytes 2097152 | tf_op jit(solution)/shard_map/all_to_all | solution.py:476
  53.9 16.9 %collective-permute-done.10.refs_12_ = bf16[512,512]{1,0:T(8,128)(2,1)} collective-permute-done((bf16[512,512]{1,0:T(8,128)(2,1)}, bf16[512,512]{1,0:T(8,128)(2,1)}, u32[]{:S(2)}, u32[]{:S(2)}) %collective-permute-start.10) | collective-permute-done | bytes 524320 | tf_op jit(solution)/shard_map/ppermute | solution.py:323
  77.2 29.1 %shard_map.68 = (bf16[2048,256]{1,0:T(8,128)(2,1)}, bf16[2048,512]{1,0:T(8,128)(2,1)}) custom-call(s32[2]{0:T(128)} %pad_add_fusion.places_ref, bf16[256,2048]{1,0:T(8,128)(2,1)} %bitcast.28, bf16[256,2048]{1,0:T(8,128)(2,1)} %collective-permute-done.2.refs_1_, bf16[256,2048]{1,0:T(8,128)(2,1)} %copy-done.1, ...), custom_call_target="tpu_custom_call" | custom-call | flops 12348030976 | bytes 16777216 | tf_op jit(solution)/shard_map/pallas_call | solution.py:502
  106.4 3.6 %all-to-all-start.2 = ((bf16[8,256,512]{2,1,0:T(8,128)(2,1)}), bf16[8,256,512]{2,1,0:T(8,128)(2,1)S(1)}, u32[]{:S(2)}, u32[]{:S(2)}) async-start(bf16[8,256,512]{2,1,0:T(8,128)(2,1)} %bitcast.25), calls=%async_computation.2 | async-start | bytes 4194304 | tf_op jit(solution)/shard_map/all_to_all | solution.py:544
  110.0 2.5 %collective-permute-start.19 = (bf16[512,256]{1,0:T(8,128)(2,1)S(1)}, bf16[512,256]{1,0:T(8,128)(2,1)S(1)}, u32[]{:S(2)}, u32[]{:S(2)}) collective-permute-start(bf16[512,256]{1,0:T(8,128)(2,1)S(1)} %get-tuple-element.70), channel_id=1, source_target_pairs={{0,3},{1,2},{2,1},{3,0},{4,7},{5,6},{6,5},{7,4},{8,11},{9,10},{10,... | collective-permute-start | bytes 786440 | tf_op jit(solution)/shard_map/ppermute | solution.py:323
  112.4 9.8 %collective-permute-start.18 = (bf16[512,256]{1,0:T(8,128)(2,1)S(1)}, bf16[512,256]{1,0:T(8,128)(2,1)S(1)}, u32[]{:S(2)}, u32[]{:S(2)}) collective-permute-start(bf16[512,256]{1,0:T(8,128)(2,1)S(1)} %get-tuple-element.70), channel_id=1, source_target_pairs={{0,2},{1,3},{2,0},{3,1},{4,6},{5,7},{6,4},{7,5},{8,10},{9,11},{10,... | collective-permute-start | bytes 786440 | tf_op jit(solution)/shard_map/ppermute | solution.py:323
  122.8 17.5 %collective-permute-done.18 = bf16[512,256]{1,0:T(8,128)(2,1)S(1)} collective-permute-done((bf16[512,256]{1,0:T(8,128)(2,1)S(1)}, bf16[512,256]{1,0:T(8,128)(2,1)S(1)}, u32[]{:S(2)}, u32[]{:S(2)}) %collective-permute-start.18) | collective-permute-done | bytes 262176 | tf_op jit(solution)/shard_map/ppermute | solution.py:323
  141.5 6.9 %shard_map.69 = (bf16[8,64,256]{2,1,0:T(8,128)(2,1)}, bf16[8,64,256]{2,1,0:T(8,128)(2,1)}, bf16[8,64,256]{2,1,0:T(8,128)(2,1)}, bf16[8,64,256]{2,1,0:T(8,128)(2,1)}) custom-call(s32[2]{0:T(128)} %pad_add_fusion.places_ref, bf16[256,2048]{1,0:T(8,128)(2,1)} %bitcast.29, bf16[256,2048]{1,0:T(8,128)(2,1)} %collective-permute-done.2.refs_1_, ...), custom_call_target="tpu_custom_call" | custom-call | flops 2147483648 | bytes 8388608 | tf_op jit(solution)/shard_map/pallas_call | solution.py:528
  148.5 3.2 %collective-permute-start.22 = (bf16[8,64,256]{2,1,0:T(8,128)(2,1)}, bf16[8,64,256]{2,1,0:T(8,128)(2,1)}, u32[]{:S(2)}, u32[]{:S(2)}) collective-permute-start(bf16[8,64,256]{2,1,0:T(8,128)(2,1)} %get-tuple-element.87), channel_id=1, source_target_pairs={{0,2},{1,3},{2,0},{3,1},{4,6},{5,7},{6,4},{7,5},{8,10},{9,11},{10,... | collective-permute-start | bytes 786440 | tf_op jit(solution)/shard_map/ppermute | solution.py:323
  156.7 9.5 %all_to_all.58.refs_10_ = bf16[8,32,256]{2,1,0:T(8,128)(2,1)} all-to-all(bf16[8,32,256]{2,1,0:T(8,128)(2,1)} %get-tuple-element.75), channel_id=1, replica_groups=mesh['seq'=8,'fsdp'=4] {'seq'}, dimensions={0} | all-to-all | bytes 262144 | tf_op jit(solution)/shard_map/all_to_all | solution.py:562
  166.2 5.8 %shard_map.73 = (bf16[8,64,32]{2,1,0:T(8,128)(2,1)}, bf16[8,64,32]{2,1,0:T(8,128)(2,1)}, bf16[8,64,32]{2,1,0:T(8,128)(2,1)}, bf16[8,64,32]{2,1,0:T(8,128)(2,1)}) custom-call(s32[2]{0:T(128)} %pad_add_fusion.places_ref, bf16[256,2048]{1,0:T(8,128)(2,1)} %bitcast.30, bf16[256,2048]{1,0:T(8,128)(2,1)} %collective-permute-done.2.refs_1_, ...), custom_call_target="tpu_custom_call" | custom-call | flops 268435456 | bytes 8388608 | tf_op jit(solution)/shard_map/pallas_call | solution.py:528
  172.1 3.2 %collective-permute-start.25 = (bf16[8,64,32]{2,1,0:T(8,128)(2,1)}, bf16[8,64,32]{2,1,0:T(8,128)(2,1)S(1)}, u32[]{:S(2)}, u32[]{:S(2)}) collective-permute-start(bf16[8,64,32]{2,1,0:T(8,128)(2,1)} %get-tuple-element.91), channel_id=1, source_target_pairs={{0,2},{1,3},{2,0},{3,1},{4,6},{5,7},{6,4},{7,5},{8,10},{9,11},{10,... | collective-permute-start | bytes 98312 | tf_op jit(solution)/shard_map/ppermute | solution.py:323
  176.5 3.1 %collective-permute-done.24.refs_5_ = bf16[8,64,32]{2,1,0:T(8,128)(2,1)S(1)} collective-permute-done((bf16[8,64,32]{2,1,0:T(8,128)(2,1)}, bf16[8,64,32]{2,1,0:T(8,128)(2,1)S(1)}, u32[]{:S(2)}, u32[]{:S(2)}) %collective-permute-start.24) | collective-permute-done | bytes 32800 | tf_op jit(solution)/shard_map/ppermute | solution.py:323
  179.5 5.9 %collective-permute-done.25.refs_6_ = bf16[8,64,32]{2,1,0:T(8,128)(2,1)S(1)} collective-permute-done((bf16[8,64,32]{2,1,0:T(8,128)(2,1)}, bf16[8,64,32]{2,1,0:T(8,128)(2,1)S(1)}, u32[]{:S(2)}, u32[]{:S(2)}) %collective-permute-start.25) | collective-permute-done | bytes 32800 | tf_op jit(solution)/shard_map/ppermute | solution.py:323
  188.5 3.4 %all-to-all-start.5 = ((bf16[8,80,256]{2,1,0:T(8,128)(2,1)}), bf16[8,80,256]{2,1,0:T(8,128)(2,1)S(1)}, u32[]{:S(2)}, u32[]{:S(2)}) async-start(bf16[8,80,256]{2,1,0:T(8,128)(2,1)} %shard_map.74), calls=%async_computation.5 | async-start | bytes 655360 | tf_op jit(solution)/shard_map/all_to_all | solution.py:611
  192.0 7.6 %all-to-all-done.5.packed_ref = bf16[8,80,256]{2,1,0:T(8,128)(2,1)S(1)} async-done(((bf16[8,80,256]{2,1,0:T(8,128)(2,1)}), bf16[8,80,256]{2,1,0:T(8,128)(2,1)S(1)}, u32[]{:S(2)}, u32[]{:S(2)}) %all-to-all-start.5) | async-done | bytes 327712 | tf_op jit(solution)/shard_map/all_to_all | solution.py:611
  199.5 3.6 %all-to-all-start.4 = ((bf16[8,256,256]{2,1,0:T(8,128)(2,1)}), bf16[8,256,256]{2,1,0:T(8,128)(2,1)S(1)}, u32[]{:S(2)}, u32[]{:S(2)}) async-start(bf16[8,256,256]{2,1,0:T(8,128)(2,1)} %bitcast.17), calls=%async_computation.4 | async-start | bytes 2097152 | tf_op jit(solution)/shard_map/all_to_all | solution.py:563
  203.1 8.0 %shard_map.72 = bf16[1,256,2048]{2,1,0:T(8,128)(2,1)} custom-call(s32[2]{0:T(128)} %pad_add_fusion.places_ref, bf16[8,256,512]{2,1,0:T(8,128)(2,1)} %copy-done, bf16[256,256]{1,0:T(8,128)(2,1)} %get-tuple-element.77.shared_ref, bf16[4,512,256]{2,1,0:T(8,128)(2,1)} %get-tuple-element.96.w_shared_ref, bf16[4,512,256]{2,1,0:T(8,128)(2,1)} %get-tuple-element.78.refs_0_, ...), custom_call_target="tpu_custom_call" | custom-call | flops 2415919104 | bytes 9437184 | tf_op jit(solution)/shard_map/pallas_call | solution.py:576
  213.0 5.5 %all-to-all-done.4.blocks_ref = bf16[8,256,256]{2,1,0:T(8,128)(2,1)S(1)} async-done(((bf16[8,256,256]{2,1,0:T(8,128)(2,1)}), bf16[8,256,256]{2,1,0:T(8,128)(2,1)S(1)}, u32[]{:S(2)}, u32[]{:S(2)}) %all-to-all-start.4) | async-done | bytes 1048608 | tf_op jit(solution)/shard_map/all_to_all | solution.py:563
  (88 shorter events, 38.2 us)
Async XLA Ops:
  0.6 28.2 %collective-permute-start = (bf16[256,2048]{1,0:T(8,128)(2,1)}, bf16[256,2048]{1,0:T(8,128)(2,1)S(1)}, u32[]{:S(2)}, u32[]{:S(2)}) collective-permute-start(bf16[256,2048]{1,0:T(8,128)(2,1)} %bitcast.26), channel_id=1, source_target_pairs={{0,8},{4,12},{8,0},{12,4},{16,24},{20,28},{24,16},{28,20},{1,9},{5... | collective-permute-start | bytes 3145736 | tf_op jit(solution)/shard_map/ppermute | solution.py:323
  3.6 25.2 %collective-permute-start.1 = (bf16[256,2048]{1,0:T(8,128)(2,1)}, bf16[256,2048]{1,0:T(8,128)(2,1)S(1)}, u32[]{:S(2)}, u32[]{:S(2)}) collective-permute-start(bf16[256,2048]{1,0:T(8,128)(2,1)} %bitcast.27), channel_id=1, source_target_pairs={{0,16},{4,20},{8,24},{12,28},{16,0},{20,4},{24,8},{28,12},{1,17},{... | collective-permute-start | bytes 3145736 | tf_op jit(solution)/shard_map/ppermute | solution.py:323
  6.5 22.3 %all-to-all-start = ((f32[8,4,256]{2,1,0:T(4,128)}), f32[8,4,256]{2,1,0:T(4,128)S(1)}, u32[]{:S(2)}, u32[]{:S(2)}) async-start(f32[8,4,256]{2,1,0:T(4,128)} %all_to_all.40), calls=%async_computation | async-start | bytes 65536 | tf_op jit(solution)/shard_map/all_to_all | solution.py:456
  12.1 33.7 %collective-permute-start.9 = (bf16[512,512]{1,0:T(8,128)(2,1)}, bf16[512,512]{1,0:T(8,128)(2,1)}, u32[]{:S(2)}, u32[]{:S(2)}) collective-permute-start(bf16[512,512]{1,0:T(8,128)(2,1)} %get-tuple-element.99.refs_10_), channel_id=1, source_target_pairs={{0,1},{1,0},{2,3},{3,2},{4,5},{5,4},{6,7},{7,6},{8,9},{9,8},{10,11... | collective-permute-start | bytes 1572872 | tf_op jit(solution)/shard_map/ppermute | solution.py:323
  29.7 16.2 %collective-permute-start.5 = (bf16[128,2048]{1,0:T(8,128)(2,1)}, bf16[128,2048]{1,0:T(8,128)(2,1)S(1)}, u32[]{:S(2)}, u32[]{:S(2)}) collective-permute-start(bf16[128,2048]{1,0:T(8,128)(2,1)} %slice.15), channel_id=1, source_target_pairs={{0,16},{4,20},{8,24},{12,28},{16,0},{20,4},{24,8},{28,12},{1,17},{... | collective-permute-start | bytes 1572872 | tf_op jit(solution)/shard_map/ppermute | solution.py:323
  32.1 14.6 %collective-permute-start.6 = (bf16[128,2048]{1,0:T(8,128)(2,1)}, bf16[128,2048]{1,0:T(8,128)(2,1)}, u32[]{:S(2)}, u32[]{:S(2)}) collective-permute-start(bf16[128,2048]{1,0:T(8,128)(2,1)} %slice.16), channel_id=1, source_target_pairs={{0,8},{4,12},{8,0},{12,4},{16,24},{20,28},{24,16},{28,20},{1,9},{5... | collective-permute-start | bytes 1572872 | tf_op jit(solution)/shard_map/ppermute | solution.py:323
  32.6 38.2 %collective-permute-start.10 = (bf16[512,512]{1,0:T(8,128)(2,1)}, bf16[512,512]{1,0:T(8,128)(2,1)}, u32[]{:S(2)}, u32[]{:S(2)}) collective-permute-start(bf16[512,512]{1,0:T(8,128)(2,1)} %get-tuple-element.99.refs_10_), channel_id=1, source_target_pairs={{0,2},{1,3},{2,0},{3,1},{4,6},{5,7},{6,4},{7,5},{8,10},{9,11},{10,... | collective-permute-start | bytes 1572872 | tf_op jit(solution)/shard_map/ppermute | solution.py:323
  35.2 35.6 %collective-permute-start.11 = (bf16[512,512]{1,0:T(8,128)(2,1)}, bf16[512,512]{1,0:T(8,128)(2,1)}, u32[]{:S(2)}, u32[]{:S(2)}) collective-permute-start(bf16[512,512]{1,0:T(8,128)(2,1)} %get-tuple-element.99.refs_10_), channel_id=1, source_target_pairs={{0,3},{1,2},{2,1},{3,0},{4,7},{5,6},{6,5},{7,4},{8,11},{9,10},{10,... | collective-permute-start | bytes 1572872 | tf_op jit(solution)/shard_map/ppermute | solution.py:323
  45.8 31.4 %collective-permute-start.2 = (bf16[256,2048]{1,0:T(8,128)(2,1)S(1)}, bf16[256,2048]{1,0:T(8,128)(2,1)}, u32[]{:S(2)}, u32[]{:S(2)}) collective-permute-start(bf16[256,2048]{1,0:T(8,128)(2,1)S(1)} %bitcast.31), channel_id=1, source_target_pairs={{0,4},{4,0},{8,12},{12,8},{16,20},{20,16},{24,28},{28,24},{1,5},{5... | collective-permute-start | bytes 3145736 | tf_op jit(solution)/shard_map/ppermute | solution.py:323
  45.9 31.3 %collective-permute-start.3 = (bf16[256,2048]{1,0:T(8,128)(2,1)S(1)}, bf16[256,2048]{1,0:T(8,128)(2,1)}, u32[]{:S(2)}, u32[]{:S(2)}) collective-permute-start(bf16[256,2048]{1,0:T(8,128)(2,1)S(1)} %collective-permute-done.refs_2_), channel_id=1, source_target_pairs={{0,4},{4,0},{8,12},{12,8},{16,20},{20,16},{24,28},{28,24},{1,5},{5... | collective-permute-start | bytes 3145736 | tf_op jit(solution)/shard_map/ppermute | solution.py:323
  46.7 30.5 %collective-permute-start.4 = (bf16[256,2048]{1,0:T(8,128)(2,1)S(1)}, bf16[256,2048]{1,0:T(8,128)(2,1)}, u32[]{:S(2)}, u32[]{:S(2)}) collective-permute-start(bf16[256,2048]{1,0:T(8,128)(2,1)S(1)} %collective-permute-done.1.refs_4_), channel_id=1, source_target_pairs={{0,4},{4,0},{8,12},{12,8},{16,20},{20,16},{24,28},{28,24},{1,5},{5... | collective-permute-start | bytes 3145736 | tf_op jit(solution)/shard_map/ppermute | solution.py:323
  49.5 27.7 %all-to-all-start.1 = ((bf16[256,8,256]{2,0,1:T(8,128)(2,1)}), bf16[256,8,256]{2,0,1:T(8,128)(2,1)}, u32[]{:S(2)}, u32[]{:S(2)}) async-start(bf16[256,8,256]{2,0,1:T(8,128)(2,1)} %bitcast.24), calls=%async_computation.1 | async-start | bytes 2097152 | tf_op jit(solution)/shard_map/all_to_all | solution.py:476
  75.2 65.8 %collective-permute-start.13 = (bf16[4,512,256]{2,1,0:T(8,128)(2,1)}, bf16[4,512,256]{2,1,0:T(8,128)(2,1)}, u32[]{:S(2)}, u32[]{:S(2)}) collective-permute-start(bf16[4,512,256]{2,1,0:T(8,128)(2,1)} %get-tuple-element.78.refs_0_), channel_id=1, source_target_pairs={{0,8},{4,12},{8,0},{12,4},{16,24},{20,28},{24,16},{28,20},{1,9},{5... | collective-permute-start | bytes 3145736 | tf_op jit(solution)/shard_map/ppermute | solution.py:323
  76.7 64.3 %collective-permute-start.15 = (bf16[4,512,256]{2,1,0:T(8,128)(2,1)}, bf16[4,512,256]{2,1,0:T(8,128)(2,1)}, u32[]{:S(2)}, u32[]{:S(2)}) collective-permute-start(bf16[4,512,256]{2,1,0:T(8,128)(2,1)} %get-tuple-element.78.refs_0_), channel_id=1, source_target_pairs={{0,16},{4,20},{8,24},{12,28},{16,0},{20,4},{24,8},{28,12},{1,17},{... | collective-permute-start | bytes 3145736 | tf_op jit(solution)/shard_map/ppermute | solution.py:323
  106.4 46.5 %all-to-all-start.2 = ((bf16[8,256,512]{2,1,0:T(8,128)(2,1)}), bf16[8,256,512]{2,1,0:T(8,128)(2,1)S(1)}, u32[]{:S(2)}, u32[]{:S(2)}) async-start(bf16[8,256,512]{2,1,0:T(8,128)(2,1)} %bitcast.25), calls=%async_computation.2 | async-start | bytes 4194304 | tf_op jit(solution)/shard_map/all_to_all | solution.py:544
  110.0 12.8 %collective-permute-start.19 = (bf16[512,256]{1,0:T(8,128)(2,1)S(1)}, bf16[512,256]{1,0:T(8,128)(2,1)S(1)}, u32[]{:S(2)}, u32[]{:S(2)}) collective-permute-start(bf16[512,256]{1,0:T(8,128)(2,1)S(1)} %get-tuple-element.70), channel_id=1, source_target_pairs={{0,3},{1,2},{2,1},{3,0},{4,7},{5,6},{6,5},{7,4},{8,11},{9,10},{10,... | collective-permute-start | bytes 786440 | tf_op jit(solution)/shard_map/ppermute | solution.py:323
  112.4 27.8 %collective-permute-start.18 = (bf16[512,256]{1,0:T(8,128)(2,1)S(1)}, bf16[512,256]{1,0:T(8,128)(2,1)S(1)}, u32[]{:S(2)}, u32[]{:S(2)}) collective-permute-start(bf16[512,256]{1,0:T(8,128)(2,1)S(1)} %get-tuple-element.70), channel_id=1, source_target_pairs={{0,2},{1,3},{2,0},{3,1},{4,6},{5,7},{6,4},{7,5},{8,10},{9,11},{10,... | collective-permute-start | bytes 786440 | tf_op jit(solution)/shard_map/ppermute | solution.py:323
  122.3 18.0 %collective-permute-start.17 = (bf16[512,256]{1,0:T(8,128)(2,1)S(1)}, bf16[512,256]{1,0:T(8,128)(2,1)S(1)}, u32[]{:S(2)}, u32[]{:S(2)}) collective-permute-start(bf16[512,256]{1,0:T(8,128)(2,1)S(1)} %get-tuple-element.70), channel_id=1, source_target_pairs={{0,1},{1,0},{2,3},{3,2},{4,5},{5,4},{6,7},{7,6},{8,9},{9,8},{10,11... | collective-permute-start | bytes 786440 | tf_op jit(solution)/shard_map/ppermute | solution.py:323
  141.0 11.9 %collective-permute-start.14 = (bf16[4,512,256]{2,1,0:T(8,128)(2,1)}, bf16[4,512,256]{2,1,0:T(8,128)(2,1)}, u32[]{:S(2)}, u32[]{:S(2)}) collective-permute-start(bf16[4,512,256]{2,1,0:T(8,128)(2,1)} %collective-permute-done.13.refs_2_), channel_id=1, source_target_pairs={{0,4},{4,0},{8,12},{12,8},{16,20},{20,16},{24,28},{28,24},{1,5},{5... | collective-permute-start | bytes 3145736 | tf_op jit(solution)/shard_map/ppermute | solution.py:323
  148.4 26.9 %collective-permute-start.21 = (bf16[8,64,256]{2,1,0:T(8,128)(2,1)}, bf16[8,64,256]{2,1,0:T(8,128)(2,1)S(1)}, u32[]{:S(2)}, u32[]{:S(2)}) collective-permute-start(bf16[8,64,256]{2,1,0:T(8,128)(2,1)} %get-tuple-element.86), channel_id=1, source_target_pairs={{0,1},{1,0},{2,3},{3,2},{4,5},{5,4},{6,7},{7,6},{8,9},{9,8},{10,11... | collective-permute-start | bytes 786440 | tf_op jit(solution)/shard_map/ppermute | solution.py:323
  148.5 28.0 %collective-permute-start.22 = (bf16[8,64,256]{2,1,0:T(8,128)(2,1)}, bf16[8,64,256]{2,1,0:T(8,128)(2,1)}, u32[]{:S(2)}, u32[]{:S(2)}) collective-permute-start(bf16[8,64,256]{2,1,0:T(8,128)(2,1)} %get-tuple-element.87), channel_id=1, source_target_pairs={{0,2},{1,3},{2,0},{3,1},{4,6},{5,7},{6,4},{7,5},{8,10},{9,11},{10,... | collective-permute-start | bytes 786440 | tf_op jit(solution)/shard_map/ppermute | solution.py:323
  151.7 24.8 %collective-permute-start.23 = (bf16[8,64,256]{2,1,0:T(8,128)(2,1)}, bf16[8,64,256]{2,1,0:T(8,128)(2,1)S(1)}, u32[]{:S(2)}, u32[]{:S(2)}) collective-permute-start(bf16[8,64,256]{2,1,0:T(8,128)(2,1)} %get-tuple-element.88), channel_id=1, source_target_pairs={{0,3},{1,2},{2,1},{3,0},{4,7},{5,6},{6,5},{7,4},{8,11},{9,10},{10,... | collective-permute-start | bytes 786440 | tf_op jit(solution)/shard_map/ppermute | solution.py:323
  172.1 13.4 %collective-permute-start.25 = (bf16[8,64,32]{2,1,0:T(8,128)(2,1)}, bf16[8,64,32]{2,1,0:T(8,128)(2,1)S(1)}, u32[]{:S(2)}, u32[]{:S(2)}) collective-permute-start(bf16[8,64,32]{2,1,0:T(8,128)(2,1)} %get-tuple-element.91), channel_id=1, source_target_pairs={{0,2},{1,3},{2,0},{3,1},{4,6},{5,7},{6,4},{7,5},{8,10},{9,11},{10,... | collective-permute-start | bytes 98312 | tf_op jit(solution)/shard_map/ppermute | solution.py:323
  199.5 18.9 %all-to-all-start.4 = ((bf16[8,256,256]{2,1,0:T(8,128)(2,1)}), bf16[8,256,256]{2,1,0:T(8,128)(2,1)S(1)}, u32[]{:S(2)}, u32[]{:S(2)}) async-start(bf16[8,256,256]{2,1,0:T(8,128)(2,1)} %bitcast.17), calls=%async_computation.4 | async-start | bytes 2097152 | tf_op jit(solution)/shard_map/all_to_all | solution.py:563
  (22 other events, 201.8 us)

commit v4 on v3

v4 whole, which is shorter than its diff:
```python
import functools

import jax
import jax.numpy as jnp
from jax import lax
from jax.experimental import pallas as pl
from jax.experimental.pallas import tpu as pltpu
from jax.sharding import PartitionSpec as P

CHUNK = 128
EPSILON = 1e-05
VMEM_LIMIT = 60 * 1024 * 1024

f32 = jnp.float32
bf16 = jnp.bfloat16


def dot_nn(a, b):
    return lax.dot_general(a, b, (((1,), (0,)), ((), ())), preferred_element_type=f32)


def dot_nt(a, b):
    return lax.dot_general(a, b, (((1,), (1,)), ((), ())), preferred_element_type=f32)


def dot_tn(a, b):
    return lax.dot_general(a, b, (((0,), (0,)), ((), ())), preferred_element_type=f32)


def by_head(rows, heads, head_size):
    if heads == 1:
        return rows
    lane = lax.broadcasted_iota(jnp.int32, rows.shape, 1)
    parts = []
    for h in range(heads):
        inside = (lane >= h * head_size) & (lane < (h + 1) * head_size)
        parts.append(jnp.where(inside, rows, jnp.zeros_like(rows)))
    return jnp.concatenate(parts, axis=0)


def decayed(affinity, decays, heads):
    tiled = jnp.concatenate([affinity] * heads, axis=1) if heads > 1 else affinity
    return (tiled * decays.astype(f32)).astype(bf16)


def spans(k, state_size):
    rows = pl.ds(pl.multiple_of(k * CHUNK, CHUNK), CHUNK)
    return rows, pl.ds(pl.multiple_of(k * state_size, state_size), state_size)


def fill_mean(mean_ref, heads, head_size):
    row = lax.broadcasted_iota(jnp.int32, mean_ref.shape, 0)
    col = lax.broadcasted_iota(jnp.int32, mean_ref.shape, 1)
    same = jnp.zeros(mean_ref.shape, jnp.bool_)
    for h in range(heads):
        low, high = h * head_size, (h + 1) * head_size
        same |= (row >= low) & (row < high) & (col >= low) & (col < high)
    mean_ref[...] = jnp.where(same, 1.0 / head_size, 0.0).astype(bf16)


def forward_kernel(sources, arrays, slots, group, heads, head_size, place_ref, *refs):
    array_refs, refs = refs[:arrays], refs[arrays:]
    in_hbm, out_hbm, refs = refs[:7], refs[7:14], refs[14:]
    in_refs, out_refs, (held, mean_ref, carry, sems, loads, stores) = refs[:7], refs[7:14], refs[14:]
    w_ref, m_ref, te_ref, fs_ref, en_ref, lv_ref, dt_ref = in_refs
    x_ref, b_ref, c_ref, z_ref, rs_ref, sf_ref, rn_ref = out_refs
    pieces = len(sources)
    rows_each = held.shape[1]
    width, state_size = x_ref.shape[1], b_ref.shape[1]
    chunks = dt_ref.shape[0]

    def fetch(i):
        array, start = sources[i]
        source = array_refs[array].at[pl.ds(start, rows_each)]
        return pltpu.make_async_copy(source, held.at[i % slots], sems.at[i % slots])

    in_loads = [
        pltpu.make_async_copy(source, target, loads.at[n])
        for n, (source, target) in enumerate(zip(in_hbm, in_refs))
    ]
    out_stores = [
        pltpu.make_async_copy(source, target, stores.at[n])
        for n, (source, target) in enumerate(zip(out_refs, out_hbm))
    ]
    in_loads[0].start()
    for i in range(slots):
        fetch(i).start()
    for load in in_loads[1:]:
        load.start()
    fill_mean(mean_ref, heads, head_size)

    in_loads[0].wait()
    for first in range(0, pieces, group):
        for i in range(first, first + group):
            fetch(i).wait()
        slot = first % slots
        block = held[slot : slot + group].reshape(group * rows_each, held.shape[2])
        result = dot_nn(block, w_ref[...]).astype(bf16)
        for i in range(first, first + group):
            if i + slots < pieces:
                fetch(i + slots).start()
            offset = (2 * lax.bitwise_xor(place_ref[0], i // 2) + i % 2) * rows_each
            target = pl.ds(pl.multiple_of(offset, rows_each), rows_each)
            part = slice((i - first) * rows_each, (i - first + 1) * rows_each)
            x_ref[target, :] = result[part, :width]
            b_ref[target, :] = result[part, width : width + state_size]
            c_ref[target, :] = result[part, width + state_size :]
    for store in out_stores[:3]:
        store.start()
    for load in in_loads[1:]:
        load.wait()

    carry[...] = jnp.zeros_like(carry)

    def reverse_states(i, _):
        k = chunks - 1 - i
        rows, state = spans(k, state_size)
        rn_ref[state, :] = carry[...].astype(bf16)
        term = dot_tn(b_ref[rows, :], x_ref[rows, :] * fs_ref[rows, :])
        carry[...] = dt_ref[k] * carry[...] + term
        return 0

    lax.fori_loop(0, chunks, reverse_states, 0, unroll=2)
    out_stores[6].start()
    carry[...] = jnp.zeros_like(carry)

    def outputs(k, _):
        rows, state = spans(k, state_size)
        x, b, c = x_ref[rows, :], b_ref[rows, :], c_ref[rows, :]
        state_in = carry[...].astype(bf16)
        sf_ref[state, :] = state_in
        weights = decayed(dot_nt(c, b), m_ref[rows, :], heads)
        y = dot_nn(weights, by_head(x, heads, head_size))
        y = y + en_ref[rows, :].astype(f32) * dot_nn(c, state_in)
        y = y + lv_ref[rows, :].astype(f32) * dot_nn(c, rn_ref[state, :])
        mean_square = dot_nn((y * y).astype(bf16), mean_ref[...])
        inverse = lax.rsqrt(mean_square + EPSILON)
        z_ref[rows, :] = (y * inverse).astype(bf16)
        rs_ref[rows, :] = inverse.astype(bf16)
        carry[...] = dt_ref[k] * carry[...] + dot_tn(b, x * te_ref[rows, :])
        return 0

    lax.fori_loop(0, chunks, outputs, 0, unroll=2)
    for store in out_stores[3:6]:
        store.start()
    for store in out_stores:
        store.wait()


def backward_kernel(heads, head_size, *refs):
    in_hbm, out_hbm, refs = refs[:15], refs[15:17], refs[17:]
    in_refs, (dx_ref, shared_ref), refs = refs[:15], refs[15:17], refs[17:]
    dy_ref, ge_ref, mean_ref, carry, loads, stores = refs
    g_ref, z_ref, rs_ref, c_ref, en_ref, dt_ref = in_refs[:6]
    x_ref, b_ref, m_ref, mt_ref, te_ref, fs_ref, lv_ref, sf_ref, rn_ref = in_refs[6:15]
    state_size = b_ref.shape[1]
    chunks = dt_ref.shape[0]
    in_loads = [
        pltpu.make_async_copy(source, target, loads.at[n])
        for n, (source, target) in enumerate(zip(in_hbm, in_refs))
    ]
    for load in in_loads:
        load.start()
    fill_mean(mean_ref, heads, head_size)
    carry[...] = jnp.zeros_like(carry)
    for load in in_loads[:6]:
        load.wait()

    def end_adjoints(i, _):
        k = chunks - 1 - i
        rows, state = spans(k, state_size)
        g, z = g_ref[rows, :].astype(f32), z_ref[rows, :].astype(f32)
        mean_gz = dot_nn((g * z).astype(bf16), mean_ref[...])
        dy = ((g - z * mean_gz) * rs_ref[rows, :].astype(f32)).astype(bf16)
        dy_ref[rows, :] = dy
        ge_ref[state, :] = carry[...].astype(bf16)
        carry[...] = dt_ref[k] * carry[...] + dot_tn(c_ref[rows, :], dy * en_ref[rows, :])
        return 0

    lax.fori_loop(0, chunks, end_adjoints, 0, unroll=2)
    carry[...] = jnp.zeros_like(carry)
    for load in in_loads[6:]:
        load.wait()

    def gradients(k, _):
        rows, state = spans(k, state_size)
        x, b, c, dy = x_ref[rows, :], b_ref[rows, :], c_ref[rows, :], dy_ref[rows, :]
        te, fs, en, lv = te_ref[rows, :], fs_ref[rows, :], en_ref[rows, :], lv_ref[rows, :]
        ge, gs = ge_ref[state, :], carry[...].astype(bf16)
        grad_weights = dot_nt(dy, by_head(x, heads, head_size)) * m_ref[rows, :].astype(f32)
        da = grad_weights[:, :CHUNK]
        for h in range(1, heads):
            da = da + grad_weights[:, h * CHUNK : (h + 1) * CHUNK]
        da = da.astype(bf16)
        turned = decayed(dot_nt(b, c), mt_ref[rows, :], heads)
        dx = dot_nn(turned, by_head(dy, heads, head_size))
        dx = dx + te.astype(f32) * dot_nn(b, ge)
        dx = dx + fs.astype(f32) * dot_nn(b, gs)
        dx_ref[rows, :] = dx.astype(bf16)
        dy_lv = dy * lv
        dc = dot_nn(da, b) + dot_nt(dy * en, sf_ref[state, :]) + dot_nt(dy_lv, rn_ref[state, :])
        db = dot_tn(da, c) + dot_nt(x * te, ge) + dot_nt(x * fs, gs)
        shared_ref[:state_size, rows] = db.T.astype(bf16)
        shared_ref[state_size:, rows] = dc.T.astype(bf16)
        carry[...] = dt_ref[k] * carry[...] + dot_tn(c, dy_lv)
        return 0

    lax.fori_loop(0, chunks, gradients, 0, unroll=2)
    out_stores = [
        pltpu.make_async_copy(source, target, stores.at[n])
        for n, (source, target) in enumerate(zip((dx_ref, shared_ref), out_hbm))
    ]
    for store in out_stores:
        store.start()
    for store in out_stores:
        store.wait()


def sum_kernel(parts_ref, dx_ref, sum_ref, packed_ref):
    total = parts_ref[0].astype(f32)
    for n in range(1, parts_ref.shape[0]):
        total = total + parts_ref[n].astype(f32)
    total = total.astype(bf16)
    sum_ref[...] = total
    count = packed_ref.shape[0]
    part, tokens = total.shape[0], total.shape[1] // count
    if packed_ref.shape[1] > tokens + part or packed_ref.shape[2] > dx_ref.shape[1]:
        packed_ref[...] = jnp.zeros_like(packed_ref)
    for n in range(count):
        block = slice(n * tokens, (n + 1) * tokens)
        packed_ref[n, :tokens, : dx_ref.shape[1]] = dx_ref[block, :]
        packed_ref[n, tokens : tokens + part, :tokens] = total[:, block]


def tokens_kernel(place_ref, packed_ref, own_ref, partner_ref, even_ref, odd_ref, out_ref, *lhs):
    own_lhs, partner_lhs, even_lhs, odd_lhs = lhs
    count = packed_ref.shape[0]
    tokens, width = partner_lhs.shape
    part = (own_lhs.shape[1] - width) // count

    @pl.when(pl.program_id(0) == 0)
    def _():
        for r in range(count):
            target = (even_lhs, odd_lhs)[r % 2] if r > 1 else (own_lhs, partner_lhs)[r]
            start = (r // 2 - 1) * width if r > 1 else 0
            source = lax.bitwise_xor(place_ref[0], r)
            target[:, start : start + width] = packed_ref[source, :tokens, :width]
        turned = [packed_ref[n, tokens : tokens + part, :tokens] for n in range(count)]
        own_lhs[:, width:] = jnp.concatenate(turned, axis=0).T

    result = dot_nt(own_lhs[...], own_ref[...])
    result = result + dot_nt(partner_lhs[...], partner_ref[:, :width])
    result = result + dot_nt(even_lhs[...], even_ref[...])
    result = result + dot_nt(odd_lhs[...], odd_ref[...])
    out_ref[0] = result.astype(bf16)


def spread_kernel(blocks_ref, out_ref):
    width = blocks_ref.shape[2]
    for n in range(blocks_ref.shape[0]):
        out_ref[0, :, n * width : (n + 1) * width] = blocks_ref[n]


def add_kernel(*refs):
    head_ref, shared_refs, out_ref = refs[0], refs[1:-1], refs[-1]
    rows = head_ref.shape[1]
    out_ref[:, :rows, :] = head_ref[...]
    total = shared_refs[0][...].astype(f32)
    for ref in shared_refs[1:]:
        total = total + ref[...].astype(f32)
    total = total.astype(bf16)
    extra = out_ref.shape[1] - rows
    part = total.shape[2]
    out_ref[:, rows:, :] = jnp.zeros((out_ref.shape[0], extra, out_ref.shape[2]), bf16)
    for q in range(rows // extra):
        out_ref[:, rows:, q * part : (q + 1) * part] = total[:, q * extra : (q + 1) * extra]


def weight_kernel(sources, arrays, slots, group, parts, is_turned, places_ref, *refs):
    array_refs, grad_ref = refs[:arrays], refs[arrays]
    out_refs, (held, total, result, sems) = refs[arrays + 1 : -4], refs[-4:]
    pieces = len(sources)
    rows = held.shape[1]
    hidden = held.shape[2]

    def fetch(i):
        array, start = sources[i]
        source = array_refs[array].at[pl.ds(start, rows)]
        return pltpu.make_async_copy(source, held.at[i % slots], sems.at[i % slots])

    for i in range(slots):
        fetch(i).start()
    for first in range(0, pieces, group):
        turned = []
        for i in range(first, first + group):
            offset = (2 * lax.bitwise_xor(places_ref[0], i // 2) + i % 2) * rows
            target = pl.ds(pl.multiple_of(offset, rows), rows)
            turned.append(grad_ref[:, target] if is_turned else grad_ref[target, :].T)
        for i in range(first, first + group):
            fetch(i).wait()
        slot = first % slots
        block = held[slot : slot + group].reshape(group * rows, hidden)
        term = dot_nn(jnp.concatenate(turned, axis=1), block)
        if first > 0:
            term = term + total[...]
        if first + group < pieces:
            total[...] = term
        else:
            result[...] = term.T.astype(bf16)
        for i in range(first, first + group):
            if i + slots < pieces:
                fetch(i + slots).start()
    each = out_refs[0].shape[-2]
    count = hidden // (parts * each)
    for k in range(parts):
        for j in range(count):
            if len(out_refs) == 1:
                out_refs[0][k, j] = result[(j * parts + k) * each : (j * parts + k + 1) * each, :]
            else:
                mine = (j * parts + lax.bitwise_xor(places_ref[1], k)) * each
                out_refs[k][j] = result[pl.ds(pl.multiple_of(mine, each), each), :]


def finish_kernel(packed_ref, out_ref):
    count, _, width = packed_ref.shape
    rows = out_ref.shape[0]
    extra = packed_ref.shape[1] - rows
    part = (out_ref.shape[1] - count * width) // count
    for n in range(count):
        out_ref[:, n * width : (n + 1) * width] = packed_ref[n, :rows].astype(f32)
        start = count * width + n * part
        for q in range(rows // extra):
            block = packed_ref[n, rows:, q * part : (q + 1) * part]
            out_ref[q * extra : (q + 1) * extra, start : start + part] = block.astype(f32)


def resident(array):
    return pl.BlockSpec(array.shape, lambda k: (0,) * len(array.shape))


def after(value, *earlier):
    return lax.optimization_barrier((value,) + earlier)[0]


def permute_xor(a, axis, mask):
    count = lax.axis_size(axis)
    return lax.ppermute(a, axis, [(i, i ^ mask) for i in range(count)])


def gather_rows(rows, axis, beside, work, last):
    count = lax.axis_size(axis)
    bits = count.bit_length() - 1
    half = rows.shape[0] // 2
    if bits == 3:
        held = {r: permute_xor(rows, axis, r) for r in (2, 4, 1)}
        held, beside = lax.optimization_barrier((held, beside))
        held[3], held[5] = permute_xor(held[2], axis, 1), permute_xor(held[4], axis, 1)
        corner = [
            permute_xor(held[2][:half], axis, 4),
            permute_xor(held[4][half:], axis, 2),
        ]
        last = after(last, held[3])
        held, corner, done = lax.optimization_barrier((held, corner, work(beside)))
        held = {r: [a] for r, a in held.items()}
        held[0], held[6] = [rows], corner
        held[7] = [permute_xor(a, axis, 1) for a in corner]
    else:
        done = work(beside)
        upper = list(range(1, bits))
        orders = (upper + [0], upper[1:] + upper[:1] + [0])
        both = ({0: rows[:half]}, {0: rows[half:]})
        for step in range(bits):
            for part in range(2):
                mask = 1 << orders[part][step]
                for r in list(both[part]):
                    both[part][r ^ mask] = permute_xor(both[part][r], axis, mask)
        held = {r: [both[0][r], both[1][r]] for r in range(count)}
    arrays, sources = [], []
    for r in range(count):
        for part in range(2):
            whole_block = len(held[r]) == 1
            if part == 0 or not whole_block:
                arrays.append(held[r][part])
            sources.append((len(arrays) - 1, half * part if whole_block else 0))
    return arrays, tuple(sources), done, last


def exchange_xor(pieces, axis):
    return [pieces[0]] + [permute_xor(p, axis, r) for r, p in enumerate(pieces) if r > 0]


def tables_kernel(log_ref, *refs):
    out_refs, table_refs, sems = refs[:7], refs[7:14], refs[14]
    te_ref, fs_ref, en_ref, lv_ref, dt_ref, m_ref, mt_ref = table_refs
    heads = log_ref.shape[0]
    chunks = dt_ref.shape[0]
    head_size = te_ref.shape[1] // heads
    row = lax.broadcasted_iota(jnp.int32, (CHUNK, CHUNK), 0)
    col = lax.broadcasted_iota(jnp.int32, (CHUNK, CHUNK), 1)
    logs = jnp.concatenate(
        [log_ref[:, k * CHUNK : (k + 1) * CHUNK] for k in range(chunks)], axis=0
    )
    cumulative = lax.dot_general(
        logs, (row <= col).astype(f32), (((1,), (0,)), ((), ())),
        precision=lax.Precision.HIGHEST, preferred_element_type=f32,
    )
    exclusive = cumulative - logs
    cum_t, exc_t = cumulative.T, exclusive.T
    total = cum_t[CHUNK - 1 : CHUNK, :]
    spreads = (
        (te_ref, jnp.exp(total - cum_t)),
        (fs_ref, jnp.exp(exc_t)),
        (en_ref, jnp.exp(cum_t)),
        (lv_ref, jnp.exp(total - exc_t)),
    )
    chunk_decay = jnp.exp(total)
    diagonal = (row == col).astype(f32)
    for k in range(chunks):
        rows = slice(k * CHUNK, (k + 1) * CHUNK)
        picked = range(k * heads, (k + 1) * heads)
        for ref, source in spreads:
            ref[rows, :] = jnp.concatenate(
                [jnp.broadcast_to(source[:, n : n + 1], (CHUNK, head_size)) for n in picked], axis=1
            ).astype(bf16)
        dt_ref[k] = jnp.concatenate(
            [jnp.broadcast_to(chunk_decay[:, n : n + 1], (1, head_size)) for n in picked], axis=1
        )
        for h, n in enumerate(picked):
            cum_col, exc_col = cum_t[:, n : n + 1], exc_t[:, n : n + 1]
            cum_row, exc_row = cumulative[n : n + 1, :], exclusive[n : n + 1, :]
            below, above = cum_col - cum_row, exc_row - exc_col
            exponent = jnp.where(row > col, below, jnp.where(row < col, above, 0.0))
            turned = jnp.where(row < col, -below, jnp.where(row > col, -above, 0.0))
            columns = slice(h * CHUNK, (h + 1) * CHUNK)
            m_ref[rows, columns] = (jnp.exp(exponent) + diagonal).astype(bf16)
            mt_ref[rows, columns] = (jnp.exp(turned) + diagonal).astype(bf16)
    stores = [
        pltpu.make_async_copy(source, target, sems.at[n])
        for n, (source, target) in enumerate(zip(table_refs, out_refs))
    ]
    for store in stores:
        store.start()
    for store in stores:
        store.wait()


def on_device(tokens, w_in, log_decay, grad_out):
    local_tokens = tokens[0]
    upstream = grad_out[0]
    token_count, hidden_width = local_tokens.shape
    head_count = log_decay.shape[1]
    inner_width = upstream.shape[1]
    head_size = inner_width // head_count
    state_size = (w_in.shape[1] - inner_width) // 2
    seq_count = lax.axis_size("seq")
    fsdp_count = lax.axis_size("fsdp")
    place = lax.axis_index("seq")
    row_place = lax.axis_index("fsdp")
    heads = head_count // seq_count
    width = heads * head_size
    length = token_count * seq_count
    shared = 2 * state_size
    chunks = length // CHUNK
    extent = hidden_width // fsdp_count
    shape = jax.ShapeDtypeStruct
    params = pltpu.CompilerParams(vmem_limit_bytes=VMEM_LIMIT)
    scalar = [pl.BlockSpec(memory_space=pltpu.SMEM)]
    places = jnp.stack([place, row_place]).astype(jnp.int32)

    def cost(flops, moved):
        return pl.CostEstimate(flops=flops, bytes_accessed=moved, transcendentals=0)

    def columns(r):
        return lax.dynamic_slice_in_dim(w_in, lax.bitwise_xor(place, r) * width, width, 1)

    w_columns = lax.all_gather(
        jnp.concatenate([columns(0), w_in[:, inner_width:]], axis=1), "fsdp", axis=0, tiled=True
    )
    log_rates = lax.all_to_all(log_decay[0], "seq", 0, 1, tiled=True)

    table_shapes = (
        [shape((length, width), bf16)] * 4
        + [shape((chunks, 1, width), f32)]
        + [shape((length, heads * CHUNK), bf16)] * 2
    )
    in_hbm = [pl.BlockSpec(memory_space=pltpu.HBM)]
    scratch = lambda *buffers: [pltpu.VMEM(a.shape, a.dtype) for a in buffers]
    make_tables = pl.pallas_call(
        tables_kernel,
        grid=(1,),
        out_shape=table_shapes,
        in_specs=[resident(log_rates)],
        out_specs=in_hbm * 7,
        scratch_shapes=scratch(*table_shapes) + [pltpu.SemaphoreType.DMA((7,))],
        compiler_params=params,
        cost_estimate=cost(0, 120 * length * width),
    )
    arrays, sources, tables, upstream = gather_rows(
        local_tokens, "seq", log_rates, make_tables, upstream
    )
    to_end, from_start, enter, leave, chunk_decay, decays, turned = tables

    count = len(sources)
    slots = min(count, 16)
    group = min(slots, 4)
    held = shape((slots, token_count // 2, hidden_width), bf16)
    by_position = shape((length, width), bf16)
    by_state = shape((chunks * state_size, width), bf16)
    state_rows = shape((length, state_size), bf16)
    mean = shape((width, width), bf16)
    carry = shape((state_size, width), f32)

    rest = jnp.concatenate([columns(r) for r in range(2, seq_count, 2)], axis=1)
    w_even = lax.all_gather(after(rest, w_columns), "fsdp", axis=0, tiled=True)

    *arrays, w_columns = lax.optimization_barrier((*arrays, w_columns))
    g = lax.all_to_all(upstream, "seq", 1, 0, tiled=True)
    operands = (w_columns, decays, to_end, from_start, enter, leave, chunk_decay)
    kept = [by_position, state_rows, state_rows, by_position, by_position, by_state, by_state]
    forward = pl.pallas_call(
        functools.partial(
            forward_kernel, sources, len(arrays), slots, group, heads, head_size
        ),
        out_shape=kept,
        in_specs=scalar + in_hbm * (len(arrays) + 7),
        out_specs=in_hbm * 7,
        scratch_shapes=scratch(*operands, *kept, held, mean, carry)
        + [
            pltpu.SemaphoreType.DMA((slots,)),
            pltpu.SemaphoreType.DMA((7,)),
            pltpu.SemaphoreType.DMA((7,)),
        ],
        compiler_params=params,
        cost_estimate=cost(
            4 * length * hidden_width * (width + shared) + 160 * length * width * CHUNK,
            4 * length * hidden_width,
        ),
    )(places, *arrays, *operands)
    (x, b, c, z, inverse, states_in, states_next), g = lax.optimization_barrier((forward, g))

    mixed_blocks = lax.all_to_all(z.reshape(seq_count, token_count, width), "seq", 0, 0)
    operands = (
        g, z, inverse, c, enter, chunk_decay,
        x, b, decays, turned, to_end, from_start, leave, states_in, states_next,
    )
    grads = [by_position, shape((shared, length), bf16)]
    backward = pl.pallas_call(
        functools.partial(backward_kernel, heads, head_size),
        out_shape=grads,
        in_specs=in_hbm * 15,
        out_specs=in_hbm * 2,
        scratch_shapes=scratch(*operands, *grads, by_position, by_state, mean, carry)
        + [pltpu.SemaphoreType.DMA((15,)), pltpu.SemaphoreType.DMA((2,))],
        compiler_params=params,
        cost_estimate=cost(240 * length * width * CHUNK, 40 * length * width),
    )(*operands)
    (dx, shared_partial), mixed_blocks = lax.optimization_barrier((backward, mixed_blocks))

    rows_each = hidden_width // (seq_count * fsdp_count)

    def weight_columns(grad, columns, is_turned):
        total = shape((columns, hidden_width), f32)
        result = shape((hidden_width, columns), bf16)
        if not is_turned:
            parts = [shape((fsdp_count, seq_count, rows_each, columns), bf16)]
        else:
            parts = [shape((seq_count, rows_each, columns), bf16)] * fsdp_count
        return pl.pallas_call(
            functools.partial(weight_kernel, sources, len(arrays), slots, group, fsdp_count, is_turned),
            out_shape=parts,
            grid=(1,),
            in_specs=scalar + in_hbm * len(arrays) + [resident(grad)],
            out_specs=[resident(a) for a in parts],
            scratch_shapes=scratch(held, total, result) + [pltpu.SemaphoreType.DMA((slots,))],
            compiler_params=params,
            cost_estimate=cost(4 * length * hidden_width * columns, 4 * length * hidden_width),
        )(places, *arrays, grad)

    part = shared // seq_count
    arrived = lax.all_to_all(shared_partial.reshape(seq_count, part, length), "seq", 0, 0)
    (head_weights,) = weight_columns(dx, width, False)
    head_sums = lax.psum_scatter(
        head_weights.reshape(hidden_width, width), "fsdp", scatter_dimension=0, tiled=True
    ).reshape(seq_count, rows_each, width)
    arrived, _, w_even = lax.optimization_barrier((arrived, head_weights, w_even))
    sums = [
        shape((part, length), bf16),
        shape((seq_count, token_count + max(part, 16), max(width, token_count)), bf16),
    ]
    shared_columns, packed = pl.pallas_call(
        sum_kernel,
        grid=(1,),
        out_shape=sums,
        in_specs=[resident(arrived), resident(dx)],
        out_specs=[resident(a) for a in sums],
        compiler_params=params,
    )(arrived, dx)

    grad_blocks = lax.all_to_all(packed, "seq", 0, 0)
    shared_weights = weight_columns(shared_columns, part, True)
    shared_arrived = exchange_xor(shared_weights, "fsdp")
    mixed_shape = shape((1, token_count, inner_width), bf16)
    mixer_out = pl.pallas_call(
        spread_kernel,
        grid=(1,),
        out_shape=mixed_shape,
        in_specs=[resident(mixed_blocks)],
        out_specs=resident(mixed_shape),
        compiler_params=params,
    )(after(mixed_blocks, shared_columns))
    w_partner = permute_xor(after(w_columns, arrived), "seq", 1)
    w_odd = permute_xor(w_even, "seq", 1)
    grad_blocks, shared_arrived, mixer_out, w_partner, w_odd = lax.optimization_barrier(
        (grad_blocks, shared_arrived, mixer_out, w_partner, w_odd)
    )

    grad_tokens_shape = shape((1, token_count, hidden_width), bf16)
    by_rows = lambda a: pl.BlockSpec((extent, a.shape[1]), lambda k: (k, 0))
    w_blocks = [w_columns, w_partner, w_even, w_odd]
    grad_tokens = pl.pallas_call(
        tokens_kernel,
        grid=(fsdp_count,),
        out_shape=grad_tokens_shape,
        in_specs=scalar + [resident(grad_blocks)] + [by_rows(a) for a in w_blocks],
        out_specs=pl.BlockSpec((1, token_count, extent), lambda k: (0, 0, k)),
        scratch_shapes=scratch(
            shape((token_count, width + shared), bf16),
            shape((token_count, width), bf16),
            shape((token_count, w_even.shape[1]), bf16),
            shape((token_count, w_odd.shape[1]), bf16),
        ),
        compiler_params=params,
        cost_estimate=cost(
            4 * token_count * hidden_width * (inner_width + shared),
            4 * hidden_width * (inner_width + shared),
        ),
    )(places, grad_blocks, *w_blocks)
    extra = 16
    packed = shape((seq_count, rows_each + extra, width), bf16)
    packed_sums = pl.pallas_call(
        add_kernel,
        grid=(1,),
        out_shape=packed,
        in_specs=[resident(a) for a in [head_sums, *shared_arrived]],
        out_specs=resident(packed),
        compiler_params=params,
    )(head_sums, *shared_arrived)
    owned = lax.all_to_all(packed_sums, "seq", 0, 0)
    finished = shape((rows_each, inner_width + shared), f32)
    grad_weights = pl.pallas_call(
        finish_kernel,
        grid=(1,),
        out_shape=finished,
        in_specs=[resident(owned)],
        out_specs=resident(finished),
        compiler_params=params,
    )(owned)
    return mixer_out, grad_tokens, grad_weights


def solution(mesh):
    return jax.shard_map(
        on_device,
        mesh=mesh,
        in_specs=(
            P("fsdp", "seq", None),
            P("fsdp", None),
            P("fsdp", None, "seq"),
            P("fsdp", "seq", None),
        ),
        out_specs=(P("fsdp", "seq", None), P("fsdp", "seq", None), P(("seq", "fsdp"), None)),
        check_vma=False,
    )
```

time: 223 us -> 183 us (0.82)
  waiting for transfers between devices: 71.5 us -> 30.3 us
  starting transfers between devices: 56.8 us -> 31.1 us
  blocking collectives: 9.51 us -> 24.1 us
  between operations: 0.92 us -> 14 us
  Pallas kernels: 68.1 us -> 72.4 us
  local copies, waits for them, and re-layouts: 11.5 us -> 7.51 us
    ppermute x27 -> x14, starting transfers between devices: 38.4 us -> 11.9 us  [permute_xor(): return lax.ppermute(a, axis, [(i, i ^ mask) for i in range(count)])]
    ppermute x27 -> x14, waiting for transfers between devices: 43.4 us -> 17.8 us  [permute_xor(): return lax.ppermute(a, axis, [(i, i ^ mask) for i in range(count)])]
    all_to_all x1, blocking collectives: 9.51 us -> 24.1 us  [on_device(): log_rates = lax.all_to_all(log_decay[0], 'seq', 0, 1, tiled=True)]
    all_to_all x4, waiting for transfers between devices: 20.5 us -> 8.79 us  [the longest x1 8.63 us: on_device(): lax.all_to_all(shared_partial.reshape(seq_count, part, length), 'seq', 0, 0)]
    all_to_all x1, waiting for transfers between devices: 7.57 us -> 0.01 us  [on_device(): owned = lax.all_to_all(packed_sums, 'seq', 0, 0)]
    pallas_call x3 -> x4, Pallas kernels: 40.7 us -> 45.7 us  [the longest x1 18.9 us: on_device(): pl.pallas_call(functools.partial(forward_kernel, sources, len(arrays), sl...]
    reduce_scatter x0 -> x1, waiting for transfers between devices: none -> 2.98 us  [on_device(): lax.psum_scatter(head_weights.reshape(hidden_width, width), 'fsdp', scatt...]
    another operation x3 -> x0, other arithmetic: 2.96 us -> none  [the longest x2 2.82 us: on_device(): w_stack = jnp.stack(w_own)]
  transfers between devices with their start and end apart: 32 -> 22, of which waited for: 7 -> 7; matrix products, arithmetic and copies ran while one was open for 5% -> 3% of each run, Pallas kernels for 29% -> 38%
where the time goes in v4:
time: 183 us; the launch traced here: 182 us
  Pallas kernels  72.4 us (40%)
  starting transfers between devices  31.1 us (17%)
  waiting for transfers between devices  30.3 us (17%)
  blocking collectives  24.1 us (13%)
  between operations  14 us (8%)
  local copies, waits for them, and re-layouts  7.51 us (4%)
  other arithmetic  2.35 us (1%)
    all_to_all x1, blocking collectives, on_device(): log_rates = lax.all_to_all(log_decay[0], 'seq', 0, 1, tiled=True)  24.1 us
    pallas_call x1, Pallas kernels, on_device(): pl.pallas_call(functools.partial(forward_kernel, sources, len(arrays), sl...  18.9 us
    ppermute x14, waiting for transfers between devices, permute_xor(): return lax.ppermute(a, axis, [(i, i ^ mask) for i in range(count)])  17.8 us
    pallas_call x1, Pallas kernels, on_device(): pl.pallas_call(functools.partial(backward_kernel, heads, head_size), out_...  15.2 us
    pallas_call x2, Pallas kernels, weight_columns(): pl.pallas_call(functools.partial(weight_kernel, sources, len(arrays), slo...  12.4 us
    ppermute x14, starting transfers between devices, permute_xor(): return lax.ppermute(a, axis, [(i, i ^ mask) for i in range(count)])  11.9 us
    pallas_call x1, Pallas kernels, gather_rows(): held, corner, done = lax.optimization_barrier((held, corner, work(beside)))  9.19 us
    all_to_all x1, waiting for transfers between devices, on_device(): lax.all_to_all(shared_partial.reshape(seq_count, part, length), 'seq', 0, 0)  8.63 us
  transfers between devices with their start and end apart: 22, of which 7 were waited for; matrix products, arithmetic and copies ran while one was open for 3% of the time, Pallas kernels for 38%

profile of v4, /device:TPU:0, one launch (start us, length us, event | category | flops | bytes accessed | tf_op | source)
XLA Modules:
  0.0 181.8 jit_solution(10998401242800478580)
XLA Ops:
  7.3 2.3 %constant_dynamic-slice_fusion.2 = (bf16[512,256]{1,0:T(8,128)(2,1)S(1)}, bf16[512,256]{1,0:T(8,128)(2,1)S(1)}, bf16[512,256]{1,0:T(8,128)(2,1)S(1)}, bf16[512,256]{1,0:T(8,128)(2,1)}, bf16[512,256]{1,0:T(8,128)(2,1)}) fusion(bf16[512,2304]{1,0:T(8,128)(2,1)} %param.5, s32[]{:T(128)S(6)} %select_n.13, s32[]{:T(128)S(6)} %select_n.12, s32[]{:T(128)S(6)} %select_n.15, ...), kind=kLoop, calls=%fused_computation.5 | loop fusion | bytes 2621456 | tf_op jit(solution)/shard_map/dynamic_slice | solution.py:474
  10.9 2.6 %collective-permute-start.1 = (bf16[256,2048]{1,0:T(8,128)(2,1)S(1)}, bf16[256,2048]{1,0:T(8,128)(2,1)S(1)}, u32[]{:S(2)}, u32[]{:S(2)}) collective-permute-start(bf16[256,2048]{1,0:T(8,128)(2,1)S(1)} %bitcast.22), channel_id=1, source_target_pairs={{0,8},{4,12},{8,0},{12,4},{16,24},{20,28},{24,16},{28,20},{1,9},{5... | collective-permute-start | bytes 3145736 | tf_op jit(solution)/shard_map/ppermute | solution.py:347
  15.1 24.1 %all_to_all.58 = f32[8,4,256]{2,1,0:T(4,128)} all-to-all(f32[8,4,256]{2,1,0:T(4,128)S(1)} %all_to_all.40), channel_id=1, replica_groups=mesh['seq'=8,'fsdp'=4] {'seq'}, dimensions={0} | all-to-all | bytes 65536 | tf_op jit(solution)/shard_map/all_to_all | solution.py:479
  43.6 9.2 %shard_map.67 = (bf16[2048,256]{1,0:T(8,128)(2,1)}, bf16[2048,256]{1,0:T(8,128)(2,1)}, bf16[2048,256]{1,0:T(8,128)(2,1)}, bf16[2048,256]{1,0:T(8,128)(2,1)}, f32...) custom-call(f32[4,2048]{1,0:T(4,128)} %bitcast.30), custom_call_target="tpu_custom_call" | custom-call | bytes 62914560 | tf_op jit(solution)/shard_map/pallas_call | solution.py:363
  52.8 3.0 %collective-permute-done.5.refs_6_ = bf16[128,2048]{1,0:T(8,128)(2,1)} collective-permute-done((bf16[128,2048]{1,0:T(8,128)(2,1)}, bf16[128,2048]{1,0:T(8,128)(2,1)}, u32[]{:S(2)}, u32[]{:S(2)}) %collective-permute-start.5) | collective-permute-done | bytes 524320 | tf_op jit(solution)/shard_map/ppermute | solution.py:347
  59.8 2.3 %copy.12 = bf16[32,8,8,256]{3,2,0,1:T(8,128)(2,1)} copy(bf16[32,8,8,256]{3,2,1,0:T(8,128)(2,1)} %bitcast.24) | data formatting | bytes 2097152 | tf_op jit(solution)/shard_map/all_to_all | solution.py:517
  62.1 3.6 %all-to-all-start.1 = ((bf16[256,8,256]{2,0,1:T(8,128)(2,1)}), bf16[256,8,256]{2,0,1:T(8,128)(2,1)S(1)}, u32[]{:S(2)}, u32[]{:S(2)}) async-start(bf16[256,8,256]{2,0,1:T(8,128)(2,1)} %bitcast.17), calls=%async_computation.1 | async-start | bytes 2097152 | tf_op jit(solution)/shard_map/all_to_all | solution.py:517
  65.7 18.9 %shard_map.68 = (bf16[2048,256]{1,0:T(8,128)(2,1)}, bf16[2048,128]{1,0:T(8,128)(2,1)}, bf16[2048,128]{1,0:T(8,128)(2,1)}, bf16[2048,256]{1,0:T(8,128)(2,1)}, bf1...) custom-call(s32[2]{0:T(128)} %pad_add_fusion.place_ref.places_ref, ...), custom_call_target="tpu_custom_call" | custom-call | flops 19327352832 | bytes 16777216 | tf_op jit(solution)/shard_map/pallas_call | solution.py:520
  84.7 4.2 %all-to-all-start.2 = ((bf16[8,256,256]{2,1,0:T(8,128)(2,1)}), bf16[8,256,256]{2,1,0:T(8,128)(2,1)S(1)}, u32[]{:S(2)}, u32[]{:S(2)}) async-start(bf16[8,256,256]{2,1,0:T(8,128)(2,1)} %bitcast.28), calls=%async_computation.2 | async-start | bytes 2097152 | tf_op jit(solution)/shard_map/all_to_all | solution.py:541
  88.9 15.2 %shard_map.69 = (bf16[2048,256]{1,0:T(8,128)(2,1)}, bf16[256,2048]{1,0:T(8,128)(2,1)}) custom-call(bf16[2048,256]{1,0:T(8,128)(2,1)} %bitcast.26, bf16[2048,256]{1,0:T(8,128)(2,1)} %get-tuple-element.123.refs_1_, bf16[2048,256]{1,0:T(8,128)(2,1)} %get-tuple-element.124.refs_2_, bf16[2048,128]{1,0:T(8,128)(2,1)} %get-tuple-element.125.refs_3_, ...), custom_call_target="tpu_custom_call" | custom-call | flops 16106127360 | bytes 20971520 | tf_op jit(solution)/shard_map/pallas_call | solution.py:547
  104.3 4.1 %all-to-all-start.3 = ((bf16[8,32,2048]{2,1,0:T(8,128)(2,1)}), bf16[8,32,2048]{2,1,0:T(8,128)(2,1)S(1)}, u32[]{:S(2)}, u32[]{:S(2)}) async-start(bf16[8,32,2048]{2,1,0:T(8,128)(2,1)} %bitcast.27), calls=%async_computation.3 | async-start | bytes 2097152 | tf_op jit(solution)/shard_map/all_to_all | solution.py:580
  108.6 6.5 %shard_map.70 = bf16[4,8,64,256]{3,2,1,0:T(8,128)(2,1)} custom-call(s32[2]{0:T(128)} %pad_add_fusion.place_ref.places_ref, bf16[256,2048]{1,0:T(8,128)(2,1)} %bitcast.19, bf16[256,2048]{1,0:T(8,128)(2,1)} %collective-permute-done.refs_1_, bf16[256,2048]{1,0:T(8,128)(2,1)} %copy-done.2, bf16[256,2048]{1,0:T(8,128)(2,1)} %copy-done.7, ...), custom_call_target="tpu_custom_call" | custom-call | flops 4294967296 | bytes 16777216 | tf_op jit(solution)/shard_map/pallas_call | solution.py:568
  115.2 8.6 %all-to-all-done.3.parts_ref = bf16[8,32,2048]{2,1,0:T(8,128)(2,1)S(1)} async-done(((bf16[8,32,2048]{2,1,0:T(8,128)(2,1)}), bf16[8,32,2048]{2,1,0:T(8,128)(2,1)S(1)}, u32[]{:S(2)}, u32[]{:S(2)}) %all-to-all-start.3) | async-done | bytes 1048608 | tf_op jit(solution)/shard_map/all_to_all | solution.py:580
  124.8 2.8 %shard_map.71 = (bf16[32,2048]{1,0:T(8,128)(2,1)}, bf16[8,288,256]{2,1,0:T(8,128)(2,1)}) custom-call(bf16[8,32,2048]{2,1,0:T(8,128)(2,1)} %copy-done.1, bf16[2048,256]{1,0:T(8,128)(2,1)} %get-tuple-element.134.refs_10_.dx_ref), custom_call_target="tpu_custom_call" | custom-call | tf_op jit(solution)/shard_map/pallas_call | solution.py:590
  127.6 3.6 %all-to-all-start.4 = ((bf16[8,288,256]{2,1,0:T(8,128)(2,1)}), bf16[8,288,256]{2,1,0:T(8,128)(2,1)S(1)}, u32[]{:S(2)}, u32[]{:S(2)}) async-start(bf16[8,288,256]{2,1,0:T(8,128)(2,1)} %get-tuple-element.137), calls=%async_computation.4 | async-start | bytes 2359296 | tf_op jit(solution)/shard_map/all_to_all | solution.py:599
  131.2 5.8 %shard_map.72 = (bf16[8,64,32]{2,1,0:T(8,128)(2,1)}, bf16[8,64,32]{2,1,0:T(8,128)(2,1)}, bf16[8,64,32]{2,1,0:T(8,128)(2,1)}, bf16[8,64,32]{2,1,0:T(8,128)(2,1)}) custom-call(s32[2]{0:T(128)} %pad_add_fusion.place_ref.places_ref, bf16[256,2048]{1,0:T(8,128)(2,1)} %bitcast.20, bf16[256,2048]{1,0:T(8,128)(2,1)} %collective-permute-done.refs_1_, ...), custom_call_target="tpu_custom_call" | custom-call | flops 536870912 | bytes 16777216 | tf_op jit(solution)/shard_map/pallas_call | solution.py:568
  137.0 1.8 collective-permute-start.10
  140.6 2.3 %shard_map.73 = bf16[1,256,2048]{2,1,0:T(8,128)(2,1)} custom-call(bf16[8,256,256]{2,1,0:T(8,128)(2,1)} %copy-done), custom_call_target="tpu_custom_call" | custom-call | tf_op jit(solution)/shard_map/pallas_call | solution.py:603
  142.9 13.6 %collective-permute-done.10.refs_3_ = bf16[8,64,32]{2,1,0:T(8,128)(2,1)S(1)} collective-permute-done((bf16[8,64,32]{2,1,0:T(8,128)(2,1)}, bf16[8,64,32]{2,1,0:T(8,128)(2,1)S(1)}, u32[]{:S(2)}, u32[]{:S(2)}) %collective-permute-start.10) | collective-permute-done | bytes 32800 | tf_op jit(solution)/shard_map/ppermute | solution.py:347
  156.5 3.0 %reduce-scatter.2.cloned.1.call-done = bf16[512,256]{1,0:T(8,128)(2,1)} async-done(((bf16[2048,256]{1,0:T(8,128)(2,1)}), bf16[512,256]{1,0:T(8,128)(2,1)}) %reduce-scatter.2.cloned.1.call-update) | async-done | bytes 262160 | tf_op jit(solution)/shard_map/reduce_scatter | solution.py:582
  159.5 2.0 %shard_map.75 = bf16[8,80,256]{2,1,0:T(8,128)(2,1)} custom-call(bf16[8,64,256]{2,1,0:T(8,128)(2,1)} %bitcast.29, bf16[8,64,32]{2,1,0:T(8,128)(2,1)} %get-tuple-element.151.refs_1_, bf16[8,64,32]{2,1,0:T(8,128)(2,1)} %copy-done.13, bf16[8,64,32]{2,1,0:T(8,128)(2,1)} %copy-done.11, bf16[8,64,32]{2,1,0:T(8,128)(2,1)} %copy-done.12), custom_call_target="tpu_custom_call" | custom-call | tf_op jit(solution)/shard_map/pallas_call | solution.py:640
  161.5 3.5 %all-to-all-start.5 = ((bf16[8,80,256]{2,1,0:T(8,128)(2,1)}), bf16[8,80,256]{2,1,0:T(8,128)(2,1)S(1)}, u32[]{:S(2)}, u32[]{:S(2)}) async-start(bf16[8,80,256]{2,1,0:T(8,128)(2,1)} %shard_map.75), calls=%async_computation.6 | async-start | bytes 655360 | tf_op jit(solution)/shard_map/all_to_all | solution.py:648
  165.0 7.7 %shard_map.74 = bf16[1,256,2048]{2,1,0:T(8,128)(2,1)} custom-call(s32[2]{0:T(128)} %pad_add_fusion.place_ref.places_ref, bf16[8,288,256]{2,1,0:T(8,128)(2,1)} %copy-done.5, bf16[2048,512]{1,0:T(8,128)(2,1)} %all-gather.3.cloned.1.call-done.refs_10_.own_ref, bf16[2048,512]{1,0:T(8,128)(2,1)} %collective-permute-done.12.partner_ref, ...), custom_call_target="tpu_custom_call" | custom-call | flops 4831838208 | bytes 18874368 | tf_op jit(solution)/shard_map/pallas_call | solution.py:620
  173.4 1.9 %shard_map.76 = f32[64,2304]{1,0:T(8,128)} custom-call(bf16[8,80,256]{2,1,0:T(8,128)(2,1)} %copy-done.4), custom_call_target="tpu_custom_call" | custom-call | tf_op jit(solution)/shard_map/pallas_call | solution.py:650
  (72 shorter events, 15.3 us)
Async XLA Ops:
  7.2 52.0 %all-gather.3.cloned.1.call-start = ((), (), s32[]{:S(2)}) async-start(), calls=%async_computation.7 | async-start | bytes 2621440 | tf_op jit(solution)/shard_map/all_gather | solution.py:476
  10.4 113.4 %all-gather.5.cloned.1.call-start = ((), (), s32[]{:S(2)}) async-start(), calls=%async_computation.8 | async-start | bytes 3932160 | tf_op jit(solution)/shard_map/all_gather | solution.py:514
  10.4 28.8 %collective-permute-start = (bf16[256,2048]{1,0:T(8,128)(2,1)S(1)}, bf16[256,2048]{1,0:T(8,128)(2,1)}, u32[]{:S(2)}, u32[]{:S(2)}) collective-permute-start(bf16[256,2048]{1,0:T(8,128)(2,1)S(1)} %bitcast.21), channel_id=1, source_target_pairs={{0,4},{4,0},{8,12},{12,8},{16,20},{20,16},{24,28},{28,24},{1,5},{5... | collective-permute-start | bytes 3145736 | tf_op jit(solution)/shard_map/ppermute | solution.py:347
  10.9 28.3 %collective-permute-start.1 = (bf16[256,2048]{1,0:T(8,128)(2,1)S(1)}, bf16[256,2048]{1,0:T(8,128)(2,1)S(1)}, u32[]{:S(2)}, u32[]{:S(2)}) collective-permute-start(bf16[256,2048]{1,0:T(8,128)(2,1)S(1)} %bitcast.22), channel_id=1, source_target_pairs={{0,8},{4,12},{8,0},{12,4},{16,24},{20,28},{24,16},{28,20},{1,9},{5... | collective-permute-start | bytes 3145736 | tf_op jit(solution)/shard_map/ppermute | solution.py:347
  13.5 25.7 %collective-permute-start.2 = (bf16[256,2048]{1,0:T(8,128)(2,1)S(1)}, bf16[256,2048]{1,0:T(8,128)(2,1)S(1)}, u32[]{:S(2)}, u32[]{:S(2)}) collective-permute-start(bf16[256,2048]{1,0:T(8,128)(2,1)S(1)} %bitcast.23), channel_id=1, source_target_pairs={{0,16},{4,20},{8,24},{12,28},{16,0},{20,4},{24,8},{28,12},{1,17},{... | collective-permute-start | bytes 3145736 | tf_op jit(solution)/shard_map/ppermute | solution.py:347
  15.0 42.5 %copy-start.9 = (bf16[512,256]{1,0:T(8,128)(2,1)S(1)}, bf16[512,256]{1,0:T(8,128)(2,1)}, u32[]{:S(2)}) copy-start(bf16[512,256]{1,0:T(8,128)(2,1)} %get-tuple-element.158) | copy-start | bytes 786436
  15.1 42.5 %copy-start.10 = (bf16[512,256]{1,0:T(8,128)(2,1)S(1)}, bf16[512,256]{1,0:T(8,128)(2,1)}, u32[]{:S(2)}) copy-start(bf16[512,256]{1,0:T(8,128)(2,1)} %get-tuple-element.159) | copy-start | bytes 786436
  39.2 17.7 %collective-permute-start.3 = (bf16[256,2048]{1,0:T(8,128)(2,1)S(1)}, bf16[256,2048]{1,0:T(8,128)(2,1)S(1)}, u32[]{:S(2)}, u32[]{:S(2)}) collective-permute-start(bf16[256,2048]{1,0:T(8,128)(2,1)S(1)} %collective-permute-done.1.refs_2_), channel_id=1, source_target_pairs={{0,4},{4,0},{8,12},{12,8},{16,20},{20,16},{24,28},{28,24},{1,5},{5... | collective-permute-start | bytes 3145736 | tf_op jit(solution)/shard_map/ppermute | solution.py:347
  39.4 17.6 %collective-permute-start.4 = (bf16[256,2048]{1,0:T(8,128)(2,1)S(1)}, bf16[256,2048]{1,0:T(8,128)(2,1)}, u32[]{:S(2)}, u32[]{:S(2)}) collective-permute-start(bf16[256,2048]{1,0:T(8,128)(2,1)S(1)} %collective-permute-done.2.refs_4_), channel_id=1, source_target_pairs={{0,4},{4,0},{8,12},{12,8},{16,20},{20,16},{24,28},{28,24},{1,5},{5... | collective-permute-start | bytes 3145736 | tf_op jit(solution)/shard_map/ppermute | solution.py:347
  41.5 14.2 %collective-permute-start.5 = (bf16[128,2048]{1,0:T(8,128)(2,1)}, bf16[128,2048]{1,0:T(8,128)(2,1)}, u32[]{:S(2)}, u32[]{:S(2)}) collective-permute-start(bf16[128,2048]{1,0:T(8,128)(2,1)} %slice.9), channel_id=1, source_target_pairs={{0,16},{4,20},{8,24},{12,28},{16,0},{20,4},{24,8},{28,12},{1,17},{... | collective-permute-start | bytes 1572872 | tf_op jit(solution)/shard_map/ppermute | solution.py:347
  43.0 13.9 %collective-permute-start.6 = (bf16[128,2048]{1,0:T(8,128)(2,1)}, bf16[128,2048]{1,0:T(8,128)(2,1)}, u32[]{:S(2)}, u32[]{:S(2)}) collective-permute-start(bf16[128,2048]{1,0:T(8,128)(2,1)} %slice.10), channel_id=1, source_target_pairs={{0,8},{4,12},{8,0},{12,4},{16,24},{20,28},{24,16},{28,20},{1,9},{5... | collective-permute-start | bytes 1572872 | tf_op jit(solution)/shard_map/ppermute | solution.py:347
  57.0 8.7 %collective-permute-start.7 = (bf16[128,2048]{1,0:T(8,128)(2,1)}, bf16[128,2048]{1,0:T(8,128)(2,1)}, u32[]{:S(2)}, u32[]{:S(2)}) collective-permute-start(bf16[128,2048]{1,0:T(8,128)(2,1)} %collective-permute-done.5.refs_6_), channel_id=1, source_target_pairs={{0,4},{4,0},{8,12},{12,8},{16,20},{20,16},{24,28},{28,24},{1,5},{5... | collective-permute-start | bytes 1572872 | tf_op jit(solution)/shard_map/ppermute | solution.py:347
  57.1 8.7 %collective-permute-start.8 = (bf16[128,2048]{1,0:T(8,128)(2,1)}, bf16[128,2048]{1,0:T(8,128)(2,1)}, u32[]{:S(2)}, u32[]{:S(2)}) collective-permute-start(bf16[128,2048]{1,0:T(8,128)(2,1)} %collective-permute-done.6.refs_7_), channel_id=1, source_target_pairs={{0,4},{4,0},{8,12},{12,8},{16,20},{20,16},{24,28},{28,24},{1,5},{5... | collective-permute-start | bytes 1572872 | tf_op jit(solution)/shard_map/ppermute | solution.py:347
  62.1 22.6 %all-to-all-start.1 = ((bf16[256,8,256]{2,0,1:T(8,128)(2,1)}), bf16[256,8,256]{2,0,1:T(8,128)(2,1)S(1)}, u32[]{:S(2)}, u32[]{:S(2)}) async-start(bf16[256,8,256]{2,0,1:T(8,128)(2,1)} %bitcast.17), calls=%async_computation.1 | async-start | bytes 2097152 | tf_op jit(solution)/shard_map/all_to_all | solution.py:517
  84.7 19.6 %all-to-all-start.2 = ((bf16[8,256,256]{2,1,0:T(8,128)(2,1)}), bf16[8,256,256]{2,1,0:T(8,128)(2,1)S(1)}, u32[]{:S(2)}, u32[]{:S(2)}) async-start(bf16[8,256,256]{2,1,0:T(8,128)(2,1)} %bitcast.28), calls=%async_computation.2 | async-start | bytes 2097152 | tf_op jit(solution)/shard_map/all_to_all | solution.py:541
  104.3 19.5 %all-to-all-start.3 = ((bf16[8,32,2048]{2,1,0:T(8,128)(2,1)}), bf16[8,32,2048]{2,1,0:T(8,128)(2,1)S(1)}, u32[]{:S(2)}, u32[]{:S(2)}) async-start(bf16[8,32,2048]{2,1,0:T(8,128)(2,1)} %bitcast.27), calls=%async_computation.3 | async-start | bytes 2097152 | tf_op jit(solution)/shard_map/all_to_all | solution.py:580
  108.4 51.1 %reduce-scatter.2.cloned.1.call-start = ((), (), s32[]{:S(2)}) async-start(), calls=%async_computation.9 | async-start | bytes 1310720 | tf_op jit(solution)/shard_map/reduce_scatter | solution.py:582
  123.8 32.7 %collective-permute-start.13 = (bf16[2048,768]{1,0:T(8,128)(2,1)}, bf16[2048,768]{1,0:T(8,128)(2,1)}, u32[]{:S(2)}, u32[]{:S(2)}) collective-permute-start(bf16[2048,768]{1,0:T(8,128)(2,1)} %all-gather.5.cloned.1.call-done.even_ref), channel_id=1, source_target_pairs={{0,4},{4,0},{8,12},{12,8},{16,20},{20,16},{24,28},{28,24},{1,5},{5... | collective-permute-start | bytes 9437192 | tf_op jit(solution)/shard_map/ppermute | solution.py:347
  123.8 32.7 %collective-permute-start.12 = (bf16[2048,512]{1,0:T(8,128)(2,1)}, bf16[2048,512]{1,0:T(8,128)(2,1)}, u32[]{:S(2)}, u32[]{:S(2)}) collective-permute-start(bf16[2048,512]{1,0:T(8,128)(2,1)} %all-gather.3.cloned.1.call-done.refs_10_.own_ref), channel_id=1, source_target_pairs={{0,4},{4,0},{8,12},{12,8},{16,20},{20,16},{24,28},{28,24},{1,5},{5... | collective-permute-start | bytes 6291464 | tf_op jit(solution)/shard_map/ppermute | solution.py:347
  127.6 28.9 %all-to-all-start.4 = ((bf16[8,288,256]{2,1,0:T(8,128)(2,1)}), bf16[8,288,256]{2,1,0:T(8,128)(2,1)S(1)}, u32[]{:S(2)}, u32[]{:S(2)}) async-start(bf16[8,288,256]{2,1,0:T(8,128)(2,1)} %get-tuple-element.137), calls=%async_computation.4 | async-start | bytes 2359296 | tf_op jit(solution)/shard_map/all_to_all | solution.py:599
  137.0 19.4 %collective-permute-start.10 = (bf16[8,64,32]{2,1,0:T(8,128)(2,1)}, bf16[8,64,32]{2,1,0:T(8,128)(2,1)S(1)}, u32[]{:S(2)}, u32[]{:S(2)}) collective-permute-start(bf16[8,64,32]{2,1,0:T(8,128)(2,1)} %get-tuple-element.141), channel_id=1, source_target_pairs={{0,2},{1,3},{2,0},{3,1},{4,6},{5,7},{6,4},{7,5},{8,10},{9,11},{10,... | collective-permute-start | bytes 98312 | tf_op jit(solution)/shard_map/ppermute | solution.py:347
  138.8 17.7 %collective-permute-start.11 = (bf16[8,64,32]{2,1,0:T(8,128)(2,1)}, bf16[8,64,32]{2,1,0:T(8,128)(2,1)S(1)}, u32[]{:S(2)}, u32[]{:S(2)}) collective-permute-start(bf16[8,64,32]{2,1,0:T(8,128)(2,1)} %get-tuple-element.142), channel_id=1, source_target_pairs={{0,3},{1,2},{2,1},{3,0},{4,7},{5,6},{6,5},{7,4},{8,11},{9,10},{10,... | collective-permute-start | bytes 98312 | tf_op jit(solution)/shard_map/ppermute | solution.py:347
  140.1 16.3 %collective-permute-start.9 = (bf16[8,64,32]{2,1,0:T(8,128)(2,1)}, bf16[8,64,32]{2,1,0:T(8,128)(2,1)S(1)}, u32[]{:S(2)}, u32[]{:S(2)}) collective-permute-start(bf16[8,64,32]{2,1,0:T(8,128)(2,1)} %get-tuple-element.140), channel_id=1, source_target_pairs={{0,1},{1,0},{2,3},{3,2},{4,5},{5,4},{6,7},{7,6},{8,9},{9,8},{10,11... | collective-permute-start | bytes 98312 | tf_op jit(solution)/shard_map/ppermute | solution.py:347
  161.5 11.2 %all-to-all-start.5 = ((bf16[8,80,256]{2,1,0:T(8,128)(2,1)}), bf16[8,80,256]{2,1,0:T(8,128)(2,1)S(1)}, u32[]{:S(2)}, u32[]{:S(2)}) async-start(bf16[8,80,256]{2,1,0:T(8,128)(2,1)} %shard_map.75), calls=%async_computation.6 | async-start | bytes 655360 | tf_op jit(solution)/shard_map/all_to_all | solution.py:648
  (13 other events, 90.5 us)
Sparse Core Ops, SparseCore 0:
  10.5 48.6 all-gather.2
  60.7 62.2 all-gather.4
  125.3 34.1 reduce-scatter.1

commit v5 on v4

--- a/solution.py
+++ b/solution.py
@@ -120,7 +120,7 @@
         carry[...] = dt_ref[k] * carry[...] + term
         return 0
 
-    lax.fori_loop(0, chunks, reverse_states, 0, unroll=2)
+    lax.fori_loop(0, chunks, reverse_states, 0, unroll=8)
     out_stores[6].start()
     carry[...] = jnp.zeros_like(carry)
 
@@ -140,7 +140,7 @@
         carry[...] = dt_ref[k] * carry[...] + dot_tn(b, x * te_ref[rows, :])
         return 0
 
-    lax.fori_loop(0, chunks, outputs, 0, unroll=2)
+    lax.fori_loop(0, chunks, outputs, 0, unroll=8)
     for store in out_stores[3:6]:
         store.start()
     for store in out_stores:
@@ -177,7 +177,7 @@
         carry[...] = dt_ref[k] * carry[...] + dot_tn(c_ref[rows, :], dy * en_ref[rows, :])
         return 0
 
-    lax.fori_loop(0, chunks, end_adjoints, 0, unroll=2)
+    lax.fori_loop(0, chunks, end_adjoints, 0, unroll=8)
     carry[...] = jnp.zeros_like(carry)
     for load in in_loads[6:]:
         load.wait()
@@ -205,7 +205,7 @@
         carry[...] = dt_ref[k] * carry[...] + dot_tn(c, dy_lv)
         return 0
 
-    lax.fori_loop(0, chunks, gradients, 0, unroll=2)
+    lax.fori_loop(0, chunks, gradients, 0, unroll=8)
     out_stores = [
         pltpu.make_async_copy(source, target, stores.at[n])
         for n, (source, target) in enumerate(zip((dx_ref, shared_ref), out_hbm))
@@ -232,26 +232,30 @@
         packed_ref[n, tokens : tokens + part, :tokens] = total[:, block]
 
 
-def tokens_kernel(place_ref, packed_ref, own_ref, partner_ref, even_ref, odd_ref, out_ref, *lhs):
-    own_lhs, partner_lhs, even_lhs, odd_lhs = lhs
+def tokens_kernel(where, place_ref, packed_ref, own_ref, partner_ref, *refs):
+    columns, (out_ref, lhs_ref, own_lhs) = refs[:-3], refs[-3:]
     count = packed_ref.shape[0]
-    tokens, width = partner_lhs.shape
-    part = (own_lhs.shape[1] - width) // count
+    tokens, first = own_lhs.shape
+    width = lhs_ref.shape[1] // count
+    part = (first - width) // count
 
     @pl.when(pl.program_id(0) == 0)
     def _():
         for r in range(count):
-            target = (even_lhs, odd_lhs)[r % 2] if r > 1 else (own_lhs, partner_lhs)[r]
-            start = (r // 2 - 1) * width if r > 1 else 0
-            source = lax.bitwise_xor(place_ref[0], r)
-            target[:, start : start + width] = packed_ref[source, :tokens, :width]
+            source = packed_ref[lax.bitwise_xor(place_ref[0], r), :tokens, :width]
+            lhs_ref[:, r * width : (r + 1) * width] = source
+        own_lhs[:, :width] = lhs_ref[:, :width]
         turned = [packed_ref[n, tokens : tokens + part, :tokens] for n in range(count)]
         own_lhs[:, width:] = jnp.concatenate(turned, axis=0).T
 
     result = dot_nt(own_lhs[...], own_ref[...])
-    result = result + dot_nt(partner_lhs[...], partner_ref[:, :width])
-    result = result + dot_nt(even_lhs[...], even_ref[...])
-    result = result + dot_nt(odd_lhs[...], odd_ref[...])
+    result = result + dot_nt(lhs_ref[:, width : 2 * width], partner_ref[:, :width])
+    for r in range(2, count):
+        column = r * width
+        for array, start, extent in where[r]:
+            block = columns[array][:, start : start + extent]
+            result = result + dot_nt(lhs_ref[:, column : column + extent], block)
+            column += extent
     out_ref[0] = result.astype(bf16)
 
 
@@ -269,11 +273,9 @@
     for ref in shared_refs[1:]:
         total = total + ref[...].astype(f32)
     total = total.astype(bf16)
-    extra = out_ref.shape[1] - rows
-    part = total.shape[2]
-    out_ref[:, rows:, :] = jnp.zeros((out_ref.shape[0], extra, out_ref.shape[2]), bf16)
-    for q in range(rows // extra):
-        out_ref[:, rows:, q * part : (q + 1) * part] = total[:, q * extra : (q + 1) * extra]
+    if out_ref.shape[2] > total.shape[2]:
+        out_ref[:, rows:, :] = jnp.zeros_like(out_ref[:, rows:, :])
+    out_ref[:, rows:, : total.shape[2]] = total
 
 
 def weight_kernel(sources, arrays, slots, group, parts, is_turned, places_ref, *refs):
@@ -310,15 +312,19 @@
         for i in range(first, first + group):
             if i + slots < pieces:
                 fetch(i + slots).start()
-    each = out_refs[0].shape[-2]
+    columns = result.shape[1]
+    each = out_refs[0].shape[-2] * out_refs[0].shape[-1] // columns
     count = hidden // (parts * each)
     for k in range(parts):
         for j in range(count):
             if len(out_refs) == 1:
                 out_refs[0][k, j] = result[(j * parts + k) * each : (j * parts + k + 1) * each, :]
-            else:
-                mine = (j * parts + lax.bitwise_xor(places_ref[1], k)) * each
-                out_refs[k][j] = result[pl.ds(pl.multiple_of(mine, each), each), :]
+                continue
+            mine = (j * parts + lax.bitwise_xor(places_ref[1], k)) * each
+            rows = out_refs[k].shape[1]
+            for q in range(each // rows):
+                source = pl.ds(pl.multiple_of(mine + q * rows, rows), rows)
+                out_refs[k][j, :, q * columns : (q + 1) * columns] = result[source, :]
 
 
 def finish_kernel(packed_ref, out_ref):
@@ -347,7 +353,7 @@
     return lax.ppermute(a, axis, [(i, i ^ mask) for i in range(count)])
 
 
-def gather_rows(rows, axis, beside, work, last):
+def gather_rows(rows, axis, beside, work):
     count = lax.axis_size(axis)
     bits = count.bit_length() - 1
     half = rows.shape[0] // 2
@@ -359,13 +365,12 @@
             permute_xor(held[2][:half], axis, 4),
             permute_xor(held[4][half:], axis, 2),
         ]
-        last = after(last, held[3])
-        held, corner, done = lax.optimization_barrier((held, corner, work(beside)))
+        held, corner, done = lax.optimization_barrier((held, corner, work(*beside)))
         held = {r: [a] for r, a in held.items()}
         held[0], held[6] = [rows], corner
         held[7] = [permute_xor(a, axis, 1) for a in corner]
     else:
-        done = work(beside)
+        done = work(*beside)
         upper = list(range(1, bits))
         orders = (upper + [0], upper[1:] + upper[:1] + [0])
         both = ({0: rows[:half]}, {0: rows[half:]})
@@ -382,7 +387,7 @@
             if part == 0 or not whole_block:
                 arrays.append(held[r][part])
             sources.append((len(arrays) - 1, half * part if whole_block else 0))
-    return arrays, tuple(sources), done, last
+    return arrays, tuple(sources), done
 
 
 def exchange_xor(pieces, axis):
@@ -495,8 +500,17 @@
         compiler_params=params,
         cost_estimate=cost(0, 120 * length * width),
     )
-    arrays, sources, tables, upstream = gather_rows(
-        local_tokens, "seq", log_rates, make_tables, upstream
+    neighbours = [r for r in range(2, seq_count, 2) if r & (r - 1) == 0]
+    others = [r for r in range(2, seq_count, 2) if r & (r - 1)]
+    first_part = width // 2
+    rest = [columns(r) for r in others] + [columns(r)[:, :first_part] for r in neighbours]
+
+    def second_step(log_rates, upstream, rest):
+        blocks = upstream.reshape(token_count, seq_count, width).transpose(1, 0, 2)
+        return make_tables(log_rates), blocks, jnp.concatenate(rest, axis=1)
+
+    arrays, sources, (tables, upstream, rest) = gather_rows(
+        local_tokens, "seq", (log_rates, upstream, rest), second_step
     )
     to_end, from_start, enter, leave, chunk_decay, decays, turned = tables
 
@@ -510,11 +524,10 @@
     mean = shape((width, width), bf16)
     carry = shape((state_size, width), f32)
 
-    rest = jnp.concatenate([columns(r) for r in range(2, seq_count, 2)], axis=1)
-    w_even = lax.all_gather(after(rest, w_columns), "fsdp", axis=0, tiled=True)
+    w_even = lax.all_gather(rest, "fsdp", axis=0, tiled=True)
 
     *arrays, w_columns = lax.optimization_barrier((*arrays, w_columns))
-    g = lax.all_to_all(upstream, "seq", 1, 0, tiled=True)
+    g = lax.all_to_all(upstream, "seq", 0, 0).reshape(length, width)
     operands = (w_columns, decays, to_end, from_start, enter, leave, chunk_decay)
     kept = [by_position, state_rows, state_rows, by_position, by_position, by_state, by_state]
     forward = pl.pallas_call(
@@ -554,9 +567,11 @@
         compiler_params=params,
         cost_estimate=cost(240 * length * width * CHUNK, 40 * length * width),
     )(*operands)
-    (dx, shared_partial), mixed_blocks = lax.optimization_barrier((backward, mixed_blocks))
+    backward, mixed_blocks = lax.optimization_barrier((backward, mixed_blocks))
+    dx, shared_partial = backward
 
     rows_each = hidden_width // (seq_count * fsdp_count)
+    extra = 16
 
     def weight_columns(grad, columns, is_turned):
         total = shape((columns, hidden_width), f32)
@@ -564,7 +579,7 @@
         if not is_turned:
             parts = [shape((fsdp_count, seq_count, rows_each, columns), bf16)]
         else:
-            parts = [shape((seq_count, rows_each, columns), bf16)] * fsdp_count
+            parts = [shape((seq_count, extra, columns * rows_each // extra), bf16)] * fsdp_count
         return pl.pallas_call(
             functools.partial(weight_kernel, sources, len(arrays), slots, group, fsdp_count, is_turned),
             out_shape=parts,
@@ -582,7 +597,9 @@
     head_sums = lax.psum_scatter(
         head_weights.reshape(hidden_width, width), "fsdp", scatter_dimension=0, tiled=True
     ).reshape(seq_count, rows_each, width)
-    arrived, _, w_even = lax.optimization_barrier((arrived, head_weights, w_even))
+    second_part = after(w_columns, head_weights)[:, first_part:width]
+    w_across = [permute_xor(second_part, "seq", r) for r in neighbours]
+    arrived, second_part, w_even = lax.optimization_barrier((arrived, second_part, w_even))
     sums = [
         shape((part, length), bf16),
         shape((seq_count, token_count + max(part, 16), max(width, token_count)), bf16),
@@ -609,25 +626,31 @@
         compiler_params=params,
     )(after(mixed_blocks, shared_columns))
     w_partner = permute_xor(after(w_columns, arrived), "seq", 1)
-    w_odd = permute_xor(w_even, "seq", 1)
+    w_even = [w_even, *w_across]
+    w_odd = [permute_xor(a, "seq", 1) for a in w_even]
     grad_blocks, shared_arrived, mixer_out, w_partner, w_odd = lax.optimization_barrier(
-        (grad_blocks, shared_arrived, mixer_out, w_partner, w_odd)
-    )
+        (grad_blocks, shared_arrived, mixer_out, w_partner, w_odd, head_sums)
+    )[:-1]
 
     grad_tokens_shape = shape((1, token_count, hidden_width), bf16)
     by_rows = lambda a: pl.BlockSpec((extent, a.shape[1]), lambda k: (k, 0))
-    w_blocks = [w_columns, w_partner, w_even, w_odd]
+    where = {}
+    for n, r in enumerate(others):
+        where[r] = [(0, n * width, width)]
+    for n, r in enumerate(neighbours):
+        start = len(others) * width + n * first_part
+        where[r] = [(0, start, first_part), (1 + n, 0, width - first_part)]
+    for r in range(2, seq_count, 2):
+        where[r + 1] = [(array + len(w_even), start, extent) for array, start, extent in where[r]]
+    w_blocks = [w_columns, w_partner, *w_even, *w_odd]
     grad_tokens = pl.pallas_call(
-        tokens_kernel,
+        functools.partial(tokens_kernel, where),
         grid=(fsdp_count,),
         out_shape=grad_tokens_shape,
         in_specs=scalar + [resident(grad_blocks)] + [by_rows(a) for a in w_blocks],
         out_specs=pl.BlockSpec((1, token_count, extent), lambda k: (0, 0, k)),
         scratch_shapes=scratch(
-            shape((token_count, width + shared), bf16),
-            shape((token_count, width), bf16),
-            shape((token_count, w_even.shape[1]), bf16),
-            shape((token_count, w_odd.shape[1]), bf16),
+            shape((token_count, inner_width), bf16), shape((token_count, width + shared), bf16)
         ),
         compiler_params=params,
         cost_estimate=cost(
@@ -635,7 +658,6 @@
             4 * hidden_width * (inner_width + shared),
         ),
     )(places, grad_blocks, *w_blocks)
-    extra = 16
     packed = shape((seq_count, rows_each + extra, width), bf16)
     packed_sums = pl.pallas_call(
         add_kernel,

time: 183 us -> 175 us (0.956)
  blocking collectives: 24.1 us -> 0 us
  waiting for transfers between devices: 30.3 us -> 39.1 us
  starting transfers between devices: 31.1 us -> 39 us
  Pallas kernels: 72.4 us -> 68.3 us
  local copies, waits for them, and re-layouts: 7.51 us -> 10.8 us
    all_to_all x1 -> x0, blocking collectives: 24.1 us -> none  [on_device(): log_rates = lax.all_to_all(log_decay[0], 'seq', 0, 1, tiled=True)]
    all_to_all x1 -> x2, waiting for transfers between devices: 0.01 us -> 17.9 us  [the longest x1 17.9 us: on_device(): log_rates = lax.all_to_all(log_decay[0], 'seq', 0, 1, tiled=True)]
    ppermute x14 -> x18, waiting for transfers between devices: 17.8 us -> 10.5 us  [permute_xor(): return lax.ppermute(a, axis, [(i, i ^ mask) for i in range(count)])]
    all_to_all x1 -> x2, starting transfers between devices: 3.63 us -> 7.51 us  [the longest x1 3.96 us: on_device(): log_rates = lax.all_to_all(log_decay[0], 'seq', 0, 1, tiled=True)]
    reduce_scatter x1, waiting for transfers between devices: 2.98 us -> 0.02 us  [on_device(): lax.psum_scatter(head_weights.reshape(hidden_width, width), 'fsdp', scatt...]
    slice x0 -> x2, local copies, waits for them, and re-layouts: none -> 2.75 us  [the longest x1 1.67 us: on_device(): columns(r)[:, :first_part]]
    pallas_call x1, Pallas kernels: 18.9 us -> 16.2 us  [on_device(): pl.pallas_call(functools.partial(forward_kernel, sources, len(arrays), sl...]
    all_to_all x1, starting transfers between devices: 3.46 us -> 5.95 us  [on_device(): owned = lax.all_to_all(packed_sums, 'seq', 0, 0)]
  transfers between devices with their start and end apart: 22 -> 27, of which waited for: 7 -> 7; matrix products, arithmetic and copies ran while one was open for 3% -> 5% of each run, Pallas kernels for 38% -> 37%
where the time goes in v5:
time: 175 us; the launch traced here: 174 us
  Pallas kernels  68.3 us (39%)
  waiting for transfers between devices  39.1 us (22%)
  starting transfers between devices  39 us (22%)
  between operations  14.1 us (8%)
  local copies, waits for them, and re-layouts  10.8 us (6%)
  other arithmetic  2.22 us (1%)
    all_to_all x1, waiting for transfers between devices, on_device(): log_rates = lax.all_to_all(log_decay[0], 'seq', 0, 1, tiled=True)  17.9 us
    pallas_call x1, Pallas kernels, on_device(): pl.pallas_call(functools.partial(forward_kernel, sources, len(arrays), sl...  16.2 us
    ppermute x18, starting transfers between devices, permute_xor(): return lax.ppermute(a, axis, [(i, i ^ mask) for i in range(count)])  13.8 us
    pallas_call x1, Pallas kernels, on_device(): pl.pallas_call(functools.partial(backward_kernel, heads, head_size), out_...  12.9 us
    pallas_call x2, Pallas kernels, weight_columns(): pl.pallas_call(functools.partial(weight_kernel, sources, len(arrays), slo...  12.6 us
    ppermute x18, waiting for transfers between devices, permute_xor(): return lax.ppermute(a, axis, [(i, i ^ mask) for i in range(count)])  10.5 us
    pallas_call x1, Pallas kernels, second_step(): return (make_tables(log_rates), blocks, jnp.concatenate(rest, axis=1))  9.3 us
    pallas_call x1, Pallas kernels, on_device(): pl.pallas_call(functools.partial(tokens_kernel, where), grid=(fsdp_count,...  8.52 us
  transfers between devices with their start and end apart: 27, of which 7 were waited for; matrix products, arithmetic and copies ran while one was open for 5% of the time, Pallas kernels for 37%

profile of v5, /device:TPU:0, one launch (start us, length us, event | category | flops | bytes accessed | tf_op | source)
XLA Modules:
  0.0 173.6 jit_solution(10154772440758077756)
XLA Ops:
  9.9 2.6 %collective-permute-start.1 = (bf16[256,2048]{1,0:T(8,128)(2,1)S(1)}, bf16[256,2048]{1,0:T(8,128)(2,1)S(1)}, u32[]{:S(2)}, u32[]{:S(2)}) collective-permute-start(bf16[256,2048]{1,0:T(8,128)(2,1)S(1)} %bitcast.23), channel_id=1, source_target_pairs={{0,8},{4,12},{8,0},{12,4},{16,24},{20,28},{24,16},{28,20},{1,9},{5... | collective-permute-start | bytes 3145736 | tf_op jit(solution)/shard_map/ppermute | solution.py:353
  14.6 4.0 %all-to-all-start = ((f32[8,4,256]{2,1,0:T(4,128)}), f32[8,4,256]{2,1,0:T(4,128)}, u32[]{:S(2)}, u32[]{:S(2)}) async-start(f32[8,4,256]{2,1,0:T(4,128)} %all_to_all.29), calls=%async_computation | async-start | bytes 65536 | tf_op jit(solution)/shard_map/all_to_all | solution.py:484
  20.2 17.9 %all-to-all-done = f32[8,4,256]{2,1,0:T(4,128)} async-done(((f32[8,4,256]{2,1,0:T(4,128)}), f32[8,4,256]{2,1,0:T(4,128)}, u32[]{:S(2)}, u32[]{:S(2)}) %all-to-all-start) | async-done | bytes 32800 | tf_op jit(solution)/shard_map/all_to_all | solution.py:484
  42.5 9.3 %shard_map.67 = (bf16[2048,256]{1,0:T(8,128)(2,1)}, bf16[2048,256]{1,0:T(8,128)(2,1)}, bf16[2048,256]{1,0:T(8,128)(2,1)}, bf16[2048,256]{1,0:T(8,128)(2,1)}, f32...) custom-call(f32[4,2048]{1,0:T(4,128)} %bitcast.4.log_ref), custom_call_target="tpu_custom_call" | custom-call | bytes 62914560 | tf_op jit(solution)/shard_map/pallas_call | solution.py:510
  51.8 2.3 %copy.12 = bf16[32,8,8,256]{3,2,0,1:T(8,128)(2,1)} copy(bf16[32,8,8,256]{3,2,1,0:T(8,128)(2,1)} %bitcast.25) | data formatting | bytes 2097152 | tf_op jit(solution)/shard_map/reshape | solution.py:509
  57.1 3.6 %all-to-all-start.1 = ((bf16[8,256,256]{2,1,0:T(8,128)(2,1)}), bf16[8,256,256]{2,1,0:T(8,128)(2,1)S(1)}, u32[]{:S(2)}, u32[]{:S(2)}) async-start(bf16[8,256,256]{2,1,0:T(8,128)(2,1)} %bitcast.18), calls=%async_computation.1 | async-start | bytes 2097152 | tf_op jit(solution)/shard_map/all_to_all | solution.py:530
  62.4 16.2 %shard_map.68 = (bf16[2048,256]{1,0:T(8,128)(2,1)}, bf16[2048,128]{1,0:T(8,128)(2,1)}, bf16[2048,128]{1,0:T(8,128)(2,1)}, bf16[2048,256]{1,0:T(8,128)(2,1)}, bf1...) custom-call(s32[2]{0:T(128)} %pad_add_fusion.place_ref.places_ref, ...), custom_call_target="tpu_custom_call" | custom-call | flops 19327352832 | bytes 16777216 | tf_op jit(solution)/shard_map/pallas_call | solution.py:533
  78.6 4.1 %all-to-all-start.2 = ((bf16[8,256,256]{2,1,0:T(8,128)(2,1)}), bf16[8,256,256]{2,1,0:T(8,128)(2,1)S(1)}, u32[]{:S(2)}, u32[]{:S(2)}) async-start(bf16[8,256,256]{2,1,0:T(8,128)(2,1)} %bitcast.29), calls=%async_computation.2 | async-start | bytes 2097152 | tf_op jit(solution)/shard_map/all_to_all | solution.py:554
  82.7 12.9 %shard_map.69 = (bf16[2048,256]{1,0:T(8,128)(2,1)}, bf16[256,2048]{1,0:T(8,128)(2,1)}) custom-call(bf16[2048,256]{1,0:T(8,128)(2,1)} %bitcast.27, bf16[2048,256]{1,0:T(8,128)(2,1)} %get-tuple-element.134.refs_1_, bf16[2048,256]{1,0:T(8,128)(2,1)} %get-tuple-element.135.refs_2_, bf16[2048,128]{1,0:T(8,128)(2,1)} %get-tuple-element.136.refs_3_, ...), custom_call_target="tpu_custom_call" | custom-call | flops 16106127360 | bytes 20971520 | tf_op jit(solution)/shard_map/pallas_call | solution.py:560
  95.6 2.5 %all-to-all-done.2.blocks_ref = bf16[8,256,256]{2,1,0:T(8,128)(2,1)S(1)} async-done(((bf16[8,256,256]{2,1,0:T(8,128)(2,1)}), bf16[8,256,256]{2,1,0:T(8,128)(2,1)S(1)}, u32[]{:S(2)}, u32[]{:S(2)}) %all-to-all-start.2) | async-done | bytes 1048608 | tf_op jit(solution)/shard_map/all_to_all | solution.py:554
  98.1 3.6 %all-to-all-start.3 = ((bf16[8,32,2048]{2,1,0:T(8,128)(2,1)}), bf16[8,32,2048]{2,1,0:T(8,128)(2,1)S(1)}, u32[]{:S(2)}, u32[]{:S(2)}) async-start(bf16[8,32,2048]{2,1,0:T(8,128)(2,1)} %bitcast.28), calls=%async_computation.3 | async-start | bytes 2097152 | tf_op jit(solution)/shard_map/all_to_all | solution.py:595
  101.8 6.5 %shard_map.70 = bf16[4,8,64,256]{3,2,1,0:T(8,128)(2,1)} custom-call(s32[2]{0:T(128)} %pad_add_fusion.place_ref.places_ref, bf16[256,2048]{1,0:T(8,128)(2,1)} %bitcast.20, bf16[256,2048]{1,0:T(8,128)(2,1)} %collective-permute-done.refs_1_, bf16[256,2048]{1,0:T(8,128)(2,1)} %copy-done.2, bf16[256,2048]{1,0:T(8,128)(2,1)} %copy-done.7, ...), custom_call_target="tpu_custom_call" | custom-call | flops 4294967296 | bytes 16777216 | tf_op jit(solution)/shard_map/pallas_call | solution.py:583
  109.4 7.6 %all-to-all-done.3.parts_ref = bf16[8,32,2048]{2,1,0:T(8,128)(2,1)S(1)} async-done(((bf16[8,32,2048]{2,1,0:T(8,128)(2,1)}), bf16[8,32,2048]{2,1,0:T(8,128)(2,1)S(1)}, u32[]{:S(2)}, u32[]{:S(2)}) %all-to-all-start.3) | async-done | bytes 1048608 | tf_op jit(solution)/shard_map/all_to_all | solution.py:595
  118.7 2.8 %shard_map.71 = (bf16[32,2048]{1,0:T(8,128)(2,1)}, bf16[8,288,256]{2,1,0:T(8,128)(2,1)}) custom-call(bf16[8,32,2048]{2,1,0:T(8,128)(2,1)} %copy-done.1, bf16[2048,256]{1,0:T(8,128)(2,1)} %get-tuple-element.145.refs_10_.dx_ref), custom_call_target="tpu_custom_call" | custom-call | tf_op jit(solution)/shard_map/pallas_call | solution.py:607
  121.5 3.8 %all-to-all-start.4 = ((bf16[8,288,256]{2,1,0:T(8,128)(2,1)}), bf16[8,288,256]{2,1,0:T(8,128)(2,1)S(1)}, u32[]{:S(2)}, u32[]{:S(2)}) async-start(bf16[8,288,256]{2,1,0:T(8,128)(2,1)} %get-tuple-element.149), calls=%async_computation.4 | async-start | bytes 2359296 | tf_op jit(solution)/shard_map/all_to_all | solution.py:616
  125.3 7.0 %collective-permute-done.14.refs_1_ = bf16[2048,128]{1,0:T(8,128)(2,1)S(1)} collective-permute-done((bf16[2048,128]{1,0:T(8,128)(2,1)S(1)}, bf16[2048,128]{1,0:T(8,128)(2,1)S(1)}, u32[]{:S(2)}, u32[]{:S(2)}) %collective-permute-start.14) | collective-permute-done | bytes 524320 | tf_op jit(solution)/shard_map/ppermute | solution.py:353
  132.9 6.1 %shard_map.72 = (bf16[8,16,128]{2,1,0:T(8,128)(2,1)}, bf16[8,16,128]{2,1,0:T(8,128)(2,1)}, bf16[8,16,128]{2,1,0:T(8,128)(2,1)}, bf16[8,16,128]{2,1,0:T(8,128)(2,1)}) custom-call(s32[2]{0:T(128)} %pad_add_fusion.place_ref.places_ref, bf16[256,2048]{1,0:T(8,128)(2,1)} %bitcast.21, bf16[256,2048]{1,0:T(8,128)(2,1)} %collective-permute-done.refs_1_, ...), custom_call_target="tpu_custom_call" | custom-call | flops 536870912 | bytes 16777216 | tf_op jit(solution)/shard_map/pallas_call | solution.py:583
  139.0 2.6 %collective-permute-start.10 = (bf16[8,16,128]{2,1,0:T(8,128)(2,1)}, bf16[8,16,128]{2,1,0:T(8,128)(2,1)S(1)}, u32[]{:S(2)}, u32[]{:S(2)}) collective-permute-start(bf16[8,16,128]{2,1,0:T(8,128)(2,1)} %get-tuple-element.153), channel_id=1, source_target_pairs={{0,2},{1,3},{2,0},{3,1},{4,6},{5,7},{6,4},{7,5},{8,10},{9,11},{10,... | collective-permute-start | bytes 98312 | tf_op jit(solution)/shard_map/ppermute | solution.py:353
  143.3 2.3 %shard_map.73 = bf16[1,256,2048]{2,1,0:T(8,128)(2,1)} custom-call(bf16[8,256,256]{2,1,0:T(8,128)(2,1)} %copy-done), custom_call_target="tpu_custom_call" | custom-call | tf_op jit(solution)/shard_map/pallas_call | solution.py:620
  145.7 1.9 %collective-permute-done.11.refs_4_ = bf16[8,16,128]{2,1,0:T(8,128)(2,1)S(1)} collective-permute-done((bf16[8,16,128]{2,1,0:T(8,128)(2,1)}, bf16[8,16,128]{2,1,0:T(8,128)(2,1)S(1)}, u32[]{:S(2)}, u32[]{:S(2)}) %collective-permute-start.11) | collective-permute-done | bytes 32800 | tf_op jit(solution)/shard_map/ppermute | solution.py:353
  148.2 1.8 %shard_map.75 = bf16[8,80,256]{2,1,0:T(8,128)(2,1)} custom-call(bf16[8,64,256]{2,1,0:T(8,128)(2,1)} %bitcast.30, bf16[8,16,128]{2,1,0:T(8,128)(2,1)} %get-tuple-element.165.refs_1_, bf16[8,16,128]{2,1,0:T(8,128)(2,1)} %copy-done.14, bf16[8,16,128]{2,1,0:T(8,128)(2,1)} %copy-done.12, bf16[8,16,128]{2,1,0:T(8,128)(2,1)} %copy-done.13), custom_call_target="tpu_custom_call" | custom-call | tf_op jit(solution)/shard_map/pallas_call | solution.py:662
  149.9 6.0 %all-to-all-start.5 = ((bf16[8,80,256]{2,1,0:T(8,128)(2,1)}), bf16[8,80,256]{2,1,0:T(8,128)(2,1)S(1)}, u32[]{:S(2)}, u32[]{:S(2)}) async-start(bf16[8,80,256]{2,1,0:T(8,128)(2,1)} %shard_map.75), calls=%async_computation.6 | async-start | bytes 655360 | tf_op jit(solution)/shard_map/all_to_all | solution.py:670
  155.9 8.5 %shard_map.74 = bf16[1,256,2048]{2,1,0:T(8,128)(2,1)} custom-call(s32[2]{0:T(128)} %pad_add_fusion.place_ref.places_ref, bf16[8,288,256]{2,1,0:T(8,128)(2,1)} %copy-done.5, bf16[2048,512]{1,0:T(8,128)(2,1)} %all-gather.3.cloned.1.call-done.refs_10_.own_ref, bf16[2048,512]{1,0:T(8,128)(2,1)} %collective-permute-done.12.partner_ref, ...), custom_call_target="tpu_custom_call" | custom-call | flops 4831838208 | bytes 18874368 | tf_op jit(solution)/shard_map/pallas_call | solution.py:646
  165.2 1.9 %shard_map.76 = f32[64,2304]{1,0:T(8,128)} custom-call(bf16[8,80,256]{2,1,0:T(8,128)(2,1)} %copy-done.4), custom_call_target="tpu_custom_call" | custom-call | tf_op jit(solution)/shard_map/pallas_call | solution.py:672
  (93 shorter events, 21.8 us)
Async XLA Ops:
  7.2 54.3 %all-gather.3.cloned.1.call-start = ((), (), s32[]{:S(2)}) async-start(), calls=%async_computation.7 | async-start | bytes 2621440 | tf_op jit(solution)/shard_map/all_gather | solution.py:481
  9.4 28.8 %collective-permute-start = (bf16[256,2048]{1,0:T(8,128)(2,1)S(1)}, bf16[256,2048]{1,0:T(8,128)(2,1)}, u32[]{:S(2)}, u32[]{:S(2)}) collective-permute-start(bf16[256,2048]{1,0:T(8,128)(2,1)S(1)} %bitcast.22), channel_id=1, source_target_pairs={{0,4},{4,0},{8,12},{12,8},{16,20},{20,16},{24,28},{28,24},{1,5},{5... | collective-permute-start | bytes 3145736 | tf_op jit(solution)/shard_map/ppermute | solution.py:353
  9.9 28.3 %collective-permute-start.1 = (bf16[256,2048]{1,0:T(8,128)(2,1)S(1)}, bf16[256,2048]{1,0:T(8,128)(2,1)S(1)}, u32[]{:S(2)}, u32[]{:S(2)}) collective-permute-start(bf16[256,2048]{1,0:T(8,128)(2,1)S(1)} %bitcast.23), channel_id=1, source_target_pairs={{0,8},{4,12},{8,0},{12,4},{16,24},{20,28},{24,16},{28,20},{1,9},{5... | collective-permute-start | bytes 3145736 | tf_op jit(solution)/shard_map/ppermute | solution.py:353
  12.4 25.7 %collective-permute-start.2 = (bf16[256,2048]{1,0:T(8,128)(2,1)S(1)}, bf16[256,2048]{1,0:T(8,128)(2,1)S(1)}, u32[]{:S(2)}, u32[]{:S(2)}) collective-permute-start(bf16[256,2048]{1,0:T(8,128)(2,1)S(1)} %bitcast.24), channel_id=1, source_target_pairs={{0,16},{4,20},{8,24},{12,28},{16,0},{20,4},{24,8},{28,12},{1,17},{... | collective-permute-start | bytes 3145736 | tf_op jit(solution)/shard_map/ppermute | solution.py:353
  14.6 23.5 %all-to-all-start = ((f32[8,4,256]{2,1,0:T(4,128)}), f32[8,4,256]{2,1,0:T(4,128)}, u32[]{:S(2)}, u32[]{:S(2)}) async-start(f32[8,4,256]{2,1,0:T(4,128)} %all_to_all.29), calls=%async_computation | async-start | bytes 65536 | tf_op jit(solution)/shard_map/all_to_all | solution.py:484
  38.2 17.8 %collective-permute-start.3 = (bf16[256,2048]{1,0:T(8,128)(2,1)S(1)}, bf16[256,2048]{1,0:T(8,128)(2,1)S(1)}, u32[]{:S(2)}, u32[]{:S(2)}) collective-permute-start(bf16[256,2048]{1,0:T(8,128)(2,1)S(1)} %collective-permute-done.1.refs_2_), channel_id=1, source_target_pairs={{0,4},{4,0},{8,12},{12,8},{16,20},{20,16},{24,28},{28,24},{1,5},{5... | collective-permute-start | bytes 3145736 | tf_op jit(solution)/shard_map/ppermute | solution.py:353
  38.3 17.6 %collective-permute-start.4 = (bf16[256,2048]{1,0:T(8,128)(2,1)S(1)}, bf16[256,2048]{1,0:T(8,128)(2,1)}, u32[]{:S(2)}, u32[]{:S(2)}) collective-permute-start(bf16[256,2048]{1,0:T(8,128)(2,1)S(1)} %collective-permute-done.2.refs_4_), channel_id=1, source_target_pairs={{0,4},{4,0},{8,12},{12,8},{16,20},{20,16},{24,28},{28,24},{1,5},{5... | collective-permute-start | bytes 3145736 | tf_op jit(solution)/shard_map/ppermute | solution.py:353
  40.4 14.5 %collective-permute-start.5 = (bf16[128,2048]{1,0:T(8,128)(2,1)}, bf16[128,2048]{1,0:T(8,128)(2,1)}, u32[]{:S(2)}, u32[]{:S(2)}) collective-permute-start(bf16[128,2048]{1,0:T(8,128)(2,1)} %slice.20), channel_id=1, source_target_pairs={{0,16},{4,20},{8,24},{12,28},{16,0},{20,4},{24,8},{28,12},{1,17},{... | collective-permute-start | bytes 1572872 | tf_op jit(solution)/shard_map/ppermute | solution.py:353
  42.0 13.9 %collective-permute-start.6 = (bf16[128,2048]{1,0:T(8,128)(2,1)}, bf16[128,2048]{1,0:T(8,128)(2,1)}, u32[]{:S(2)}, u32[]{:S(2)}) collective-permute-start(bf16[128,2048]{1,0:T(8,128)(2,1)} %slice.21), channel_id=1, source_target_pairs={{0,8},{4,12},{8,0},{12,4},{16,24},{20,28},{24,16},{28,20},{1,9},{5... | collective-permute-start | bytes 1572872 | tf_op jit(solution)/shard_map/ppermute | solution.py:353
  57.1 21.5 %all-to-all-start.1 = ((bf16[8,256,256]{2,1,0:T(8,128)(2,1)}), bf16[8,256,256]{2,1,0:T(8,128)(2,1)S(1)}, u32[]{:S(2)}, u32[]{:S(2)}) async-start(bf16[8,256,256]{2,1,0:T(8,128)(2,1)} %bitcast.18), calls=%async_computation.1 | async-start | bytes 2097152 | tf_op jit(solution)/shard_map/all_to_all | solution.py:530
  60.6 56.4 %all-gather.5.cloned.1.call-start = ((), (), s32[]{:S(2)}) async-start(), calls=%async_computation.8 | async-start | bytes 2621440 | tf_op jit(solution)/shard_map/all_gather | solution.py:527
  78.6 19.5 %all-to-all-start.2 = ((bf16[8,256,256]{2,1,0:T(8,128)(2,1)}), bf16[8,256,256]{2,1,0:T(8,128)(2,1)S(1)}, u32[]{:S(2)}, u32[]{:S(2)}) async-start(bf16[8,256,256]{2,1,0:T(8,128)(2,1)} %bitcast.29), calls=%async_computation.2 | async-start | bytes 2097152 | tf_op jit(solution)/shard_map/all_to_all | solution.py:554
  98.1 18.9 %all-to-all-start.3 = ((bf16[8,32,2048]{2,1,0:T(8,128)(2,1)}), bf16[8,32,2048]{2,1,0:T(8,128)(2,1)S(1)}, u32[]{:S(2)}, u32[]{:S(2)}) async-start(bf16[8,32,2048]{2,1,0:T(8,128)(2,1)} %bitcast.28), calls=%async_computation.3 | async-start | bytes 2097152 | tf_op jit(solution)/shard_map/all_to_all | solution.py:595
  101.7 45.9 %reduce-scatter.2.cloned.1.call-start = ((), (), s32[]{:S(2)}) async-start(), calls=%async_computation.9 | async-start | bytes 1310720 | tf_op jit(solution)/shard_map/reduce_scatter | solution.py:597
  117.1 30.6 %collective-permute-start.12 = (bf16[2048,512]{1,0:T(8,128)(2,1)}, bf16[2048,512]{1,0:T(8,128)(2,1)}, u32[]{:S(2)}, u32[]{:S(2)}) collective-permute-start(bf16[2048,512]{1,0:T(8,128)(2,1)} %all-gather.3.cloned.1.call-done.refs_10_.own_ref), channel_id=1, source_target_pairs={{0,4},{4,0},{8,12},{12,8},{16,20},{20,16},{24,28},{28,24},{1,5},{5... | collective-permute-start | bytes 6291464 | tf_op jit(solution)/shard_map/ppermute | solution.py:353
  117.1 30.6 %collective-permute-start.13 = (bf16[2048,512]{1,0:T(8,128)(2,1)}, bf16[2048,512]{1,0:T(8,128)(2,1)}, u32[]{:S(2)}, u32[]{:S(2)}) collective-permute-start(bf16[2048,512]{1,0:T(8,128)(2,1)} %all-gather.5.cloned.1.call-done.refs_0_), channel_id=1, source_target_pairs={{0,4},{4,0},{8,12},{12,8},{16,20},{20,16},{24,28},{28,24},{1,5},{5... | collective-permute-start | bytes 6291464 | tf_op jit(solution)/shard_map/ppermute | solution.py:353
  117.6 14.8 %collective-permute-start.14 = (bf16[2048,128]{1,0:T(8,128)(2,1)S(1)}, bf16[2048,128]{1,0:T(8,128)(2,1)S(1)}, u32[]{:S(2)}, u32[]{:S(2)}) collective-permute-start(bf16[2048,128]{1,0:T(8,128)(2,1)S(1)} %slice.23), channel_id=1, source_target_pairs={{0,8},{4,12},{8,0},{12,4},{16,24},{20,28},{24,16},{28,20},{1,9},{5... | collective-permute-start | bytes 1572872 | tf_op jit(solution)/shard_map/ppermute | solution.py:353
  118.1 14.8 %collective-permute-start.16 = (bf16[2048,128]{1,0:T(8,128)(2,1)S(1)}, bf16[2048,128]{1,0:T(8,128)(2,1)S(1)}, u32[]{:S(2)}, u32[]{:S(2)}) collective-permute-start(bf16[2048,128]{1,0:T(8,128)(2,1)S(1)} %slice.23), channel_id=1, source_target_pairs={{0,16},{4,20},{8,24},{12,28},{16,0},{20,4},{24,8},{28,12},{1,17},{... | collective-permute-start | bytes 1572872 | tf_op jit(solution)/shard_map/ppermute | solution.py:353
  121.5 26.1 %all-to-all-start.4 = ((bf16[8,288,256]{2,1,0:T(8,128)(2,1)}), bf16[8,288,256]{2,1,0:T(8,128)(2,1)S(1)}, u32[]{:S(2)}, u32[]{:S(2)}) async-start(bf16[8,288,256]{2,1,0:T(8,128)(2,1)} %get-tuple-element.149), calls=%async_computation.4 | async-start | bytes 2359296 | tf_op jit(solution)/shard_map/all_to_all | solution.py:616
  132.4 9.3 %collective-permute-start.15 = (bf16[2048,128]{1,0:T(8,128)(2,1)S(1)}, bf16[2048,128]{1,0:T(8,128)(2,1)S(1)}, u32[]{:S(2)}, u32[]{:S(2)}) collective-permute-start(bf16[2048,128]{1,0:T(8,128)(2,1)S(1)} %collective-permute-done.14.refs_1_), channel_id=1, source_target_pairs={{0,4},{4,0},{8,12},{12,8},{16,20},{20,16},{24,28},{28,24},{1,5},{5... | collective-permute-start | bytes 1572872 | tf_op jit(solution)/shard_map/ppermute | solution.py:353
  132.9 10.1 %collective-permute-start.17 = (bf16[2048,128]{1,0:T(8,128)(2,1)S(1)}, bf16[2048,128]{1,0:T(8,128)(2,1)S(1)}, u32[]{:S(2)}, u32[]{:S(2)}) collective-permute-start(bf16[2048,128]{1,0:T(8,128)(2,1)S(1)} %collective-permute-done.16.refs_2_), channel_id=1, source_target_pairs={{0,4},{4,0},{8,12},{12,8},{16,20},{20,16},{24,28},{28,24},{1,5},{5... | collective-permute-start | bytes 1572872 | tf_op jit(solution)/shard_map/ppermute | solution.py:353
  139.0 6.7 %collective-permute-start.10 = (bf16[8,16,128]{2,1,0:T(8,128)(2,1)}, bf16[8,16,128]{2,1,0:T(8,128)(2,1)S(1)}, u32[]{:S(2)}, u32[]{:S(2)}) collective-permute-start(bf16[8,16,128]{2,1,0:T(8,128)(2,1)} %get-tuple-element.153), channel_id=1, source_target_pairs={{0,2},{1,3},{2,0},{3,1},{4,6},{5,7},{6,4},{7,5},{8,10},{9,11},{10,... | collective-permute-start | bytes 98312 | tf_op jit(solution)/shard_map/ppermute | solution.py:353
  141.6 5.9 %collective-permute-start.11 = (bf16[8,16,128]{2,1,0:T(8,128)(2,1)}, bf16[8,16,128]{2,1,0:T(8,128)(2,1)S(1)}, u32[]{:S(2)}, u32[]{:S(2)}) collective-permute-start(bf16[8,16,128]{2,1,0:T(8,128)(2,1)} %get-tuple-element.154), channel_id=1, source_target_pairs={{0,3},{1,2},{2,1},{3,0},{4,7},{5,6},{6,5},{7,4},{8,11},{9,10},{10,... | collective-permute-start | bytes 98312 | tf_op jit(solution)/shard_map/ppermute | solution.py:353
  149.9 14.5 %all-to-all-start.5 = ((bf16[8,80,256]{2,1,0:T(8,128)(2,1)}), bf16[8,80,256]{2,1,0:T(8,128)(2,1)S(1)}, u32[]{:S(2)}, u32[]{:S(2)}) async-start(bf16[8,80,256]{2,1,0:T(8,128)(2,1)} %shard_map.75), calls=%async_computation.6 | async-start | bytes 655360 | tf_op jit(solution)/shard_map/all_to_all | solution.py:670
  (23 other events, 139.2 us)
Sparse Core Ops, SparseCore 0:
  9.6 48.6 all-gather.2
  63.0 47.5 all-gather.4
  112.9 25.8 reduce-scatter.1

commit v6 on v5

--- a/solution.py
+++ b/solution.py
@@ -120,7 +120,7 @@
         carry[...] = dt_ref[k] * carry[...] + term
         return 0
 
-    lax.fori_loop(0, chunks, reverse_states, 0, unroll=8)
+    lax.fori_loop(0, chunks, reverse_states, 0, unroll=16)
     out_stores[6].start()
     carry[...] = jnp.zeros_like(carry)
 
@@ -140,7 +140,7 @@
         carry[...] = dt_ref[k] * carry[...] + dot_tn(b, x * te_ref[rows, :])
         return 0
 
-    lax.fori_loop(0, chunks, outputs, 0, unroll=8)
+    lax.fori_loop(0, chunks, outputs, 0, unroll=16)
     for store in out_stores[3:6]:
         store.start()
     for store in out_stores:
@@ -177,7 +177,7 @@
         carry[...] = dt_ref[k] * carry[...] + dot_tn(c_ref[rows, :], dy * en_ref[rows, :])
         return 0
 
-    lax.fori_loop(0, chunks, end_adjoints, 0, unroll=8)
+    lax.fori_loop(0, chunks, end_adjoints, 0, unroll=16)
     carry[...] = jnp.zeros_like(carry)
     for load in in_loads[6:]:
         load.wait()
@@ -205,7 +205,7 @@
         carry[...] = dt_ref[k] * carry[...] + dot_tn(c, dy_lv)
         return 0
 
-    lax.fori_loop(0, chunks, gradients, 0, unroll=8)
+    lax.fori_loop(0, chunks, gradients, 0, unroll=16)
     out_stores = [
         pltpu.make_async_copy(source, target, stores.at[n])
         for n, (source, target) in enumerate(zip((dx_ref, shared_ref), out_hbm))
@@ -232,30 +232,29 @@
         packed_ref[n, tokens : tokens + part, :tokens] = total[:, block]
 
 
-def tokens_kernel(where, place_ref, packed_ref, own_ref, partner_ref, *refs):
-    columns, (out_ref, lhs_ref, own_lhs) = refs[:-3], refs[-3:]
+def tokens_kernel(layout, place_ref, packed_ref, *refs):
+    arrays = len(layout)
+    column_refs, out_ref, lhs_refs = refs[:arrays], refs[arrays], refs[arrays + 1 :]
     count = packed_ref.shape[0]
-    tokens, first = own_lhs.shape
-    width = lhs_ref.shape[1] // count
-    part = (first - width) // count
+    tokens = out_ref.shape[1]
 
     @pl.when(pl.program_id(0) == 0)
     def _():
-        for r in range(count):
-            source = packed_ref[lax.bitwise_xor(place_ref[0], r), :tokens, :width]
-            lhs_ref[:, r * width : (r + 1) * width] = source
-        own_lhs[:, :width] = lhs_ref[:, :width]
-        turned = [packed_ref[n, tokens : tokens + part, :tokens] for n in range(count)]
-        own_lhs[:, width:] = jnp.concatenate(turned, axis=0).T
-
-    result = dot_nt(own_lhs[...], own_ref[...])
-    result = result + dot_nt(lhs_ref[:, width : 2 * width], partner_ref[:, :width])
-    for r in range(2, count):
-        column = r * width
-        for array, start, extent in where[r]:
-            block = columns[array][:, start : start + extent]
-            result = result + dot_nt(lhs_ref[:, column : column + extent], block)
-            column += extent
+        for lhs_ref, parts in zip(lhs_refs, layout):
+            column = 0
+            for r, start, extent in parts:
+                source = lax.bitwise_xor(place_ref[0], r)
+                block = packed_ref[source, :tokens, start : start + extent]
+                lhs_ref[:, column : column + extent] = block
+                column += extent
+        width = layout[0][0][2]
+        rows = (lhs_refs[0].shape[1] - width) // count
+        turned = [packed_ref[n, tokens : tokens + rows, :tokens] for n in range(count)]
+        lhs_refs[0][:, width:] = jnp.concatenate(turned, axis=0).T
+
+    result = dot_nt(lhs_refs[0][...], column_refs[0][...])
+    for lhs_ref, column_ref in zip(lhs_refs[1:], column_refs[1:]):
+        result = result + dot_nt(lhs_ref[...], column_ref[:, : lhs_ref.shape[1]])
     out_ref[0] = result.astype(bf16)
 
 
@@ -466,7 +465,6 @@
     length = token_count * seq_count
     shared = 2 * state_size
     chunks = length // CHUNK
-    extent = hidden_width // fsdp_count
     shape = jax.ShapeDtypeStruct
     params = pltpu.CompilerParams(vmem_limit_bytes=VMEM_LIMIT)
     scalar = [pl.BlockSpec(memory_space=pltpu.SMEM)]
@@ -505,12 +503,13 @@
     first_part = width // 2
     rest = [columns(r) for r in others] + [columns(r)[:, :first_part] for r in neighbours]
 
-    def second_step(log_rates, upstream, rest):
-        blocks = upstream.reshape(token_count, seq_count, width).transpose(1, 0, 2)
-        return make_tables(log_rates), blocks, jnp.concatenate(rest, axis=1)
-
-    arrays, sources, (tables, upstream, rest) = gather_rows(
-        local_tokens, "seq", (log_rates, upstream, rest), second_step
+    blocks = upstream.reshape(token_count, seq_count, width).transpose(1, 0, 2)
+    rest = jnp.concatenate(rest, axis=1)
+    arrays, sources, (tables, upstream, rest, places) = gather_rows(
+        local_tokens,
+        "seq",
+        (log_rates, blocks, rest, places),
+        lambda log_rates, *others: (make_tables(log_rates), *others),
     )
     to_end, from_start, enter, leave, chunk_decay, decays, turned = tables
 
@@ -525,6 +524,7 @@
     carry = shape((state_size, width), f32)
 
     w_even = lax.all_gather(rest, "fsdp", axis=0, tiled=True)
+    upstream = after(upstream, w_columns)
 
     *arrays, w_columns = lax.optimization_barrier((*arrays, w_columns))
     g = lax.all_to_all(upstream, "seq", 0, 0).reshape(length, width)
@@ -549,7 +549,9 @@
             4 * length * hidden_width,
         ),
     )(places, *arrays, *operands)
-    (x, b, c, z, inverse, states_in, states_next), g = lax.optimization_barrier((forward, g))
+    w_partner = permute_xor(w_columns, "seq", 1)
+    forward, g, w_partner = lax.optimization_barrier((forward, g, w_partner))
+    x, b, c, z, inverse, states_in, states_next = forward
 
     mixed_blocks = lax.all_to_all(z.reshape(seq_count, token_count, width), "seq", 0, 0)
     operands = (
@@ -625,33 +627,32 @@
         out_specs=resident(mixed_shape),
         compiler_params=params,
     )(after(mixed_blocks, shared_columns))
-    w_partner = permute_xor(after(w_columns, arrived), "seq", 1)
-    w_even = [w_even, *w_across]
+    w_even = [w_even, *(after(a, shared_weights[0]) for a in w_across)]
     w_odd = [permute_xor(a, "seq", 1) for a in w_even]
-    grad_blocks, shared_arrived, mixer_out, w_partner, w_odd = lax.optimization_barrier(
-        (grad_blocks, shared_arrived, mixer_out, w_partner, w_odd, head_sums)
-    )[:-1]
+    shared_arrived, mixer_out, w_odd, head_sums = lax.optimization_barrier(
+        (shared_arrived, mixer_out, w_odd, head_sums)
+    )
 
     grad_tokens_shape = shape((1, token_count, hidden_width), bf16)
-    by_rows = lambda a: pl.BlockSpec((extent, a.shape[1]), lambda k: (k, 0))
-    where = {}
-    for n, r in enumerate(others):
-        where[r] = [(0, n * width, width)]
-    for n, r in enumerate(neighbours):
-        start = len(others) * width + n * first_part
-        where[r] = [(0, start, first_part), (1 + n, 0, width - first_part)]
-    for r in range(2, seq_count, 2):
-        where[r + 1] = [(array + len(w_even), start, extent) for array, start, extent in where[r]]
+    steps = 2
+    rows = hidden_width // steps
+    by_rows = lambda a: pl.BlockSpec((rows, a.shape[1]), lambda k: (k, 0))
+    layout = [[(r, 0, width) for r in others] + [(r, 0, first_part) for r in neighbours]]
+    layout += [[(r, first_part, width - first_part)] for r in neighbours]
+    odd_layout = [[(r + 1, start, extent) for r, start, extent in parts] for parts in layout]
+    layout = [[(0, 0, width)], [(1, 0, width)]] + layout + odd_layout
+    lhs_shapes = [
+        shape((token_count, sum(part[2] for part in parts) + (shared if n == 0 else 0)), bf16)
+        for n, parts in enumerate(layout)
+    ]
     w_blocks = [w_columns, w_partner, *w_even, *w_odd]
     grad_tokens = pl.pallas_call(
-        functools.partial(tokens_kernel, where),
-        grid=(fsdp_count,),
+        functools.partial(tokens_kernel, layout),
+        grid=(steps,),
         out_shape=grad_tokens_shape,
         in_specs=scalar + [resident(grad_blocks)] + [by_rows(a) for a in w_blocks],
-        out_specs=pl.BlockSpec((1, token_count, extent), lambda k: (0, 0, k)),
-        scratch_shapes=scratch(
-            shape((token_count, inner_width), bf16), shape((token_count, width + shared), bf16)
-        ),
+        out_specs=pl.BlockSpec((1, token_count, rows), lambda k: (0, 0, k)),
+        scratch_shapes=scratch(*lhs_shapes),
         compiler_params=params,
         cost_estimate=cost(
             4 * token_count * hidden_width * (inner_width + shared),
@@ -667,7 +668,7 @@
         out_specs=resident(packed),
         compiler_params=params,
     )(head_sums, *shared_arrived)
-    owned = lax.all_to_all(packed_sums, "seq", 0, 0)
+    owned = lax.all_to_all(after(packed_sums, grad_blocks), "seq", 0, 0)
     finished = shape((rows_each, inner_width + shared), f32)
     grad_weights = pl.pallas_call(
         finish_kernel,

time: 175 us -> 168 us (0.960)
  waiting for transfers between devices: 39.1 us -> 34 us
    all_to_all x1, waiting for transfers between devices: 17.9 us -> 14.6 us  [on_device(): log_rates = lax.all_to_all(log_decay[0], 'seq', 0, 1, tiled=True)]
    ppermute x18, starting transfers between devices: 13.8 us -> 16.4 us  [permute_xor(): return lax.ppermute(a, axis, [(i, i ^ mask) for i in range(count)])]
    all_to_all x1, starting transfers between devices: 5.95 us -> 3.43 us  [on_device(): owned = lax.all_to_all(after(packed_sums, grad_blocks), 'seq', 0, 0)]
    reshape x1 -> x0, local copies, waits for them, and re-layouts: 2.29 us -> none  [second_step(): blocks = upstream.reshape(token_count, seq_count, width).transpose(1, 0, 2)]
    unnamed x40 -> x39, local copies, waits for them, and re-layouts: 2.24 us -> 4.03 us
  transfers between devices with their start and end apart: 27 -> 27, of which waited for: 7 -> 11; matrix products, arithmetic and copies ran while one was open for 5% -> 5% of each run, Pallas kernels for 37% -> 39%
where the time goes in v6:
time: 168 us; the launch traced here: 167 us
  Pallas kernels  67 us (40%)
  starting transfers between devices  38.7 us (23%)
  waiting for transfers between devices  34 us (20%)
  between operations  14.1 us (8%)
  local copies, waits for them, and re-layouts  11 us (7%)
  other arithmetic  2.35 us (1%)
    ppermute x18, starting transfers between devices, permute_xor(): return lax.ppermute(a, axis, [(i, i ^ mask) for i in range(count)])  16.4 us
    pallas_call x1, Pallas kernels, on_device(): pl.pallas_call(functools.partial(forward_kernel, sources, len(arrays), sl...  15.9 us
    all_to_all x1, waiting for transfers between devices, on_device(): log_rates = lax.all_to_all(log_decay[0], 'seq', 0, 1, tiled=True)  14.6 us
    pallas_call x1, Pallas kernels, on_device(): pl.pallas_call(functools.partial(backward_kernel, heads, head_size), out_...  12.7 us
    pallas_call x2, Pallas kernels, weight_columns(): pl.pallas_call(functools.partial(weight_kernel, sources, len(arrays), slo...  12.4 us
    pallas_call x1, Pallas kernels, on_device(): make_tables(log_rates)  9.15 us
    ppermute x18, waiting for transfers between devices, permute_xor(): return lax.ppermute(a, axis, [(i, i ^ mask) for i in range(count)])  8.93 us
    pallas_call x1, Pallas kernels, on_device(): pl.pallas_call(functools.partial(tokens_kernel, layout), grid=(steps,), o...  7.94 us
  transfers between devices with their start and end apart: 27, of which 11 were waited for; matrix products, arithmetic and copies ran while one was open for 5% of the time, Pallas kernels for 39%

profile of v6, /device:TPU:0, one launch (start us, length us, event | category | flops | bytes accessed | tf_op | source)
XLA Modules:
  0.0 167.1 jit_solution(14455268331961711694)
XLA Ops:
  9.9 2.6 %collective-permute-start.1 = (bf16[256,2048]{1,0:T(8,128)(2,1)S(1)}, bf16[256,2048]{1,0:T(8,128)(2,1)S(1)}, u32[]{:S(2)}, u32[]{:S(2)}) collective-permute-start(bf16[256,2048]{1,0:T(8,128)(2,1)S(1)} %bitcast.22), channel_id=1, source_target_pairs={{0,8},{4,12},{8,0},{12,4},{16,24},{20,28},{24,16},{28,20},{1,9},{5... | collective-permute-start | bytes 3145736 | tf_op jit(solution)/shard_map/ppermute | solution.py:352
  14.6 3.3 %all-to-all-start = ((f32[8,4,256]{2,1,0:T(4,128)}), f32[8,4,256]{2,1,0:T(4,128)S(1)}, u32[]{:S(2)}, u32[]{:S(2)}) async-start(f32[8,4,256]{2,1,0:T(4,128)} %all_to_all.29), calls=%async_computation | async-start | bytes 65536 | tf_op jit(solution)/shard_map/all_to_all | solution.py:482
  20.6 1.6 copy.10
  23.4 14.6 %all-to-all-done = f32[8,4,256]{2,1,0:T(4,128)S(1)} async-done(((f32[8,4,256]{2,1,0:T(4,128)}), f32[8,4,256]{2,1,0:T(4,128)S(1)}, u32[]{:S(2)}, u32[]{:S(2)}) %all-to-all-start) | async-done | bytes 32800 | tf_op jit(solution)/shard_map/all_to_all | solution.py:482
  42.4 9.1 %shard_map.67 = (bf16[2048,256]{1,0:T(8,128)(2,1)}, bf16[2048,256]{1,0:T(8,128)(2,1)}, bf16[2048,256]{1,0:T(8,128)(2,1)}, bf16[2048,256]{1,0:T(8,128)(2,1)}, f32...) custom-call(f32[4,2048]{1,0:T(4,128)} %bitcast.29), custom_call_target="tpu_custom_call" | custom-call | bytes 62914560 | tf_op jit(solution)/shard_map/pallas_call | solution.py:512
  51.6 3.0 %collective-permute-done.5.refs_6_ = bf16[128,2048]{1,0:T(8,128)(2,1)S(1)} collective-permute-done((bf16[128,2048]{1,0:T(8,128)(2,1)}, bf16[128,2048]{1,0:T(8,128)(2,1)S(1)}, u32[]{:S(2)}, u32[]{:S(2)}) %collective-permute-start.5) | collective-permute-done | bytes 524320 | tf_op jit(solution)/shard_map/ppermute | solution.py:352
  59.2 4.4 %all-to-all-start.1 = ((bf16[8,256,256]{2,1,0:T(8,128)(2,1)}), bf16[8,256,256]{2,1,0:T(8,128)(2,1)}, u32[]{:S(2)}, u32[]{:S(2)}) async-start(bf16[8,256,256]{2,1,0:T(8,128)(2,1)} %bitcast.16), calls=%async_computation.1 | async-start | bytes 2097152 | tf_op jit(solution)/shard_map/all_to_all | solution.py:530
  63.7 15.9 %shard_map.68 = (bf16[2048,256]{1,0:T(8,128)(2,1)}, bf16[2048,128]{1,0:T(8,128)(2,1)}, bf16[2048,128]{1,0:T(8,128)(2,1)}, bf16[2048,256]{1,0:T(8,128)(2,1)}, bf1...) custom-call(s32[2]{0:T(128)} %pad_add_fusion.place_ref.places_ref, ...), custom_call_target="tpu_custom_call" | custom-call | flops 19327352832 | bytes 16777216 | tf_op jit(solution)/shard_map/pallas_call | solution.py:533
  79.6 3.9 %all-to-all-start.2 = ((bf16[8,256,256]{2,1,0:T(8,128)(2,1)}), bf16[8,256,256]{2,1,0:T(8,128)(2,1)S(1)}, u32[]{:S(2)}, u32[]{:S(2)}) async-start(bf16[8,256,256]{2,1,0:T(8,128)(2,1)} %bitcast.27), calls=%async_computation.2 | async-start | bytes 2097152 | tf_op jit(solution)/shard_map/all_to_all | solution.py:556
  83.4 12.7 %shard_map.69 = (bf16[2048,256]{1,0:T(8,128)(2,1)}, bf16[256,2048]{1,0:T(8,128)(2,1)}) custom-call(bf16[2048,256]{1,0:T(8,128)(2,1)} %bitcast.6.refs_0_, bf16[2048,256]{1,0:T(8,128)(2,1)} %get-tuple-element.138.refs_1_, bf16[2048,256]{1,0:T(8,128)(2,1)} %get-tuple-element.139.refs_2_, bf16[2048,128]{1,0:T(8,128)(2,1)} %get-tuple-element.140.refs_3_, ...), custom_call_target="tpu_custom_call" | custom-call | flops 16106127360 | bytes 20971520 | tf_op jit(solution)/shard_map/pallas_call | solution.py:562
  96.1 2.7 %all-to-all-done.2.blocks_ref = bf16[8,256,256]{2,1,0:T(8,128)(2,1)S(1)} async-done(((bf16[8,256,256]{2,1,0:T(8,128)(2,1)}), bf16[8,256,256]{2,1,0:T(8,128)(2,1)S(1)}, u32[]{:S(2)}, u32[]{:S(2)}) %all-to-all-start.2) | async-done | bytes 1048608 | tf_op jit(solution)/shard_map/all_to_all | solution.py:556
  98.9 3.6 %all-to-all-start.3 = ((bf16[8,32,2048]{2,1,0:T(8,128)(2,1)}), bf16[8,32,2048]{2,1,0:T(8,128)(2,1)S(1)}, u32[]{:S(2)}, u32[]{:S(2)}) async-start(bf16[8,32,2048]{2,1,0:T(8,128)(2,1)} %bitcast.26), calls=%async_computation.3 | async-start | bytes 2097152 | tf_op jit(solution)/shard_map/all_to_all | solution.py:597
  102.5 6.5 %shard_map.70 = bf16[4,8,64,256]{3,2,1,0:T(8,128)(2,1)} custom-call(s32[2]{0:T(128)} %pad_add_fusion.place_ref.places_ref, bf16[256,2048]{1,0:T(8,128)(2,1)} %bitcast.19, bf16[256,2048]{1,0:T(8,128)(2,1)} %collective-permute-done.refs_1_, bf16[256,2048]{1,0:T(8,128)(2,1)} %copy-done.2, bf16[256,2048]{1,0:T(8,128)(2,1)} %copy-done.7, ...), custom_call_target="tpu_custom_call" | custom-call | flops 4294967296 | bytes 16777216 | tf_op jit(solution)/shard_map/pallas_call | solution.py:585
  110.1 7.6 %all-to-all-done.3.parts_ref = bf16[8,32,2048]{2,1,0:T(8,128)(2,1)S(1)} async-done(((bf16[8,32,2048]{2,1,0:T(8,128)(2,1)}), bf16[8,32,2048]{2,1,0:T(8,128)(2,1)S(1)}, u32[]{:S(2)}, u32[]{:S(2)}) %all-to-all-start.3) | async-done | bytes 1048608 | tf_op jit(solution)/shard_map/all_to_all | solution.py:597
  118.9 2.8 %shard_map.71 = (bf16[32,2048]{1,0:T(8,128)(2,1)}, bf16[8,288,256]{2,1,0:T(8,128)(2,1)}) custom-call(bf16[8,32,2048]{2,1,0:T(8,128)(2,1)} %copy-done.1, bf16[2048,256]{1,0:T(8,128)(2,1)} %get-tuple-element.149.refs_10_.dx_ref), custom_call_target="tpu_custom_call" | custom-call | tf_op jit(solution)/shard_map/pallas_call | solution.py:609
  121.7 3.6 %all-to-all-start.4 = ((bf16[8,288,256]{2,1,0:T(8,128)(2,1)}), bf16[8,288,256]{2,1,0:T(8,128)(2,1)S(1)}, u32[]{:S(2)}, u32[]{:S(2)}) async-start(bf16[8,288,256]{2,1,0:T(8,128)(2,1)} %get-tuple-element.164), calls=%async_computation.5 | async-start | bytes 2359296 | tf_op jit(solution)/shard_map/all_to_all | solution.py:618
  125.3 5.9 %shard_map.72 = (bf16[8,16,128]{2,1,0:T(8,128)(2,1)}, bf16[8,16,128]{2,1,0:T(8,128)(2,1)}, bf16[8,16,128]{2,1,0:T(8,128)(2,1)}, bf16[8,16,128]{2,1,0:T(8,128)(2,1)}) custom-call(s32[2]{0:T(128)} %pad_add_fusion.place_ref.places_ref, bf16[256,2048]{1,0:T(8,128)(2,1)} %bitcast.20, bf16[256,2048]{1,0:T(8,128)(2,1)} %collective-permute-done.refs_1_, ...), custom_call_target="tpu_custom_call" | custom-call | flops 536870912 | bytes 16777216 | tf_op jit(solution)/shard_map/pallas_call | solution.py:585
  134.7 2.6 %collective-permute-start.11 = (bf16[8,16,128]{2,1,0:T(8,128)(2,1)}, bf16[8,16,128]{2,1,0:T(8,128)(2,1)S(1)}, u32[]{:S(2)}, u32[]{:S(2)}) collective-permute-start(bf16[8,16,128]{2,1,0:T(8,128)(2,1)} %get-tuple-element.156), channel_id=1, source_target_pairs={{0,2},{1,3},{2,0},{3,1},{4,6},{5,7},{6,4},{7,5},{8,10},{9,11},{10,... | collective-permute-start | bytes 98312 | tf_op jit(solution)/shard_map/ppermute | solution.py:352
  137.8 3.1 %collective-permute-start.12 = (bf16[8,16,128]{2,1,0:T(8,128)(2,1)}, bf16[8,16,128]{2,1,0:T(8,128)(2,1)S(1)}, u32[]{:S(2)}, u32[]{:S(2)}) collective-permute-start(bf16[8,16,128]{2,1,0:T(8,128)(2,1)} %get-tuple-element.157), channel_id=1, source_target_pairs={{0,3},{1,2},{2,1},{3,0},{4,7},{5,6},{6,5},{7,4},{8,11},{9,10},{10,... | collective-permute-start | bytes 98312 | tf_op jit(solution)/shard_map/ppermute | solution.py:352
  140.8 2.3 %shard_map.73 = bf16[1,256,2048]{2,1,0:T(8,128)(2,1)} custom-call(bf16[8,256,256]{2,1,0:T(8,128)(2,1)} %copy-done), custom_call_target="tpu_custom_call" | custom-call | tf_op jit(solution)/shard_map/pallas_call | solution.py:622
  144.6 1.9 %shard_map.75 = bf16[8,80,256]{2,1,0:T(8,128)(2,1)} custom-call(bf16[8,64,256]{2,1,0:T(8,128)(2,1)} %bitcast.28, bf16[8,16,128]{2,1,0:T(8,128)(2,1)} %get-tuple-element.170.refs_1_, bf16[8,16,128]{2,1,0:T(8,128)(2,1)} %copy-done.11, bf16[8,16,128]{2,1,0:T(8,128)(2,1)} %copy-done.12, bf16[8,16,128]{2,1,0:T(8,128)(2,1)} %copy-done.13), custom_call_target="tpu_custom_call" | custom-call | tf_op jit(solution)/shard_map/pallas_call | solution.py:663
  146.5 3.4 %all-to-all-start.5 = ((bf16[8,80,256]{2,1,0:T(8,128)(2,1)}), bf16[8,80,256]{2,1,0:T(8,128)(2,1)S(1)}, u32[]{:S(2)}, u32[]{:S(2)}) async-start(bf16[8,80,256]{2,1,0:T(8,128)(2,1)} %shard_map.75), calls=%async_computation.6 | async-start | bytes 655360 | tf_op jit(solution)/shard_map/all_to_all | solution.py:671
  150.0 7.9 %shard_map.74 = bf16[1,256,2048]{2,1,0:T(8,128)(2,1)} custom-call(s32[2]{0:T(128)} %pad_add_fusion.place_ref.places_ref, bf16[8,288,256]{2,1,0:T(8,128)(2,1)} %copy-done.5, bf16[2048,512]{1,0:T(8,128)(2,1)} %all-gather.3.cloned.1.call-done.refs_10_.refs_0_, bf16[2048,512]{1,0:T(8,128)(2,1)} %collective-permute-done.9.refs_1_, ...), custom_call_target="tpu_custom_call" | custom-call | flops 4831838208 | bytes 18874368 | tf_op jit(solution)/shard_map/pallas_call | solution.py:649
  158.7 1.9 %shard_map.76 = f32[64,2304]{1,0:T(8,128)} custom-call(bf16[8,80,256]{2,1,0:T(8,128)(2,1)} %copy-done.4), custom_call_target="tpu_custom_call" | custom-call | tf_op jit(solution)/shard_map/pallas_call | solution.py:673
  (92 shorter events, 26.0 us)
Async XLA Ops:
  7.2 51.8 %all-gather.3.cloned.1.call-start = ((), (), s32[]{:S(2)}) async-start(), calls=%async_computation.7 | async-start | bytes 2621440 | tf_op jit(solution)/shard_map/all_gather | solution.py:479
  9.4 28.7 %collective-permute-start = (bf16[256,2048]{1,0:T(8,128)(2,1)S(1)}, bf16[256,2048]{1,0:T(8,128)(2,1)}, u32[]{:S(2)}, u32[]{:S(2)}) collective-permute-start(bf16[256,2048]{1,0:T(8,128)(2,1)S(1)} %bitcast.21), channel_id=1, source_target_pairs={{0,4},{4,0},{8,12},{12,8},{16,20},{20,16},{24,28},{28,24},{1,5},{5... | collective-permute-start | bytes 3145736 | tf_op jit(solution)/shard_map/ppermute | solution.py:352
  9.9 28.2 %collective-permute-start.1 = (bf16[256,2048]{1,0:T(8,128)(2,1)S(1)}, bf16[256,2048]{1,0:T(8,128)(2,1)S(1)}, u32[]{:S(2)}, u32[]{:S(2)}) collective-permute-start(bf16[256,2048]{1,0:T(8,128)(2,1)S(1)} %bitcast.22), channel_id=1, source_target_pairs={{0,8},{4,12},{8,0},{12,4},{16,24},{20,28},{24,16},{28,20},{1,9},{5... | collective-permute-start | bytes 3145736 | tf_op jit(solution)/shard_map/ppermute | solution.py:352
  12.4 25.6 %collective-permute-start.2 = (bf16[256,2048]{1,0:T(8,128)(2,1)S(1)}, bf16[256,2048]{1,0:T(8,128)(2,1)S(1)}, u32[]{:S(2)}, u32[]{:S(2)}) collective-permute-start(bf16[256,2048]{1,0:T(8,128)(2,1)S(1)} %bitcast.23), channel_id=1, source_target_pairs={{0,16},{4,20},{8,24},{12,28},{16,0},{20,4},{24,8},{28,12},{1,17},{... | collective-permute-start | bytes 3145736 | tf_op jit(solution)/shard_map/ppermute | solution.py:352
  14.6 23.4 %all-to-all-start = ((f32[8,4,256]{2,1,0:T(4,128)}), f32[8,4,256]{2,1,0:T(4,128)S(1)}, u32[]{:S(2)}, u32[]{:S(2)}) async-start(f32[8,4,256]{2,1,0:T(4,128)} %all_to_all.29), calls=%async_computation | async-start | bytes 65536 | tf_op jit(solution)/shard_map/all_to_all | solution.py:482
  17.9 92.2 %all-gather.5.cloned.1.call-start = ((), (), s32[]{:S(2)}) async-start(), calls=%async_computation.8 | async-start | bytes 2621440 | tf_op jit(solution)/shard_map/all_gather | solution.py:526
  38.1 17.9 %collective-permute-start.3 = (bf16[256,2048]{1,0:T(8,128)(2,1)S(1)}, bf16[256,2048]{1,0:T(8,128)(2,1)S(1)}, u32[]{:S(2)}, u32[]{:S(2)}) collective-permute-start(bf16[256,2048]{1,0:T(8,128)(2,1)S(1)} %collective-permute-done.1.refs_2_), channel_id=1, source_target_pairs={{0,4},{4,0},{8,12},{12,8},{16,20},{20,16},{24,28},{28,24},{1,5},{5... | collective-permute-start | bytes 3145736 | tf_op jit(solution)/shard_map/ppermute | solution.py:352
  38.3 17.6 %collective-permute-start.4 = (bf16[256,2048]{1,0:T(8,128)(2,1)S(1)}, bf16[256,2048]{1,0:T(8,128)(2,1)}, u32[]{:S(2)}, u32[]{:S(2)}) collective-permute-start(bf16[256,2048]{1,0:T(8,128)(2,1)S(1)} %collective-permute-done.2.refs_4_), channel_id=1, source_target_pairs={{0,4},{4,0},{8,12},{12,8},{16,20},{20,16},{24,28},{28,24},{1,5},{5... | collective-permute-start | bytes 3145736 | tf_op jit(solution)/shard_map/ppermute | solution.py:352
  40.4 14.2 %collective-permute-start.5 = (bf16[128,2048]{1,0:T(8,128)(2,1)}, bf16[128,2048]{1,0:T(8,128)(2,1)S(1)}, u32[]{:S(2)}, u32[]{:S(2)}) collective-permute-start(bf16[128,2048]{1,0:T(8,128)(2,1)} %slice.20), channel_id=1, source_target_pairs={{0,16},{4,20},{8,24},{12,28},{16,0},{20,4},{24,8},{28,12},{1,17},{... | collective-permute-start | bytes 1572872 | tf_op jit(solution)/shard_map/ppermute | solution.py:352
  41.9 14.0 %collective-permute-start.6 = (bf16[128,2048]{1,0:T(8,128)(2,1)}, bf16[128,2048]{1,0:T(8,128)(2,1)}, u32[]{:S(2)}, u32[]{:S(2)}) collective-permute-start(bf16[128,2048]{1,0:T(8,128)(2,1)} %slice.21), channel_id=1, source_target_pairs={{0,8},{4,12},{8,0},{12,4},{16,24},{20,28},{24,16},{28,20},{1,9},{5... | collective-permute-start | bytes 1572872 | tf_op jit(solution)/shard_map/ppermute | solution.py:352
  59.0 20.5 %collective-permute-start.9 = (bf16[2048,512]{1,0:T(8,128)(2,1)}, bf16[2048,512]{1,0:T(8,128)(2,1)}, u32[]{:S(2)}, u32[]{:S(2)}) collective-permute-start(bf16[2048,512]{1,0:T(8,128)(2,1)} %all-gather.3.cloned.1.call-done.refs_10_.refs_0_), channel_id=1, source_target_pairs={{0,4},{4,0},{8,12},{12,8},{16,20},{20,16},{24,28},{28,24},{1,5},{5... | collective-permute-start | bytes 6291464 | tf_op jit(solution)/shard_map/ppermute | solution.py:352
  59.2 20.4 %all-to-all-start.1 = ((bf16[8,256,256]{2,1,0:T(8,128)(2,1)}), bf16[8,256,256]{2,1,0:T(8,128)(2,1)}, u32[]{:S(2)}, u32[]{:S(2)}) async-start(bf16[8,256,256]{2,1,0:T(8,128)(2,1)} %bitcast.16), calls=%async_computation.1 | async-start | bytes 2097152 | tf_op jit(solution)/shard_map/all_to_all | solution.py:530
  79.6 19.3 %all-to-all-start.2 = ((bf16[8,256,256]{2,1,0:T(8,128)(2,1)}), bf16[8,256,256]{2,1,0:T(8,128)(2,1)S(1)}, u32[]{:S(2)}, u32[]{:S(2)}) async-start(bf16[8,256,256]{2,1,0:T(8,128)(2,1)} %bitcast.27), calls=%async_computation.2 | async-start | bytes 2097152 | tf_op jit(solution)/shard_map/all_to_all | solution.py:556
  98.9 18.9 %all-to-all-start.3 = ((bf16[8,32,2048]{2,1,0:T(8,128)(2,1)}), bf16[8,32,2048]{2,1,0:T(8,128)(2,1)S(1)}, u32[]{:S(2)}, u32[]{:S(2)}) async-start(bf16[8,32,2048]{2,1,0:T(8,128)(2,1)} %bitcast.26), calls=%async_computation.3 | async-start | bytes 2097152 | tf_op jit(solution)/shard_map/all_to_all | solution.py:597
  102.4 42.1 %reduce-scatter.2.cloned.1.call-start = ((), (), s32[]{:S(2)}) async-start(), calls=%async_computation.9 | async-start | bytes 1310720 | tf_op jit(solution)/shard_map/reduce_scatter | solution.py:599
  117.8 26.8 %collective-permute-start.13 = (bf16[2048,512]{1,0:T(8,128)(2,1)}, bf16[2048,512]{1,0:T(8,128)(2,1)}, u32[]{:S(2)}, u32[]{:S(2)}) collective-permute-start(bf16[2048,512]{1,0:T(8,128)(2,1)} %all-gather.5.cloned.1.call-done.refs_2_), channel_id=1, source_target_pairs={{0,4},{4,0},{8,12},{12,8},{16,20},{20,16},{24,28},{28,24},{1,5},{5... | collective-permute-start | bytes 6291464 | tf_op jit(solution)/shard_map/ppermute | solution.py:352
  117.8 14.7 %collective-permute-start.16 = (bf16[2048,128]{1,0:T(8,128)(2,1)S(1)}, bf16[2048,128]{1,0:T(8,128)(2,1)S(1)}, u32[]{:S(2)}, u32[]{:S(2)}) collective-permute-start(bf16[2048,128]{1,0:T(8,128)(2,1)S(1)} %slice.23), channel_id=1, source_target_pairs={{0,16},{4,20},{8,24},{12,28},{16,0},{20,4},{24,8},{28,12},{1,17},{... | collective-permute-start | bytes 1572872 | tf_op jit(solution)/shard_map/ppermute | solution.py:352
  118.3 14.8 %collective-permute-start.14 = (bf16[2048,128]{1,0:T(8,128)(2,1)S(1)}, bf16[2048,128]{1,0:T(8,128)(2,1)S(1)}, u32[]{:S(2)}, u32[]{:S(2)}) collective-permute-start(bf16[2048,128]{1,0:T(8,128)(2,1)S(1)} %slice.23), channel_id=1, source_target_pairs={{0,8},{4,12},{8,0},{12,4},{16,24},{20,28},{24,16},{28,20},{1,9},{5... | collective-permute-start | bytes 1572872 | tf_op jit(solution)/shard_map/ppermute | solution.py:352
  121.7 24.8 %all-to-all-start.4 = ((bf16[8,288,256]{2,1,0:T(8,128)(2,1)}), bf16[8,288,256]{2,1,0:T(8,128)(2,1)S(1)}, u32[]{:S(2)}, u32[]{:S(2)}) async-start(bf16[8,288,256]{2,1,0:T(8,128)(2,1)} %get-tuple-element.164), calls=%async_computation.5 | async-start | bytes 2359296 | tf_op jit(solution)/shard_map/all_to_all | solution.py:618
  132.5 11.2 %collective-permute-start.17 = (bf16[2048,128]{1,0:T(8,128)(2,1)S(1)}, bf16[2048,128]{1,0:T(8,128)(2,1)S(1)}, u32[]{:S(2)}, u32[]{:S(2)}) collective-permute-start(bf16[2048,128]{1,0:T(8,128)(2,1)S(1)} %collective-permute-done.16.refs_4_), channel_id=1, source_target_pairs={{0,4},{4,0},{8,12},{12,8},{16,20},{20,16},{24,28},{28,24},{1,5},{5... | collective-permute-start | bytes 1572872 | tf_op jit(solution)/shard_map/ppermute | solution.py:352
  133.1 11.5 %collective-permute-start.15 = (bf16[2048,128]{1,0:T(8,128)(2,1)S(1)}, bf16[2048,128]{1,0:T(8,128)(2,1)S(1)}, u32[]{:S(2)}, u32[]{:S(2)}) collective-permute-start(bf16[2048,128]{1,0:T(8,128)(2,1)S(1)} %collective-permute-done.14.refs_3_), channel_id=1, source_target_pairs={{0,4},{4,0},{8,12},{12,8},{16,20},{20,16},{24,28},{28,24},{1,5},{5... | collective-permute-start | bytes 1572872 | tf_op jit(solution)/shard_map/ppermute | solution.py:352
  134.7 8.5 %collective-permute-start.11 = (bf16[8,16,128]{2,1,0:T(8,128)(2,1)}, bf16[8,16,128]{2,1,0:T(8,128)(2,1)S(1)}, u32[]{:S(2)}, u32[]{:S(2)}) collective-permute-start(bf16[8,16,128]{2,1,0:T(8,128)(2,1)} %get-tuple-element.156), channel_id=1, source_target_pairs={{0,2},{1,3},{2,0},{3,1},{4,6},{5,7},{6,4},{7,5},{8,10},{9,11},{10,... | collective-permute-start | bytes 98312 | tf_op jit(solution)/shard_map/ppermute | solution.py:352
  137.8 5.9 %collective-permute-start.12 = (bf16[8,16,128]{2,1,0:T(8,128)(2,1)}, bf16[8,16,128]{2,1,0:T(8,128)(2,1)S(1)}, u32[]{:S(2)}, u32[]{:S(2)}) collective-permute-start(bf16[8,16,128]{2,1,0:T(8,128)(2,1)} %get-tuple-element.157), channel_id=1, source_target_pairs={{0,3},{1,2},{2,1},{3,0},{4,7},{5,6},{6,5},{7,4},{8,11},{9,10},{10,... | collective-permute-start | bytes 98312 | tf_op jit(solution)/shard_map/ppermute | solution.py:352
  146.5 11.4 %all-to-all-start.5 = ((bf16[8,80,256]{2,1,0:T(8,128)(2,1)}), bf16[8,80,256]{2,1,0:T(8,128)(2,1)S(1)}, u32[]{:S(2)}, u32[]{:S(2)}) async-start(bf16[8,80,256]{2,1,0:T(8,128)(2,1)} %shard_map.75), calls=%async_computation.6 | async-start | bytes 655360 | tf_op jit(solution)/shard_map/all_to_all | solution.py:671
  (22 other events, 140.4 us)
Sparse Core Ops, SparseCore 0:
  9.6 48.4 all-gather.2
  59.6 45.7 all-gather.4
  110.2 28.7 reduce-scatter.1

commit v7 on v6

--- a/solution.py
+++ b/solution.py
@@ -61,7 +61,8 @@
 def forward_kernel(sources, arrays, slots, group, heads, head_size, place_ref, *refs):
     array_refs, refs = refs[:arrays], refs[arrays:]
     in_hbm, out_hbm, refs = refs[:7], refs[7:14], refs[14:]
-    in_refs, out_refs, (held, mean_ref, carry, sems, loads, stores) = refs[:7], refs[7:14], refs[14:]
+    in_refs, out_refs, refs = refs[:7], refs[7:14], refs[14:]
+    held, mean_ref, carry, y_ref, sems, loads, stores, y_sems = refs
     w_ref, m_ref, te_ref, fs_ref, en_ref, lv_ref, dt_ref = in_refs
     x_ref, b_ref, c_ref, z_ref, rs_ref, sf_ref, rn_ref = out_refs
     pieces = len(sources)
@@ -133,17 +134,27 @@
         y = dot_nn(weights, by_head(x, heads, head_size))
         y = y + en_ref[rows, :].astype(f32) * dot_nn(c, state_in)
         y = y + lv_ref[rows, :].astype(f32) * dot_nn(c, rn_ref[state, :])
+        y_ref[rows, :] = y
+        carry[...] = dt_ref[k] * carry[...] + dot_tn(b, x * te_ref[rows, :])
+        return 0
+
+    lax.fori_loop(0, chunks, outputs, 0, unroll=16)
+    out_stores[5].start()
+    block_stores = []
+    block = y_ref.shape[0] // (y_sems.shape[0] // 2)
+    for n in range(y_sems.shape[0] // 2):
+        rows = pl.ds(n * block, block)
+        y = y_ref[rows, :]
         mean_square = dot_nn((y * y).astype(bf16), mean_ref[...])
         inverse = lax.rsqrt(mean_square + EPSILON)
         z_ref[rows, :] = (y * inverse).astype(bf16)
         rs_ref[rows, :] = inverse.astype(bf16)
-        carry[...] = dt_ref[k] * carry[...] + dot_tn(b, x * te_ref[rows, :])
-        return 0
-
-    lax.fori_loop(0, chunks, outputs, 0, unroll=16)
-    for store in out_stores[3:6]:
-        store.start()
-    for store in out_stores:
+        for m in (3, 4):
+            source, target = out_refs[m].at[rows], out_hbm[m].at[rows]
+            store = pltpu.make_async_copy(source, target, y_sems.at[2 * n + m - 3])
+            store.start()
+            block_stores.append(store)
+    for store in out_stores[:3] + out_stores[5:] + block_stores:
         store.wait()
 
 
@@ -256,6 +267,43 @@
     for lhs_ref, column_ref in zip(lhs_refs[1:], column_refs[1:]):
         result = result + dot_nt(lhs_ref[...], column_ref[:, : lhs_ref.shape[1]])
     out_ref[0] = result.astype(bf16)
+
+
+def joined_tokens_kernel(layout, steps, place_ref, packed_ref, *refs):
+    arrays = len(layout)
+    column_refs, out_ref, joined_ref, lhs_ref, sems = refs[:arrays], *refs[arrays:]
+    count = packed_ref.shape[0]
+    tokens = out_ref.shape[1]
+    rows = joined_ref.shape[1]
+    width = layout[0][0][2]
+    part = (joined_ref.shape[2] - count * width) // count
+    loads = []
+    for step in range(steps):
+        column = 0
+        for n, parts in enumerate(layout):
+            extent = sum(p[2] for p in parts) + (count * part if n == 0 else 0)
+            source = column_refs[n].at[pl.ds(step * rows, rows), pl.ds(0, extent)]
+            target = joined_ref.at[step, :, pl.ds(column, extent)]
+            loads.append(pltpu.make_async_copy(source, target, sems.at[step * arrays + n]))
+            loads[-1].start()
+            column += extent
+
+    column = 0
+    for n, parts in enumerate(layout):
+        for r, start, extent in parts:
+            source = lax.bitwise_xor(place_ref[0], r)
+            block = packed_ref[source, :tokens, start : start + extent]
+            lhs_ref[:, column : column + extent] = block
+            column += extent
+        if n == 0:
+            turned = [packed_ref[m, tokens : tokens + part, :tokens] for m in range(count)]
+            lhs_ref[:, column : column + count * part] = jnp.concatenate(turned, axis=0).T
+            column += count * part
+    for step in range(steps):
+        for load in loads[step * arrays : (step + 1) * arrays]:
+            load.wait()
+        result = dot_nt(lhs_ref[...], joined_ref[step])
+        out_ref[0, :, step * rows : (step + 1) * rows] = result.astype(bf16)
 
 
 def spread_kernel(blocks_ref, out_ref):
@@ -537,11 +585,12 @@
         out_shape=kept,
         in_specs=scalar + in_hbm * (len(arrays) + 7),
         out_specs=in_hbm * 7,
-        scratch_shapes=scratch(*operands, *kept, held, mean, carry)
+        scratch_shapes=scratch(*operands, *kept, held, mean, carry, shape((length, width), f32))
         + [
             pltpu.SemaphoreType.DMA((slots,)),
             pltpu.SemaphoreType.DMA((7,)),
             pltpu.SemaphoreType.DMA((7,)),
+            pltpu.SemaphoreType.DMA((8,)),
         ],
         compiler_params=params,
         cost_estimate=cost(
@@ -634,9 +683,6 @@
     )
 
     grad_tokens_shape = shape((1, token_count, hidden_width), bf16)
-    steps = 2
-    rows = hidden_width // steps
-    by_rows = lambda a: pl.BlockSpec((rows, a.shape[1]), lambda k: (k, 0))
     layout = [[(r, 0, width) for r in others] + [(r, 0, first_part) for r in neighbours]]
     layout += [[(r, first_part, width - first_part)] for r in neighbours]
     odd_layout = [[(r + 1, start, extent) for r, start, extent in parts] for parts in layout]
@@ -646,19 +692,38 @@
         for n, parts in enumerate(layout)
     ]
     w_blocks = [w_columns, w_partner, *w_even, *w_odd]
-    grad_tokens = pl.pallas_call(
-        functools.partial(tokens_kernel, layout),
-        grid=(steps,),
-        out_shape=grad_tokens_shape,
-        in_specs=scalar + [resident(grad_blocks)] + [by_rows(a) for a in w_blocks],
-        out_specs=pl.BlockSpec((1, token_count, rows), lambda k: (0, 0, k)),
-        scratch_shapes=scratch(*lhs_shapes),
-        compiler_params=params,
-        cost_estimate=cost(
-            4 * token_count * hidden_width * (inner_width + shared),
-            4 * hidden_width * (inner_width + shared),
-        ),
-    )(places, grad_blocks, *w_blocks)
+    tokens_cost = cost(
+        4 * token_count * hidden_width * (inner_width + shared),
+        4 * hidden_width * (inner_width + shared),
+    )
+    if all(extent % 128 == 0 for parts in layout for _, _, extent in parts):
+        steps = 4
+        joined = shape((steps, hidden_width // steps, inner_width + shared), bf16)
+        grad_tokens = pl.pallas_call(
+            functools.partial(joined_tokens_kernel, layout, steps),
+            grid=(1,),
+            out_shape=grad_tokens_shape,
+            in_specs=scalar + [resident(grad_blocks)] + in_hbm * len(w_blocks),
+            out_specs=resident(grad_tokens_shape),
+            scratch_shapes=scratch(joined, shape((token_count, inner_width + shared), bf16))
+            + [pltpu.SemaphoreType.DMA((steps * len(w_blocks),))],
+            compiler_params=params,
+            cost_estimate=tokens_cost,
+        )(places, grad_blocks, *w_blocks)
+    else:
+        steps = 2
+        rows = hidden_width // steps
+        by_rows = lambda a: pl.BlockSpec((rows, a.shape[1]), lambda k: (k, 0))
+        grad_tokens = pl.pallas_call(
+            functools.partial(tokens_kernel, layout),
+            grid=(steps,),
+            out_shape=grad_tokens_shape,
+            in_specs=scalar + [resident(grad_blocks)] + [by_rows(a) for a in w_blocks],
+            out_specs=pl.BlockSpec((1, token_count, rows), lambda k: (0, 0, k)),
+            scratch_shapes=scratch(*lhs_shapes),
+            compiler_params=params,
+            cost_estimate=tokens_cost,
+        )(places, grad_blocks, *w_blocks)
     packed = shape((seq_count, rows_each + extra, width), bf16)
     packed_sums = pl.pallas_call(
         add_kernel,

time: 168 us -> 167 us (level)
  Pallas kernels: 67 us -> 65 us
  transfers between devices with their start and end apart: 27 -> 27, of which waited for: 11 -> 12; matrix products, arithmetic and copies ran while one was open for 5% -> 5% of each run, Pallas kernels for 39% -> 38%
where the time goes in v7:
time: 167 us; the launch traced here: 166 us
  Pallas kernels  65 us (39%)
  starting transfers between devices  38.8 us (23%)
  waiting for transfers between devices  34.5 us (21%)
  between operations  14.1 us (8%)
  local copies, waits for them, and re-layouts  11 us (7%)
  other arithmetic  2.35 us (1%)
    ppermute x18, starting transfers between devices, permute_xor(): return lax.ppermute(a, axis, [(i, i ^ mask) for i in range(count)])  16.3 us
    all_to_all x1, waiting for transfers between devices, on_device(): log_rates = lax.all_to_all(log_decay[0], 'seq', 0, 1, tiled=True)  14.6 us
    pallas_call x1, Pallas kernels, on_device(): pl.pallas_call(functools.partial(forward_kernel, sources, len(arrays), sl...  14.5 us
    pallas_call x1, Pallas kernels, on_device(): pl.pallas_call(functools.partial(backward_kernel, heads, head_size), out_...  12.7 us
    pallas_call x2, Pallas kernels, weight_columns(): pl.pallas_call(functools.partial(weight_kernel, sources, len(arrays), slo...  12.4 us
    pallas_call x1, Pallas kernels, on_device(): make_tables(log_rates)  9.15 us
    ppermute x18, waiting for transfers between devices, permute_xor(): return lax.ppermute(a, axis, [(i, i ^ mask) for i in range(count)])  9.03 us
    all_to_all x1, waiting for transfers between devices, on_device(): lax.all_to_all(shared_partial.reshape(seq_count, part, length), 'seq', 0, 0)  7.64 us
  transfers between devices with their start and end apart: 27, of which 12 were waited for; matrix products, arithmetic and copies ran while one was open for 5% of the time, Pallas kernels for 38%

profile of v7, /device:TPU:0, one launch (start us, length us, event | category | flops | bytes accessed | tf_op | source)
XLA Modules:
  0.0 165.7 jit_solution(17655497849473794210)
XLA Ops:
  9.9 2.6 %collective-permute-start.1 = (bf16[256,2048]{1,0:T(8,128)(2,1)S(1)}, bf16[256,2048]{1,0:T(8,128)(2,1)S(1)}, u32[]{:S(2)}, u32[]{:S(2)}) collective-permute-start(bf16[256,2048]{1,0:T(8,128)(2,1)S(1)} %bitcast.22), channel_id=1, source_target_pairs={{0,8},{4,12},{8,0},{12,4},{16,24},{20,28},{24,16},{28,20},{1,9},{5... | collective-permute-start | bytes 3145736 | tf_op jit(solution)/shard_map/ppermute | solution.py:400
  14.6 3.3 %all-to-all-start = ((f32[8,4,256]{2,1,0:T(4,128)}), f32[8,4,256]{2,1,0:T(4,128)S(1)}, u32[]{:S(2)}, u32[]{:S(2)}) async-start(f32[8,4,256]{2,1,0:T(4,128)} %all_to_all.29), calls=%async_computation | async-start | bytes 65536 | tf_op jit(solution)/shard_map/all_to_all | solution.py:530
  20.6 1.6 copy.10
  23.4 14.6 %all-to-all-done = f32[8,4,256]{2,1,0:T(4,128)S(1)} async-done(((f32[8,4,256]{2,1,0:T(4,128)}), f32[8,4,256]{2,1,0:T(4,128)S(1)}, u32[]{:S(2)}, u32[]{:S(2)}) %all-to-all-start) | async-done | bytes 32800 | tf_op jit(solution)/shard_map/all_to_all | solution.py:530
  42.4 9.1 %shard_map.67 = (bf16[2048,256]{1,0:T(8,128)(2,1)}, bf16[2048,256]{1,0:T(8,128)(2,1)}, bf16[2048,256]{1,0:T(8,128)(2,1)}, bf16[2048,256]{1,0:T(8,128)(2,1)}, f32...) custom-call(f32[4,2048]{1,0:T(4,128)} %bitcast.29), custom_call_target="tpu_custom_call" | custom-call | bytes 62914560 | tf_op jit(solution)/shard_map/pallas_call | solution.py:560
  51.6 3.0 %collective-permute-done.5.refs_6_ = bf16[128,2048]{1,0:T(8,128)(2,1)S(1)} collective-permute-done((bf16[128,2048]{1,0:T(8,128)(2,1)}, bf16[128,2048]{1,0:T(8,128)(2,1)S(1)}, u32[]{:S(2)}, u32[]{:S(2)}) %collective-permute-start.5) | collective-permute-done | bytes 524320 | tf_op jit(solution)/shard_map/ppermute | solution.py:400
  59.2 4.4 %all-to-all-start.1 = ((bf16[8,256,256]{2,1,0:T(8,128)(2,1)}), bf16[8,256,256]{2,1,0:T(8,128)(2,1)}, u32[]{:S(2)}, u32[]{:S(2)}) async-start(bf16[8,256,256]{2,1,0:T(8,128)(2,1)} %bitcast.16), calls=%async_computation.1 | async-start | bytes 2097152 | tf_op jit(solution)/shard_map/all_to_all | solution.py:578
  63.7 14.5 %shard_map.68 = (bf16[2048,256]{1,0:T(8,128)(2,1)}, bf16[2048,128]{1,0:T(8,128)(2,1)}, bf16[2048,128]{1,0:T(8,128)(2,1)}, bf16[2048,256]{1,0:T(8,128)(2,1)}, bf1...) custom-call(s32[2]{0:T(128)} %pad_add_fusion.place_ref.places_ref, ...), custom_call_target="tpu_custom_call" | custom-call | flops 19327352832 | bytes 16777216 | tf_op jit(solution)/shard_map/pallas_call | solution.py:581
  78.9 3.8 %all-to-all-start.2 = ((bf16[8,256,256]{2,1,0:T(8,128)(2,1)}), bf16[8,256,256]{2,1,0:T(8,128)(2,1)S(1)}, u32[]{:S(2)}, u32[]{:S(2)}) async-start(bf16[8,256,256]{2,1,0:T(8,128)(2,1)} %bitcast.27), calls=%async_computation.2 | async-start | bytes 2097152 | tf_op jit(solution)/shard_map/all_to_all | solution.py:605
  82.7 12.7 %shard_map.69 = (bf16[2048,256]{1,0:T(8,128)(2,1)}, bf16[256,2048]{1,0:T(8,128)(2,1)}) custom-call(bf16[2048,256]{1,0:T(8,128)(2,1)} %bitcast.6.refs_0_, bf16[2048,256]{1,0:T(8,128)(2,1)} %get-tuple-element.138.refs_1_, bf16[2048,256]{1,0:T(8,128)(2,1)} %get-tuple-element.139.refs_2_, bf16[2048,128]{1,0:T(8,128)(2,1)} %get-tuple-element.140.refs_3_, ...), custom_call_target="tpu_custom_call" | custom-call | flops 16106127360 | bytes 20971520 | tf_op jit(solution)/shard_map/pallas_call | solution.py:611
  95.4 2.4 %all-to-all-done.2.blocks_ref = bf16[8,256,256]{2,1,0:T(8,128)(2,1)S(1)} async-done(((bf16[8,256,256]{2,1,0:T(8,128)(2,1)}), bf16[8,256,256]{2,1,0:T(8,128)(2,1)S(1)}, u32[]{:S(2)}, u32[]{:S(2)}) %all-to-all-start.2) | async-done | bytes 1048608 | tf_op jit(solution)/shard_map/all_to_all | solution.py:605
  97.8 3.6 %all-to-all-start.3 = ((bf16[8,32,2048]{2,1,0:T(8,128)(2,1)}), bf16[8,32,2048]{2,1,0:T(8,128)(2,1)S(1)}, u32[]{:S(2)}, u32[]{:S(2)}) async-start(bf16[8,32,2048]{2,1,0:T(8,128)(2,1)} %bitcast.26), calls=%async_computation.3 | async-start | bytes 2097152 | tf_op jit(solution)/shard_map/all_to_all | solution.py:646
  101.4 6.5 %shard_map.70 = bf16[4,8,64,256]{3,2,1,0:T(8,128)(2,1)} custom-call(s32[2]{0:T(128)} %pad_add_fusion.place_ref.places_ref, bf16[256,2048]{1,0:T(8,128)(2,1)} %bitcast.19, bf16[256,2048]{1,0:T(8,128)(2,1)} %collective-permute-done.refs_1_, bf16[256,2048]{1,0:T(8,128)(2,1)} %copy-done.2, bf16[256,2048]{1,0:T(8,128)(2,1)} %copy-done.7, ...), custom_call_target="tpu_custom_call" | custom-call | flops 4294967296 | bytes 16777216 | tf_op jit(solution)/shard_map/pallas_call | solution.py:634
  109.1 7.6 %all-to-all-done.3.parts_ref = bf16[8,32,2048]{2,1,0:T(8,128)(2,1)S(1)} async-done(((bf16[8,32,2048]{2,1,0:T(8,128)(2,1)}), bf16[8,32,2048]{2,1,0:T(8,128)(2,1)S(1)}, u32[]{:S(2)}, u32[]{:S(2)}) %all-to-all-start.3) | async-done | bytes 1048608 | tf_op jit(solution)/shard_map/all_to_all | solution.py:646
  117.9 2.8 %shard_map.71 = (bf16[32,2048]{1,0:T(8,128)(2,1)}, bf16[8,288,256]{2,1,0:T(8,128)(2,1)}) custom-call(bf16[8,32,2048]{2,1,0:T(8,128)(2,1)} %copy-done.1, bf16[2048,256]{1,0:T(8,128)(2,1)} %get-tuple-element.149.refs_10_.dx_ref), custom_call_target="tpu_custom_call" | custom-call | tf_op jit(solution)/shard_map/pallas_call | solution.py:658
  120.7 3.6 %all-to-all-start.4 = ((bf16[8,288,256]{2,1,0:T(8,128)(2,1)}), bf16[8,288,256]{2,1,0:T(8,128)(2,1)S(1)}, u32[]{:S(2)}, u32[]{:S(2)}) async-start(bf16[8,288,256]{2,1,0:T(8,128)(2,1)} %get-tuple-element.164), calls=%async_computation.5 | async-start | bytes 2359296 | tf_op jit(solution)/shard_map/all_to_all | solution.py:667
  124.3 5.9 %shard_map.72 = (bf16[8,16,128]{2,1,0:T(8,128)(2,1)}, bf16[8,16,128]{2,1,0:T(8,128)(2,1)}, bf16[8,16,128]{2,1,0:T(8,128)(2,1)}, bf16[8,16,128]{2,1,0:T(8,128)(2,1)}) custom-call(s32[2]{0:T(128)} %pad_add_fusion.place_ref.places_ref, bf16[256,2048]{1,0:T(8,128)(2,1)} %bitcast.20, bf16[256,2048]{1,0:T(8,128)(2,1)} %collective-permute-done.refs_1_, ...), custom_call_target="tpu_custom_call" | custom-call | flops 536870912 | bytes 16777216 | tf_op jit(solution)/shard_map/pallas_call | solution.py:634
  133.6 2.6 %collective-permute-start.11 = (bf16[8,16,128]{2,1,0:T(8,128)(2,1)}, bf16[8,16,128]{2,1,0:T(8,128)(2,1)S(1)}, u32[]{:S(2)}, u32[]{:S(2)}) collective-permute-start(bf16[8,16,128]{2,1,0:T(8,128)(2,1)} %get-tuple-element.156), channel_id=1, source_target_pairs={{0,2},{1,3},{2,0},{3,1},{4,6},{5,7},{6,4},{7,5},{8,10},{9,11},{10,... | collective-permute-start | bytes 98312 | tf_op jit(solution)/shard_map/ppermute | solution.py:400
  136.7 3.0 %collective-permute-start.12 = (bf16[8,16,128]{2,1,0:T(8,128)(2,1)}, bf16[8,16,128]{2,1,0:T(8,128)(2,1)S(1)}, u32[]{:S(2)}, u32[]{:S(2)}) collective-permute-start(bf16[8,16,128]{2,1,0:T(8,128)(2,1)} %get-tuple-element.157), channel_id=1, source_target_pairs={{0,3},{1,2},{2,1},{3,0},{4,7},{5,6},{6,5},{7,4},{8,11},{9,10},{10,... | collective-permute-start | bytes 98312 | tf_op jit(solution)/shard_map/ppermute | solution.py:400
  139.7 2.3 %shard_map.73 = bf16[1,256,2048]{2,1,0:T(8,128)(2,1)} custom-call(bf16[8,256,256]{2,1,0:T(8,128)(2,1)} %copy-done), custom_call_target="tpu_custom_call" | custom-call | tf_op jit(solution)/shard_map/pallas_call | solution.py:671
  143.5 1.9 %shard_map.75 = bf16[8,80,256]{2,1,0:T(8,128)(2,1)} custom-call(bf16[8,64,256]{2,1,0:T(8,128)(2,1)} %bitcast.28, bf16[8,16,128]{2,1,0:T(8,128)(2,1)} %get-tuple-element.170.refs_1_, bf16[8,16,128]{2,1,0:T(8,128)(2,1)} %copy-done.11, bf16[8,16,128]{2,1,0:T(8,128)(2,1)} %copy-done.12, bf16[8,16,128]{2,1,0:T(8,128)(2,1)} %copy-done.13), custom_call_target="tpu_custom_call" | custom-call | tf_op jit(solution)/shard_map/pallas_call | solution.py:728
  145.4 3.7 %all-to-all-start.5 = ((bf16[8,80,256]{2,1,0:T(8,128)(2,1)}), bf16[8,80,256]{2,1,0:T(8,128)(2,1)S(1)}, u32[]{:S(2)}, u32[]{:S(2)}) async-start(bf16[8,80,256]{2,1,0:T(8,128)(2,1)} %shard_map.75), calls=%async_computation.6 | async-start | bytes 655360 | tf_op jit(solution)/shard_map/all_to_all | solution.py:736
  149.2 7.4 %shard_map.74 = bf16[1,256,2048]{2,1,0:T(8,128)(2,1)} custom-call(s32[2]{0:T(128)} %pad_add_fusion.place_ref.places_ref, bf16[8,288,256]{2,1,0:T(8,128)(2,1)} %copy-done.5, bf16[2048,512]{1,0:T(8,128)(2,1)} %all-gather.3.cloned.1.call-done.refs_10_.refs_0_, bf16[2048,512]{1,0:T(8,128)(2,1)} %collective-permute-done.9.refs_1_, ...), custom_call_target="tpu_custom_call" | custom-call | flops 4831838208 | bytes 18874368 | tf_op jit(solution)/shard_map/pallas_call | solution.py:702
  157.3 1.9 %shard_map.76 = f32[64,2304]{1,0:T(8,128)} custom-call(bf16[8,80,256]{2,1,0:T(8,128)(2,1)} %copy-done.4), custom_call_target="tpu_custom_call" | custom-call | tf_op jit(solution)/shard_map/pallas_call | solution.py:738
  (92 shorter events, 26.8 us)
Async XLA Ops:
  7.2 51.8 %all-gather.3.cloned.1.call-start = ((), (), s32[]{:S(2)}) async-start(), calls=%async_computation.7 | async-start | bytes 2621440 | tf_op jit(solution)/shard_map/all_gather | solution.py:527
  9.4 28.7 %collective-permute-start = (bf16[256,2048]{1,0:T(8,128)(2,1)S(1)}, bf16[256,2048]{1,0:T(8,128)(2,1)}, u32[]{:S(2)}, u32[]{:S(2)}) collective-permute-start(bf16[256,2048]{1,0:T(8,128)(2,1)S(1)} %bitcast.21), channel_id=1, source_target_pairs={{0,4},{4,0},{8,12},{12,8},{16,20},{20,16},{24,28},{28,24},{1,5},{5... | collective-permute-start | bytes 3145736 | tf_op jit(solution)/shard_map/ppermute | solution.py:400
  9.9 28.2 %collective-permute-start.1 = (bf16[256,2048]{1,0:T(8,128)(2,1)S(1)}, bf16[256,2048]{1,0:T(8,128)(2,1)S(1)}, u32[]{:S(2)}, u32[]{:S(2)}) collective-permute-start(bf16[256,2048]{1,0:T(8,128)(2,1)S(1)} %bitcast.22), channel_id=1, source_target_pairs={{0,8},{4,12},{8,0},{12,4},{16,24},{20,28},{24,16},{28,20},{1,9},{5... | collective-permute-start | bytes 3145736 | tf_op jit(solution)/shard_map/ppermute | solution.py:400
  12.4 25.6 %collective-permute-start.2 = (bf16[256,2048]{1,0:T(8,128)(2,1)S(1)}, bf16[256,2048]{1,0:T(8,128)(2,1)S(1)}, u32[]{:S(2)}, u32[]{:S(2)}) collective-permute-start(bf16[256,2048]{1,0:T(8,128)(2,1)S(1)} %bitcast.23), channel_id=1, source_target_pairs={{0,16},{4,20},{8,24},{12,28},{16,0},{20,4},{24,8},{28,12},{1,17},{... | collective-permute-start | bytes 3145736 | tf_op jit(solution)/shard_map/ppermute | solution.py:400
  14.6 23.4 %all-to-all-start = ((f32[8,4,256]{2,1,0:T(4,128)}), f32[8,4,256]{2,1,0:T(4,128)S(1)}, u32[]{:S(2)}, u32[]{:S(2)}) async-start(f32[8,4,256]{2,1,0:T(4,128)} %all_to_all.29), calls=%async_computation | async-start | bytes 65536 | tf_op jit(solution)/shard_map/all_to_all | solution.py:530
  17.9 91.1 %all-gather.5.cloned.1.call-start = ((), (), s32[]{:S(2)}) async-start(), calls=%async_computation.8 | async-start | bytes 2621440 | tf_op jit(solution)/shard_map/all_gather | solution.py:574
  38.1 17.9 %collective-permute-start.3 = (bf16[256,2048]{1,0:T(8,128)(2,1)S(1)}, bf16[256,2048]{1,0:T(8,128)(2,1)S(1)}, u32[]{:S(2)}, u32[]{:S(2)}) collective-permute-start(bf16[256,2048]{1,0:T(8,128)(2,1)S(1)} %collective-permute-done.1.refs_2_), channel_id=1, source_target_pairs={{0,4},{4,0},{8,12},{12,8},{16,20},{20,16},{24,28},{28,24},{1,5},{5... | collective-permute-start | bytes 3145736 | tf_op jit(solution)/shard_map/ppermute | solution.py:400
  38.3 17.6 %collective-permute-start.4 = (bf16[256,2048]{1,0:T(8,128)(2,1)S(1)}, bf16[256,2048]{1,0:T(8,128)(2,1)}, u32[]{:S(2)}, u32[]{:S(2)}) collective-permute-start(bf16[256,2048]{1,0:T(8,128)(2,1)S(1)} %collective-permute-done.2.refs_4_), channel_id=1, source_target_pairs={{0,4},{4,0},{8,12},{12,8},{16,20},{20,16},{24,28},{28,24},{1,5},{5... | collective-permute-start | bytes 3145736 | tf_op jit(solution)/shard_map/ppermute | solution.py:400
  40.4 14.2 %collective-permute-start.5 = (bf16[128,2048]{1,0:T(8,128)(2,1)}, bf16[128,2048]{1,0:T(8,128)(2,1)S(1)}, u32[]{:S(2)}, u32[]{:S(2)}) collective-permute-start(bf16[128,2048]{1,0:T(8,128)(2,1)} %slice.20), channel_id=1, source_target_pairs={{0,16},{4,20},{8,24},{12,28},{16,0},{20,4},{24,8},{28,12},{1,17},{... | collective-permute-start | bytes 1572872 | tf_op jit(solution)/shard_map/ppermute | solution.py:400
  41.9 14.0 %collective-permute-start.6 = (bf16[128,2048]{1,0:T(8,128)(2,1)}, bf16[128,2048]{1,0:T(8,128)(2,1)}, u32[]{:S(2)}, u32[]{:S(2)}) collective-permute-start(bf16[128,2048]{1,0:T(8,128)(2,1)} %slice.21), channel_id=1, source_target_pairs={{0,8},{4,12},{8,0},{12,4},{16,24},{20,28},{24,16},{28,20},{1,9},{5... | collective-permute-start | bytes 1572872 | tf_op jit(solution)/shard_map/ppermute | solution.py:400
  59.0 19.9 %collective-permute-start.9 = (bf16[2048,512]{1,0:T(8,128)(2,1)}, bf16[2048,512]{1,0:T(8,128)(2,1)}, u32[]{:S(2)}, u32[]{:S(2)}) collective-permute-start(bf16[2048,512]{1,0:T(8,128)(2,1)} %all-gather.3.cloned.1.call-done.refs_10_.refs_0_), channel_id=1, source_target_pairs={{0,4},{4,0},{8,12},{12,8},{16,20},{20,16},{24,28},{28,24},{1,5},{5... | collective-permute-start | bytes 6291464 | tf_op jit(solution)/shard_map/ppermute | solution.py:400
  59.2 19.7 %all-to-all-start.1 = ((bf16[8,256,256]{2,1,0:T(8,128)(2,1)}), bf16[8,256,256]{2,1,0:T(8,128)(2,1)}, u32[]{:S(2)}, u32[]{:S(2)}) async-start(bf16[8,256,256]{2,1,0:T(8,128)(2,1)} %bitcast.16), calls=%async_computation.1 | async-start | bytes 2097152 | tf_op jit(solution)/shard_map/all_to_all | solution.py:578
  78.9 18.9 %all-to-all-start.2 = ((bf16[8,256,256]{2,1,0:T(8,128)(2,1)}), bf16[8,256,256]{2,1,0:T(8,128)(2,1)S(1)}, u32[]{:S(2)}, u32[]{:S(2)}) async-start(bf16[8,256,256]{2,1,0:T(8,128)(2,1)} %bitcast.27), calls=%async_computation.2 | async-start | bytes 2097152 | tf_op jit(solution)/shard_map/all_to_all | solution.py:605
  97.8 18.9 %all-to-all-start.3 = ((bf16[8,32,2048]{2,1,0:T(8,128)(2,1)}), bf16[8,32,2048]{2,1,0:T(8,128)(2,1)S(1)}, u32[]{:S(2)}, u32[]{:S(2)}) async-start(bf16[8,32,2048]{2,1,0:T(8,128)(2,1)} %bitcast.26), calls=%async_computation.3 | async-start | bytes 2097152 | tf_op jit(solution)/shard_map/all_to_all | solution.py:646
  101.4 42.1 %reduce-scatter.2.cloned.1.call-start = ((), (), s32[]{:S(2)}) async-start(), calls=%async_computation.9 | async-start | bytes 1310720 | tf_op jit(solution)/shard_map/reduce_scatter | solution.py:648
  116.7 26.8 %collective-permute-start.13 = (bf16[2048,512]{1,0:T(8,128)(2,1)}, bf16[2048,512]{1,0:T(8,128)(2,1)}, u32[]{:S(2)}, u32[]{:S(2)}) collective-permute-start(bf16[2048,512]{1,0:T(8,128)(2,1)} %all-gather.5.cloned.1.call-done.refs_2_), channel_id=1, source_target_pairs={{0,4},{4,0},{8,12},{12,8},{16,20},{20,16},{24,28},{28,24},{1,5},{5... | collective-permute-start | bytes 6291464 | tf_op jit(solution)/shard_map/ppermute | solution.py:400
  116.7 14.7 %collective-permute-start.16 = (bf16[2048,128]{1,0:T(8,128)(2,1)S(1)}, bf16[2048,128]{1,0:T(8,128)(2,1)S(1)}, u32[]{:S(2)}, u32[]{:S(2)}) collective-permute-start(bf16[2048,128]{1,0:T(8,128)(2,1)S(1)} %slice.23), channel_id=1, source_target_pairs={{0,16},{4,20},{8,24},{12,28},{16,0},{20,4},{24,8},{28,12},{1,17},{... | collective-permute-start | bytes 1572872 | tf_op jit(solution)/shard_map/ppermute | solution.py:400
  117.2 14.8 %collective-permute-start.14 = (bf16[2048,128]{1,0:T(8,128)(2,1)S(1)}, bf16[2048,128]{1,0:T(8,128)(2,1)S(1)}, u32[]{:S(2)}, u32[]{:S(2)}) collective-permute-start(bf16[2048,128]{1,0:T(8,128)(2,1)S(1)} %slice.23), channel_id=1, source_target_pairs={{0,8},{4,12},{8,0},{12,4},{16,24},{20,28},{24,16},{28,20},{1,9},{5... | collective-permute-start | bytes 1572872 | tf_op jit(solution)/shard_map/ppermute | solution.py:400
  120.7 24.8 %all-to-all-start.4 = ((bf16[8,288,256]{2,1,0:T(8,128)(2,1)}), bf16[8,288,256]{2,1,0:T(8,128)(2,1)S(1)}, u32[]{:S(2)}, u32[]{:S(2)}) async-start(bf16[8,288,256]{2,1,0:T(8,128)(2,1)} %get-tuple-element.164), calls=%async_computation.5 | async-start | bytes 2359296 | tf_op jit(solution)/shard_map/all_to_all | solution.py:667
  131.4 11.2 %collective-permute-start.17 = (bf16[2048,128]{1,0:T(8,128)(2,1)S(1)}, bf16[2048,128]{1,0:T(8,128)(2,1)S(1)}, u32[]{:S(2)}, u32[]{:S(2)}) collective-permute-start(bf16[2048,128]{1,0:T(8,128)(2,1)S(1)} %collective-permute-done.16.refs_4_), channel_id=1, source_target_pairs={{0,4},{4,0},{8,12},{12,8},{16,20},{20,16},{24,28},{28,24},{1,5},{5... | collective-permute-start | bytes 1572872 | tf_op jit(solution)/shard_map/ppermute | solution.py:400
  132.0 11.5 %collective-permute-start.15 = (bf16[2048,128]{1,0:T(8,128)(2,1)S(1)}, bf16[2048,128]{1,0:T(8,128)(2,1)S(1)}, u32[]{:S(2)}, u32[]{:S(2)}) collective-permute-start(bf16[2048,128]{1,0:T(8,128)(2,1)S(1)} %collective-permute-done.14.refs_3_), channel_id=1, source_target_pairs={{0,4},{4,0},{8,12},{12,8},{16,20},{20,16},{24,28},{28,24},{1,5},{5... | collective-permute-start | bytes 1572872 | tf_op jit(solution)/shard_map/ppermute | solution.py:400
  133.6 8.5 %collective-permute-start.11 = (bf16[8,16,128]{2,1,0:T(8,128)(2,1)}, bf16[8,16,128]{2,1,0:T(8,128)(2,1)S(1)}, u32[]{:S(2)}, u32[]{:S(2)}) collective-permute-start(bf16[8,16,128]{2,1,0:T(8,128)(2,1)} %get-tuple-element.156), channel_id=1, source_target_pairs={{0,2},{1,3},{2,0},{3,1},{4,6},{5,7},{6,4},{7,5},{8,10},{9,11},{10,... | collective-permute-start | bytes 98312 | tf_op jit(solution)/shard_map/ppermute | solution.py:400
  136.7 5.9 %collective-permute-start.12 = (bf16[8,16,128]{2,1,0:T(8,128)(2,1)}, bf16[8,16,128]{2,1,0:T(8,128)(2,1)S(1)}, u32[]{:S(2)}, u32[]{:S(2)}) collective-permute-start(bf16[8,16,128]{2,1,0:T(8,128)(2,1)} %get-tuple-element.157), channel_id=1, source_target_pairs={{0,3},{1,2},{2,1},{3,0},{4,7},{5,6},{6,5},{7,4},{8,11},{9,10},{10,... | collective-permute-start | bytes 98312 | tf_op jit(solution)/shard_map/ppermute | solution.py:400
  145.4 11.1 %all-to-all-start.5 = ((bf16[8,80,256]{2,1,0:T(8,128)(2,1)}), bf16[8,80,256]{2,1,0:T(8,128)(2,1)S(1)}, u32[]{:S(2)}, u32[]{:S(2)}) async-start(bf16[8,80,256]{2,1,0:T(8,128)(2,1)} %shard_map.75), calls=%async_computation.6 | async-start | bytes 655360 | tf_op jit(solution)/shard_map/all_to_all | solution.py:736
  (22 other events, 141.5 us)
Sparse Core Ops, SparseCore 0:
  9.6 48.4 all-gather.2
  59.6 45.7 all-gather.4
  109.2 28.7 reduce-scatter.1

commit v8 on v7

--- a/solution.py
+++ b/solution.py
@@ -632,7 +632,7 @@
         else:
             parts = [shape((seq_count, extra, columns * rows_each // extra), bf16)] * fsdp_count
         return pl.pallas_call(
-            functools.partial(weight_kernel, sources, len(arrays), slots, group, fsdp_count, is_turned),
+            functools.partial(weight_kernel, sources, len(arrays), slots, min(slots, 2), fsdp_count, is_turned),
             out_shape=parts,
             grid=(1,),
             in_specs=scalar + in_hbm * len(arrays) + [resident(grad)],

time: 167 us -> 167 us (level)
  no operation moved by 1% of the time
where the time goes in v8:
time: 167 us; the launch traced here: 166 us
  Pallas kernels  64.7 us (39%)
  starting transfers between devices  38.8 us (23%)
  waiting for transfers between devices  34.9 us (21%)
  between operations  14.1 us (8%)
  local copies, waits for them, and re-layouts  11 us (7%)
  other arithmetic  2.35 us (1%)
    ppermute x18, starting transfers between devices, permute_xor(): return lax.ppermute(a, axis, [(i, i ^ mask) for i in range(count)])  16.2 us
    all_to_all x1, waiting for transfers between devices, on_device(): log_rates = lax.all_to_all(log_decay[0], 'seq', 0, 1, tiled=True)  14.6 us
    pallas_call x1, Pallas kernels, on_device(): pl.pallas_call(functools.partial(forward_kernel, sources, len(arrays), sl...  14.5 us
    pallas_call x1, Pallas kernels, on_device(): pl.pallas_call(functools.partial(backward_kernel, heads, head_size), out_...  12.7 us
    pallas_call x2, Pallas kernels, weight_columns(): pl.pallas_call(functools.partial(weight_kernel, sources, len(arrays), slo...  12.1 us
    ppermute x18, waiting for transfers between devices, permute_xor(): return lax.ppermute(a, axis, [(i, i ^ mask) for i in range(count)])  9.23 us
    pallas_call x1, Pallas kernels, on_device(): make_tables(log_rates)  9.15 us
    all_to_all x1, waiting for transfers between devices, on_device(): lax.all_to_all(shared_partial.reshape(seq_count, part, length), 'seq', 0, 0)  7.8 us
  transfers between devices with their start and end apart: 27, of which 12 were waited for; matrix products, arithmetic and copies ran while one was open for 5% of the time, Pallas kernels for 38%

profile of v8, /device:TPU:0, one launch (start us, length us, event | category | flops | bytes accessed | tf_op | source)
XLA Modules:
  0.0 165.7 jit_solution(17207330402848218668)
XLA Ops:
  9.9 2.6 %collective-permute-start.1 = (bf16[256,2048]{1,0:T(8,128)(2,1)S(1)}, bf16[256,2048]{1,0:T(8,128)(2,1)S(1)}, u32[]{:S(2)}, u32[]{:S(2)}) collective-permute-start(bf16[256,2048]{1,0:T(8,128)(2,1)S(1)} %bitcast.22), channel_id=1, source_target_pairs={{0,8},{4,12},{8,0},{12,4},{16,24},{20,28},{24,16},{28,20},{1,9},{5... | collective-permute-start | bytes 3145736 | tf_op jit(solution)/shard_map/ppermute | solution.py:400
  14.6 3.3 %all-to-all-start = ((f32[8,4,256]{2,1,0:T(4,128)}), f32[8,4,256]{2,1,0:T(4,128)S(1)}, u32[]{:S(2)}, u32[]{:S(2)}) async-start(f32[8,4,256]{2,1,0:T(4,128)} %all_to_all.29), calls=%async_computation | async-start | bytes 65536 | tf_op jit(solution)/shard_map/all_to_all | solution.py:530
  20.6 1.6 copy.10
  23.4 14.6 %all-to-all-done = f32[8,4,256]{2,1,0:T(4,128)S(1)} async-done(((f32[8,4,256]{2,1,0:T(4,128)}), f32[8,4,256]{2,1,0:T(4,128)S(1)}, u32[]{:S(2)}, u32[]{:S(2)}) %all-to-all-start) | async-done | bytes 32800 | tf_op jit(solution)/shard_map/all_to_all | solution.py:530
  42.4 9.1 %shard_map.67 = (bf16[2048,256]{1,0:T(8,128)(2,1)}, bf16[2048,256]{1,0:T(8,128)(2,1)}, bf16[2048,256]{1,0:T(8,128)(2,1)}, bf16[2048,256]{1,0:T(8,128)(2,1)}, f32...) custom-call(f32[4,2048]{1,0:T(4,128)} %bitcast.29), custom_call_target="tpu_custom_call" | custom-call | bytes 62914560 | tf_op jit(solution)/shard_map/pallas_call | solution.py:560
  51.6 3.0 %collective-permute-done.5.refs_6_ = bf16[128,2048]{1,0:T(8,128)(2,1)S(1)} collective-permute-done((bf16[128,2048]{1,0:T(8,128)(2,1)}, bf16[128,2048]{1,0:T(8,128)(2,1)S(1)}, u32[]{:S(2)}, u32[]{:S(2)}) %collective-permute-start.5) | collective-permute-done | bytes 524320 | tf_op jit(solution)/shard_map/ppermute | solution.py:400
  59.2 4.4 %all-to-all-start.1 = ((bf16[8,256,256]{2,1,0:T(8,128)(2,1)}), bf16[8,256,256]{2,1,0:T(8,128)(2,1)}, u32[]{:S(2)}, u32[]{:S(2)}) async-start(bf16[8,256,256]{2,1,0:T(8,128)(2,1)} %bitcast.16), calls=%async_computation.1 | async-start | bytes 2097152 | tf_op jit(solution)/shard_map/all_to_all | solution.py:578
  63.7 14.5 %shard_map.68 = (bf16[2048,256]{1,0:T(8,128)(2,1)}, bf16[2048,128]{1,0:T(8,128)(2,1)}, bf16[2048,128]{1,0:T(8,128)(2,1)}, bf16[2048,256]{1,0:T(8,128)(2,1)}, bf1...) custom-call(s32[2]{0:T(128)} %pad_add_fusion.place_ref.places_ref, ...), custom_call_target="tpu_custom_call" | custom-call | flops 19327352832 | bytes 16777216 | tf_op jit(solution)/shard_map/pallas_call | solution.py:581
  78.9 3.8 %all-to-all-start.2 = ((bf16[8,256,256]{2,1,0:T(8,128)(2,1)}), bf16[8,256,256]{2,1,0:T(8,128)(2,1)S(1)}, u32[]{:S(2)}, u32[]{:S(2)}) async-start(bf16[8,256,256]{2,1,0:T(8,128)(2,1)} %bitcast.27), calls=%async_computation.2 | async-start | bytes 2097152 | tf_op jit(solution)/shard_map/all_to_all | solution.py:605
  82.7 12.7 %shard_map.69 = (bf16[2048,256]{1,0:T(8,128)(2,1)}, bf16[256,2048]{1,0:T(8,128)(2,1)}) custom-call(bf16[2048,256]{1,0:T(8,128)(2,1)} %bitcast.6.refs_0_, bf16[2048,256]{1,0:T(8,128)(2,1)} %get-tuple-element.138.refs_1_, bf16[2048,256]{1,0:T(8,128)(2,1)} %get-tuple-element.139.refs_2_, bf16[2048,128]{1,0:T(8,128)(2,1)} %get-tuple-element.140.refs_3_, ...), custom_call_target="tpu_custom_call" | custom-call | flops 16106127360 | bytes 20971520 | tf_op jit(solution)/shard_map/pallas_call | solution.py:611
  95.4 2.4 %all-to-all-done.2.blocks_ref = bf16[8,256,256]{2,1,0:T(8,128)(2,1)S(1)} async-done(((bf16[8,256,256]{2,1,0:T(8,128)(2,1)}), bf16[8,256,256]{2,1,0:T(8,128)(2,1)S(1)}, u32[]{:S(2)}, u32[]{:S(2)}) %all-to-all-start.2) | async-done | bytes 1048608 | tf_op jit(solution)/shard_map/all_to_all | solution.py:605
  97.8 3.6 %all-to-all-start.3 = ((bf16[8,32,2048]{2,1,0:T(8,128)(2,1)}), bf16[8,32,2048]{2,1,0:T(8,128)(2,1)S(1)}, u32[]{:S(2)}, u32[]{:S(2)}) async-start(bf16[8,32,2048]{2,1,0:T(8,128)(2,1)} %bitcast.26), calls=%async_computation.3 | async-start | bytes 2097152 | tf_op jit(solution)/shard_map/all_to_all | solution.py:646
  101.4 6.3 %shard_map.70 = bf16[4,8,64,256]{3,2,1,0:T(8,128)(2,1)} custom-call(s32[2]{0:T(128)} %pad_add_fusion.place_ref.places_ref, bf16[256,2048]{1,0:T(8,128)(2,1)} %bitcast.19, bf16[256,2048]{1,0:T(8,128)(2,1)} %collective-permute-done.refs_1_, bf16[256,2048]{1,0:T(8,128)(2,1)} %copy-done.2, bf16[256,2048]{1,0:T(8,128)(2,1)} %copy-done.7, ...), custom_call_target="tpu_custom_call" | custom-call | flops 4294967296 | bytes 16777216 | tf_op jit(solution)/shard_map/pallas_call | solution.py:634
  108.9 7.8 %all-to-all-done.3.parts_ref = bf16[8,32,2048]{2,1,0:T(8,128)(2,1)S(1)} async-done(((bf16[8,32,2048]{2,1,0:T(8,128)(2,1)}), bf16[8,32,2048]{2,1,0:T(8,128)(2,1)S(1)}, u32[]{:S(2)}, u32[]{:S(2)}) %all-to-all-start.3) | async-done | bytes 1048608 | tf_op jit(solution)/shard_map/all_to_all | solution.py:646
  117.9 2.8 %shard_map.71 = (bf16[32,2048]{1,0:T(8,128)(2,1)}, bf16[8,288,256]{2,1,0:T(8,128)(2,1)}) custom-call(bf16[8,32,2048]{2,1,0:T(8,128)(2,1)} %copy-done.1, bf16[2048,256]{1,0:T(8,128)(2,1)} %get-tuple-element.149.refs_10_.dx_ref), custom_call_target="tpu_custom_call" | custom-call | tf_op jit(solution)/shard_map/pallas_call | solution.py:658
  120.7 3.6 %all-to-all-start.4 = ((bf16[8,288,256]{2,1,0:T(8,128)(2,1)}), bf16[8,288,256]{2,1,0:T(8,128)(2,1)S(1)}, u32[]{:S(2)}, u32[]{:S(2)}) async-start(bf16[8,288,256]{2,1,0:T(8,128)(2,1)} %get-tuple-element.164), calls=%async_computation.5 | async-start | bytes 2359296 | tf_op jit(solution)/shard_map/all_to_all | solution.py:667
  124.3 5.7 %shard_map.72 = (bf16[8,16,128]{2,1,0:T(8,128)(2,1)}, bf16[8,16,128]{2,1,0:T(8,128)(2,1)}, bf16[8,16,128]{2,1,0:T(8,128)(2,1)}, bf16[8,16,128]{2,1,0:T(8,128)(2,1)}) custom-call(s32[2]{0:T(128)} %pad_add_fusion.place_ref.places_ref, bf16[256,2048]{1,0:T(8,128)(2,1)} %bitcast.20, bf16[256,2048]{1,0:T(8,128)(2,1)} %collective-permute-done.refs_1_, ...), custom_call_target="tpu_custom_call" | custom-call | flops 536870912 | bytes 16777216 | tf_op jit(solution)/shard_map/pallas_call | solution.py:634
  133.6 2.6 %collective-permute-start.11 = (bf16[8,16,128]{2,1,0:T(8,128)(2,1)}, bf16[8,16,128]{2,1,0:T(8,128)(2,1)S(1)}, u32[]{:S(2)}, u32[]{:S(2)}) collective-permute-start(bf16[8,16,128]{2,1,0:T(8,128)(2,1)} %get-tuple-element.156), channel_id=1, source_target_pairs={{0,2},{1,3},{2,0},{3,1},{4,6},{5,7},{6,4},{7,5},{8,10},{9,11},{10,... | collective-permute-start | bytes 98312 | tf_op jit(solution)/shard_map/ppermute | solution.py:400
  136.7 3.0 %collective-permute-start.12 = (bf16[8,16,128]{2,1,0:T(8,128)(2,1)}, bf16[8,16,128]{2,1,0:T(8,128)(2,1)S(1)}, u32[]{:S(2)}, u32[]{:S(2)}) collective-permute-start(bf16[8,16,128]{2,1,0:T(8,128)(2,1)} %get-tuple-element.157), channel_id=1, source_target_pairs={{0,3},{1,2},{2,1},{3,0},{4,7},{5,6},{6,5},{7,4},{8,11},{9,10},{10,... | collective-permute-start | bytes 98312 | tf_op jit(solution)/shard_map/ppermute | solution.py:400
  139.7 2.3 %shard_map.73 = bf16[1,256,2048]{2,1,0:T(8,128)(2,1)} custom-call(bf16[8,256,256]{2,1,0:T(8,128)(2,1)} %copy-done), custom_call_target="tpu_custom_call" | custom-call | tf_op jit(solution)/shard_map/pallas_call | solution.py:671
  143.5 1.9 %shard_map.75 = bf16[8,80,256]{2,1,0:T(8,128)(2,1)} custom-call(bf16[8,64,256]{2,1,0:T(8,128)(2,1)} %bitcast.28, bf16[8,16,128]{2,1,0:T(8,128)(2,1)} %get-tuple-element.170.refs_1_, bf16[8,16,128]{2,1,0:T(8,128)(2,1)} %copy-done.11, bf16[8,16,128]{2,1,0:T(8,128)(2,1)} %copy-done.12, bf16[8,16,128]{2,1,0:T(8,128)(2,1)} %copy-done.13), custom_call_target="tpu_custom_call" | custom-call | tf_op jit(solution)/shard_map/pallas_call | solution.py:728
  145.5 3.7 %all-to-all-start.5 = ((bf16[8,80,256]{2,1,0:T(8,128)(2,1)}), bf16[8,80,256]{2,1,0:T(8,128)(2,1)S(1)}, u32[]{:S(2)}, u32[]{:S(2)}) async-start(bf16[8,80,256]{2,1,0:T(8,128)(2,1)} %shard_map.75), calls=%async_computation.6 | async-start | bytes 655360 | tf_op jit(solution)/shard_map/all_to_all | solution.py:736
  149.2 7.4 %shard_map.74 = bf16[1,256,2048]{2,1,0:T(8,128)(2,1)} custom-call(s32[2]{0:T(128)} %pad_add_fusion.place_ref.places_ref, bf16[8,288,256]{2,1,0:T(8,128)(2,1)} %copy-done.5, bf16[2048,512]{1,0:T(8,128)(2,1)} %all-gather.3.cloned.1.call-done.refs_10_.refs_0_, bf16[2048,512]{1,0:T(8,128)(2,1)} %collective-permute-done.9.refs_1_, ...), custom_call_target="tpu_custom_call" | custom-call | flops 4831838208 | bytes 18874368 | tf_op jit(solution)/shard_map/pallas_call | solution.py:702
  157.3 1.9 %shard_map.76 = f32[64,2304]{1,0:T(8,128)} custom-call(bf16[8,80,256]{2,1,0:T(8,128)(2,1)} %copy-done.4), custom_call_target="tpu_custom_call" | custom-call | tf_op jit(solution)/shard_map/pallas_call | solution.py:738
  (92 shorter events, 27.0 us)
Async XLA Ops:
  7.2 51.8 %all-gather.3.cloned.1.call-start = ((), (), s32[]{:S(2)}) async-start(), calls=%async_computation.7 | async-start | bytes 2621440 | tf_op jit(solution)/shard_map/all_gather | solution.py:527
  9.4 28.7 %collective-permute-start = (bf16[256,2048]{1,0:T(8,128)(2,1)S(1)}, bf16[256,2048]{1,0:T(8,128)(2,1)}, u32[]{:S(2)}, u32[]{:S(2)}) collective-permute-start(bf16[256,2048]{1,0:T(8,128)(2,1)S(1)} %bitcast.21), channel_id=1, source_target_pairs={{0,4},{4,0},{8,12},{12,8},{16,20},{20,16},{24,28},{28,24},{1,5},{5... | collective-permute-start | bytes 3145736 | tf_op jit(solution)/shard_map/ppermute | solution.py:400
  9.9 28.2 %collective-permute-start.1 = (bf16[256,2048]{1,0:T(8,128)(2,1)S(1)}, bf16[256,2048]{1,0:T(8,128)(2,1)S(1)}, u32[]{:S(2)}, u32[]{:S(2)}) collective-permute-start(bf16[256,2048]{1,0:T(8,128)(2,1)S(1)} %bitcast.22), channel_id=1, source_target_pairs={{0,8},{4,12},{8,0},{12,4},{16,24},{20,28},{24,16},{28,20},{1,9},{5... | collective-permute-start | bytes 3145736 | tf_op jit(solution)/shard_map/ppermute | solution.py:400
  12.4 25.6 %collective-permute-start.2 = (bf16[256,2048]{1,0:T(8,128)(2,1)S(1)}, bf16[256,2048]{1,0:T(8,128)(2,1)S(1)}, u32[]{:S(2)}, u32[]{:S(2)}) collective-permute-start(bf16[256,2048]{1,0:T(8,128)(2,1)S(1)} %bitcast.23), channel_id=1, source_target_pairs={{0,16},{4,20},{8,24},{12,28},{16,0},{20,4},{24,8},{28,12},{1,17},{... | collective-permute-start | bytes 3145736 | tf_op jit(solution)/shard_map/ppermute | solution.py:400
  14.6 23.4 %all-to-all-start = ((f32[8,4,256]{2,1,0:T(4,128)}), f32[8,4,256]{2,1,0:T(4,128)S(1)}, u32[]{:S(2)}, u32[]{:S(2)}) async-start(f32[8,4,256]{2,1,0:T(4,128)} %all_to_all.29), calls=%async_computation | async-start | bytes 65536 | tf_op jit(solution)/shard_map/all_to_all | solution.py:530
  17.9 90.9 %all-gather.5.cloned.1.call-start = ((), (), s32[]{:S(2)}) async-start(), calls=%async_computation.8 | async-start | bytes 2621440 | tf_op jit(solution)/shard_map/all_gather | solution.py:574
  38.1 17.9 %collective-permute-start.3 = (bf16[256,2048]{1,0:T(8,128)(2,1)S(1)}, bf16[256,2048]{1,0:T(8,128)(2,1)S(1)}, u32[]{:S(2)}, u32[]{:S(2)}) collective-permute-start(bf16[256,2048]{1,0:T(8,128)(2,1)S(1)} %collective-permute-done.1.refs_2_), channel_id=1, source_target_pairs={{0,4},{4,0},{8,12},{12,8},{16,20},{20,16},{24,28},{28,24},{1,5},{5... | collective-permute-start | bytes 3145736 | tf_op jit(solution)/shard_map/ppermute | solution.py:400
  38.3 17.6 %collective-permute-start.4 = (bf16[256,2048]{1,0:T(8,128)(2,1)S(1)}, bf16[256,2048]{1,0:T(8,128)(2,1)}, u32[]{:S(2)}, u32[]{:S(2)}) collective-permute-start(bf16[256,2048]{1,0:T(8,128)(2,1)S(1)} %collective-permute-done.2.refs_4_), channel_id=1, source_target_pairs={{0,4},{4,0},{8,12},{12,8},{16,20},{20,16},{24,28},{28,24},{1,5},{5... | collective-permute-start | bytes 3145736 | tf_op jit(solution)/shard_map/ppermute | solution.py:400
  40.4 14.2 %collective-permute-start.5 = (bf16[128,2048]{1,0:T(8,128)(2,1)}, bf16[128,2048]{1,0:T(8,128)(2,1)S(1)}, u32[]{:S(2)}, u32[]{:S(2)}) collective-permute-start(bf16[128,2048]{1,0:T(8,128)(2,1)} %slice.20), channel_id=1, source_target_pairs={{0,16},{4,20},{8,24},{12,28},{16,0},{20,4},{24,8},{28,12},{1,17},{... | collective-permute-start | bytes 1572872 | tf_op jit(solution)/shard_map/ppermute | solution.py:400
  41.9 14.0 %collective-permute-start.6 = (bf16[128,2048]{1,0:T(8,128)(2,1)}, bf16[128,2048]{1,0:T(8,128)(2,1)}, u32[]{:S(2)}, u32[]{:S(2)}) collective-permute-start(bf16[128,2048]{1,0:T(8,128)(2,1)} %slice.21), channel_id=1, source_target_pairs={{0,8},{4,12},{8,0},{12,4},{16,24},{20,28},{24,16},{28,20},{1,9},{5... | collective-permute-start | bytes 1572872 | tf_op jit(solution)/shard_map/ppermute | solution.py:400
  59.0 19.9 %collective-permute-start.9 = (bf16[2048,512]{1,0:T(8,128)(2,1)}, bf16[2048,512]{1,0:T(8,128)(2,1)}, u32[]{:S(2)}, u32[]{:S(2)}) collective-permute-start(bf16[2048,512]{1,0:T(8,128)(2,1)} %all-gather.3.cloned.1.call-done.refs_10_.refs_0_), channel_id=1, source_target_pairs={{0,4},{4,0},{8,12},{12,8},{16,20},{20,16},{24,28},{28,24},{1,5},{5... | collective-permute-start | bytes 6291464 | tf_op jit(solution)/shard_map/ppermute | solution.py:400
  59.2 19.7 %all-to-all-start.1 = ((bf16[8,256,256]{2,1,0:T(8,128)(2,1)}), bf16[8,256,256]{2,1,0:T(8,128)(2,1)}, u32[]{:S(2)}, u32[]{:S(2)}) async-start(bf16[8,256,256]{2,1,0:T(8,128)(2,1)} %bitcast.16), calls=%async_computation.1 | async-start | bytes 2097152 | tf_op jit(solution)/shard_map/all_to_all | solution.py:578
  78.9 18.9 %all-to-all-start.2 = ((bf16[8,256,256]{2,1,0:T(8,128)(2,1)}), bf16[8,256,256]{2,1,0:T(8,128)(2,1)S(1)}, u32[]{:S(2)}, u32[]{:S(2)}) async-start(bf16[8,256,256]{2,1,0:T(8,128)(2,1)} %bitcast.27), calls=%async_computation.2 | async-start | bytes 2097152 | tf_op jit(solution)/shard_map/all_to_all | solution.py:605
  97.8 18.9 %all-to-all-start.3 = ((bf16[8,32,2048]{2,1,0:T(8,128)(2,1)}), bf16[8,32,2048]{2,1,0:T(8,128)(2,1)S(1)}, u32[]{:S(2)}, u32[]{:S(2)}) async-start(bf16[8,32,2048]{2,1,0:T(8,128)(2,1)} %bitcast.26), calls=%async_computation.3 | async-start | bytes 2097152 | tf_op jit(solution)/shard_map/all_to_all | solution.py:646
  101.4 42.1 %reduce-scatter.2.cloned.1.call-start = ((), (), s32[]{:S(2)}) async-start(), calls=%async_computation.9 | async-start | bytes 1310720 | tf_op jit(solution)/shard_map/reduce_scatter | solution.py:648
  116.7 26.8 %collective-permute-start.13 = (bf16[2048,512]{1,0:T(8,128)(2,1)}, bf16[2048,512]{1,0:T(8,128)(2,1)}, u32[]{:S(2)}, u32[]{:S(2)}) collective-permute-start(bf16[2048,512]{1,0:T(8,128)(2,1)} %all-gather.5.cloned.1.call-done.refs_2_), channel_id=1, source_target_pairs={{0,4},{4,0},{8,12},{12,8},{16,20},{20,16},{24,28},{28,24},{1,5},{5... | collective-permute-start | bytes 6291464 | tf_op jit(solution)/shard_map/ppermute | solution.py:400
  116.7 14.7 %collective-permute-start.16 = (bf16[2048,128]{1,0:T(8,128)(2,1)S(1)}, bf16[2048,128]{1,0:T(8,128)(2,1)S(1)}, u32[]{:S(2)}, u32[]{:S(2)}) collective-permute-start(bf16[2048,128]{1,0:T(8,128)(2,1)S(1)} %slice.23), channel_id=1, source_target_pairs={{0,16},{4,20},{8,24},{12,28},{16,0},{20,4},{24,8},{28,12},{1,17},{... | collective-permute-start | bytes 1572872 | tf_op jit(solution)/shard_map/ppermute | solution.py:400
  117.2 14.8 %collective-permute-start.14 = (bf16[2048,128]{1,0:T(8,128)(2,1)S(1)}, bf16[2048,128]{1,0:T(8,128)(2,1)S(1)}, u32[]{:S(2)}, u32[]{:S(2)}) collective-permute-start(bf16[2048,128]{1,0:T(8,128)(2,1)S(1)} %slice.23), channel_id=1, source_target_pairs={{0,8},{4,12},{8,0},{12,4},{16,24},{20,28},{24,16},{28,20},{1,9},{5... | collective-permute-start | bytes 1572872 | tf_op jit(solution)/shard_map/ppermute | solution.py:400
  120.7 24.8 %all-to-all-start.4 = ((bf16[8,288,256]{2,1,0:T(8,128)(2,1)}), bf16[8,288,256]{2,1,0:T(8,128)(2,1)S(1)}, u32[]{:S(2)}, u32[]{:S(2)}) async-start(bf16[8,288,256]{2,1,0:T(8,128)(2,1)} %get-tuple-element.164), calls=%async_computation.5 | async-start | bytes 2359296 | tf_op jit(solution)/shard_map/all_to_all | solution.py:667
  131.4 11.2 %collective-permute-start.17 = (bf16[2048,128]{1,0:T(8,128)(2,1)S(1)}, bf16[2048,128]{1,0:T(8,128)(2,1)S(1)}, u32[]{:S(2)}, u32[]{:S(2)}) collective-permute-start(bf16[2048,128]{1,0:T(8,128)(2,1)S(1)} %collective-permute-done.16.refs_4_), channel_id=1, source_target_pairs={{0,4},{4,0},{8,12},{12,8},{16,20},{20,16},{24,28},{28,24},{1,5},{5... | collective-permute-start | bytes 1572872 | tf_op jit(solution)/shard_map/ppermute | solution.py:400
  132.0 11.5 %collective-permute-start.15 = (bf16[2048,128]{1,0:T(8,128)(2,1)S(1)}, bf16[2048,128]{1,0:T(8,128)(2,1)S(1)}, u32[]{:S(2)}, u32[]{:S(2)}) collective-permute-start(bf16[2048,128]{1,0:T(8,128)(2,1)S(1)} %collective-permute-done.14.refs_3_), channel_id=1, source_target_pairs={{0,4},{4,0},{8,12},{12,8},{16,20},{20,16},{24,28},{28,24},{1,5},{5... | collective-permute-start | bytes 1572872 | tf_op jit(solution)/shard_map/ppermute | solution.py:400
  133.6 8.5 %collective-permute-start.11 = (bf16[8,16,128]{2,1,0:T(8,128)(2,1)}, bf16[8,16,128]{2,1,0:T(8,128)(2,1)S(1)}, u32[]{:S(2)}, u32[]{:S(2)}) collective-permute-start(bf16[8,16,128]{2,1,0:T(8,128)(2,1)} %get-tuple-element.156), channel_id=1, source_target_pairs={{0,2},{1,3},{2,0},{3,1},{4,6},{5,7},{6,4},{7,5},{8,10},{9,11},{10,... | collective-permute-start | bytes 98312 | tf_op jit(solution)/shard_map/ppermute | solution.py:400
  136.7 5.9 %collective-permute-start.12 = (bf16[8,16,128]{2,1,0:T(8,128)(2,1)}, bf16[8,16,128]{2,1,0:T(8,128)(2,1)S(1)}, u32[]{:S(2)}, u32[]{:S(2)}) collective-permute-start(bf16[8,16,128]{2,1,0:T(8,128)(2,1)} %get-tuple-element.157), channel_id=1, source_target_pairs={{0,3},{1,2},{2,1},{3,0},{4,7},{5,6},{6,5},{7,4},{8,11},{9,10},{10,... | collective-permute-start | bytes 98312 | tf_op jit(solution)/shard_map/ppermute | solution.py:400
  145.5 11.1 %all-to-all-start.5 = ((bf16[8,80,256]{2,1,0:T(8,128)(2,1)}), bf16[8,80,256]{2,1,0:T(8,128)(2,1)S(1)}, u32[]{:S(2)}, u32[]{:S(2)}) async-start(bf16[8,80,256]{2,1,0:T(8,128)(2,1)} %shard_map.75), calls=%async_computation.6 | async-start | bytes 655360 | tf_op jit(solution)/shard_map/all_to_all | solution.py:736
  (22 other events, 141.4 us)
Sparse Core Ops, SparseCore 0:
  9.6 48.4 all-gather.2
  59.6 45.7 all-gather.4
  109.0 28.7 reduce-scatter.1

commit v9 on v8

--- a/solution.py
+++ b/solution.py
@@ -675,7 +675,7 @@
         in_specs=[resident(mixed_blocks)],
         out_specs=resident(mixed_shape),
         compiler_params=params,
-    )(after(mixed_blocks, shared_columns))
+    )(after(mixed_blocks, second_part))
     w_even = [w_even, *(after(a, shared_weights[0]) for a in w_across)]
     w_odd = [permute_xor(a, "seq", 1) for a in w_even]
     shared_arrived, mixer_out, w_odd, head_sums = lax.optimization_barrier(

time: 167 us -> 167 us (level)
  no operation moved by 1% of the time
where the time goes in v9:
time: 167 us; the launch traced here: 166 us
  Pallas kernels  64.7 us (39%)
  starting transfers between devices  38.8 us (23%)
  waiting for transfers between devices  34.9 us (21%)
  between operations  14.1 us (8%)
  local copies, waits for them, and re-layouts  11 us (7%)
  other arithmetic  2.35 us (1%)
    ppermute x18, starting transfers between devices, permute_xor(): return lax.ppermute(a, axis, [(i, i ^ mask) for i in range(count)])  16.2 us
    all_to_all x1, waiting for transfers between devices, on_device(): log_rates = lax.all_to_all(log_decay[0], 'seq', 0, 1, tiled=True)  14.6 us
    pallas_call x1, Pallas kernels, on_device(): pl.pallas_call(functools.partial(forward_kernel, sources, len(arrays), sl...  14.5 us
    pallas_call x1, Pallas kernels, on_device(): pl.pallas_call(functools.partial(backward_kernel, heads, head_size), out_...  12.7 us
    pallas_call x2, Pallas kernels, weight_columns(): pl.pallas_call(functools.partial(weight_kernel, sources, len(arrays), slo...  12.1 us
    ppermute x18, waiting for transfers between devices, permute_xor(): return lax.ppermute(a, axis, [(i, i ^ mask) for i in range(count)])  9.23 us
    pallas_call x1, Pallas kernels, on_device(): make_tables(log_rates)  9.15 us
    all_to_all x1, waiting for transfers between devices, on_device(): lax.all_to_all(shared_partial.reshape(seq_count, part, length), 'seq', 0, 0)  7.8 us
  transfers between devices with their start and end apart: 27, of which 12 were waited for; matrix products, arithmetic and copies ran while one was open for 5% of the time, Pallas kernels for 38%

profile of v9, /device:TPU:0, one launch (start us, length us, event | category | flops | bytes accessed | tf_op | source)
XLA Modules:
  0.0 165.7 jit_solution(17207330402848218668)
XLA Ops:
  9.9 2.6 %collective-permute-start.1 = (bf16[256,2048]{1,0:T(8,128)(2,1)S(1)}, bf16[256,2048]{1,0:T(8,128)(2,1)S(1)}, u32[]{:S(2)}, u32[]{:S(2)}) collective-permute-start(bf16[256,2048]{1,0:T(8,128)(2,1)S(1)} %bitcast.22), channel_id=1, source_target_pairs={{0,8},{4,12},{8,0},{12,4},{16,24},{20,28},{24,16},{28,20},{1,9},{5... | collective-permute-start | bytes 3145736 | tf_op jit(solution)/shard_map/ppermute | solution.py:400
  14.6 3.3 %all-to-all-start = ((f32[8,4,256]{2,1,0:T(4,128)}), f32[8,4,256]{2,1,0:T(4,128)S(1)}, u32[]{:S(2)}, u32[]{:S(2)}) async-start(f32[8,4,256]{2,1,0:T(4,128)} %all_to_all.29), calls=%async_computation | async-start | bytes 65536 | tf_op jit(solution)/shard_map/all_to_all | solution.py:530
  20.6 1.6 copy.10
  23.4 14.6 %all-to-all-done = f32[8,4,256]{2,1,0:T(4,128)S(1)} async-done(((f32[8,4,256]{2,1,0:T(4,128)}), f32[8,4,256]{2,1,0:T(4,128)S(1)}, u32[]{:S(2)}, u32[]{:S(2)}) %all-to-all-start) | async-done | bytes 32800 | tf_op jit(solution)/shard_map/all_to_all | solution.py:530
  42.4 9.1 %shard_map.67 = (bf16[2048,256]{1,0:T(8,128)(2,1)}, bf16[2048,256]{1,0:T(8,128)(2,1)}, bf16[2048,256]{1,0:T(8,128)(2,1)}, bf16[2048,256]{1,0:T(8,128)(2,1)}, f32...) custom-call(f32[4,2048]{1,0:T(4,128)} %bitcast.29), custom_call_target="tpu_custom_call" | custom-call | bytes 62914560 | tf_op jit(solution)/shard_map/pallas_call | solution.py:560
  51.6 3.0 %collective-permute-done.5.refs_6_ = bf16[128,2048]{1,0:T(8,128)(2,1)S(1)} collective-permute-done((bf16[128,2048]{1,0:T(8,128)(2,1)}, bf16[128,2048]{1,0:T(8,128)(2,1)S(1)}, u32[]{:S(2)}, u32[]{:S(2)}) %collective-permute-start.5) | collective-permute-done | bytes 524320 | tf_op jit(solution)/shard_map/ppermute | solution.py:400
  59.2 4.4 %all-to-all-start.1 = ((bf16[8,256,256]{2,1,0:T(8,128)(2,1)}), bf16[8,256,256]{2,1,0:T(8,128)(2,1)}, u32[]{:S(2)}, u32[]{:S(2)}) async-start(bf16[8,256,256]{2,1,0:T(8,128)(2,1)} %bitcast.16), calls=%async_computation.1 | async-start | bytes 2097152 | tf_op jit(solution)/shard_map/all_to_all | solution.py:578
  63.7 14.5 %shard_map.68 = (bf16[2048,256]{1,0:T(8,128)(2,1)}, bf16[2048,128]{1,0:T(8,128)(2,1)}, bf16[2048,128]{1,0:T(8,128)(2,1)}, bf16[2048,256]{1,0:T(8,128)(2,1)}, bf1...) custom-call(s32[2]{0:T(128)} %pad_add_fusion.place_ref.places_ref, ...), custom_call_target="tpu_custom_call" | custom-call | flops 19327352832 | bytes 16777216 | tf_op jit(solution)/shard_map/pallas_call | solution.py:581
  78.9 3.8 %all-to-all-start.2 = ((bf16[8,256,256]{2,1,0:T(8,128)(2,1)}), bf16[8,256,256]{2,1,0:T(8,128)(2,1)S(1)}, u32[]{:S(2)}, u32[]{:S(2)}) async-start(bf16[8,256,256]{2,1,0:T(8,128)(2,1)} %bitcast.27), calls=%async_computation.2 | async-start | bytes 2097152 | tf_op jit(solution)/shard_map/all_to_all | solution.py:605
  82.7 12.7 %shard_map.69 = (bf16[2048,256]{1,0:T(8,128)(2,1)}, bf16[256,2048]{1,0:T(8,128)(2,1)}) custom-call(bf16[2048,256]{1,0:T(8,128)(2,1)} %bitcast.6.refs_0_, bf16[2048,256]{1,0:T(8,128)(2,1)} %get-tuple-element.137.refs_1_, bf16[2048,256]{1,0:T(8,128)(2,1)} %get-tuple-element.138.refs_2_, bf16[2048,128]{1,0:T(8,128)(2,1)} %get-tuple-element.139.refs_3_, ...), custom_call_target="tpu_custom_call" | custom-call | flops 16106127360 | bytes 20971520 | tf_op jit(solution)/shard_map/pallas_call | solution.py:611
  95.4 2.4 %all-to-all-done.2.blocks_ref = bf16[8,256,256]{2,1,0:T(8,128)(2,1)S(1)} async-done(((bf16[8,256,256]{2,1,0:T(8,128)(2,1)}), bf16[8,256,256]{2,1,0:T(8,128)(2,1)S(1)}, u32[]{:S(2)}, u32[]{:S(2)}) %all-to-all-start.2) | async-done | bytes 1048608 | tf_op jit(solution)/shard_map/all_to_all | solution.py:605
  97.8 3.6 %all-to-all-start.3 = ((bf16[8,32,2048]{2,1,0:T(8,128)(2,1)}), bf16[8,32,2048]{2,1,0:T(8,128)(2,1)S(1)}, u32[]{:S(2)}, u32[]{:S(2)}) async-start(bf16[8,32,2048]{2,1,0:T(8,128)(2,1)} %bitcast.26), calls=%async_computation.3 | async-start | bytes 2097152 | tf_op jit(solution)/shard_map/all_to_all | solution.py:646
  101.4 6.3 %shard_map.70 = bf16[4,8,64,256]{3,2,1,0:T(8,128)(2,1)} custom-call(s32[2]{0:T(128)} %pad_add_fusion.place_ref.places_ref, bf16[256,2048]{1,0:T(8,128)(2,1)} %bitcast.19, bf16[256,2048]{1,0:T(8,128)(2,1)} %collective-permute-done.refs_1_, bf16[256,2048]{1,0:T(8,128)(2,1)} %copy-done.2, bf16[256,2048]{1,0:T(8,128)(2,1)} %copy-done.7, ...), custom_call_target="tpu_custom_call" | custom-call | flops 4294967296 | bytes 16777216 | tf_op jit(solution)/shard_map/pallas_call | solution.py:634
  108.9 7.8 %all-to-all-done.3.parts_ref = bf16[8,32,2048]{2,1,0:T(8,128)(2,1)S(1)} async-done(((bf16[8,32,2048]{2,1,0:T(8,128)(2,1)}), bf16[8,32,2048]{2,1,0:T(8,128)(2,1)S(1)}, u32[]{:S(2)}, u32[]{:S(2)}) %all-to-all-start.3) | async-done | bytes 1048608 | tf_op jit(solution)/shard_map/all_to_all | solution.py:646
  117.9 2.8 %shard_map.71 = (bf16[32,2048]{1,0:T(8,128)(2,1)}, bf16[8,288,256]{2,1,0:T(8,128)(2,1)}) custom-call(bf16[8,32,2048]{2,1,0:T(8,128)(2,1)} %copy-done.1, bf16[2048,256]{1,0:T(8,128)(2,1)} %get-tuple-element.148.refs_10_.dx_ref), custom_call_target="tpu_custom_call" | custom-call | tf_op jit(solution)/shard_map/pallas_call | solution.py:658
  120.7 3.6 %all-to-all-start.4 = ((bf16[8,288,256]{2,1,0:T(8,128)(2,1)}), bf16[8,288,256]{2,1,0:T(8,128)(2,1)S(1)}, u32[]{:S(2)}, u32[]{:S(2)}) async-start(bf16[8,288,256]{2,1,0:T(8,128)(2,1)} %get-tuple-element.162), calls=%async_computation.5 | async-start | bytes 2359296 | tf_op jit(solution)/shard_map/all_to_all | solution.py:667
  124.3 5.7 %shard_map.72 = (bf16[8,16,128]{2,1,0:T(8,128)(2,1)}, bf16[8,16,128]{2,1,0:T(8,128)(2,1)}, bf16[8,16,128]{2,1,0:T(8,128)(2,1)}, bf16[8,16,128]{2,1,0:T(8,128)(2,1)}) custom-call(s32[2]{0:T(128)} %pad_add_fusion.place_ref.places_ref, bf16[256,2048]{1,0:T(8,128)(2,1)} %bitcast.20, bf16[256,2048]{1,0:T(8,128)(2,1)} %collective-permute-done.refs_1_, ...), custom_call_target="tpu_custom_call" | custom-call | flops 536870912 | bytes 16777216 | tf_op jit(solution)/shard_map/pallas_call | solution.py:634
  133.6 2.6 %collective-permute-start.11 = (bf16[8,16,128]{2,1,0:T(8,128)(2,1)}, bf16[8,16,128]{2,1,0:T(8,128)(2,1)S(1)}, u32[]{:S(2)}, u32[]{:S(2)}) collective-permute-start(bf16[8,16,128]{2,1,0:T(8,128)(2,1)} %get-tuple-element.155), channel_id=1, source_target_pairs={{0,2},{1,3},{2,0},{3,1},{4,6},{5,7},{6,4},{7,5},{8,10},{9,11},{10,... | collective-permute-start | bytes 98312 | tf_op jit(solution)/shard_map/ppermute | solution.py:400
  136.7 3.0 %collective-permute-start.12 = (bf16[8,16,128]{2,1,0:T(8,128)(2,1)}, bf16[8,16,128]{2,1,0:T(8,128)(2,1)S(1)}, u32[]{:S(2)}, u32[]{:S(2)}) collective-permute-start(bf16[8,16,128]{2,1,0:T(8,128)(2,1)} %get-tuple-element.156), channel_id=1, source_target_pairs={{0,3},{1,2},{2,1},{3,0},{4,7},{5,6},{6,5},{7,4},{8,11},{9,10},{10,... | collective-permute-start | bytes 98312 | tf_op jit(solution)/shard_map/ppermute | solution.py:400
  139.7 2.3 %shard_map.73 = bf16[1,256,2048]{2,1,0:T(8,128)(2,1)} custom-call(bf16[8,256,256]{2,1,0:T(8,128)(2,1)} %copy-done), custom_call_target="tpu_custom_call" | custom-call | tf_op jit(solution)/shard_map/pallas_call | solution.py:671
  143.5 1.9 %shard_map.75 = bf16[8,80,256]{2,1,0:T(8,128)(2,1)} custom-call(bf16[8,64,256]{2,1,0:T(8,128)(2,1)} %bitcast.28, bf16[8,16,128]{2,1,0:T(8,128)(2,1)} %get-tuple-element.168.refs_1_, bf16[8,16,128]{2,1,0:T(8,128)(2,1)} %copy-done.11, bf16[8,16,128]{2,1,0:T(8,128)(2,1)} %copy-done.12, bf16[8,16,128]{2,1,0:T(8,128)(2,1)} %copy-done.13), custom_call_target="tpu_custom_call" | custom-call | tf_op jit(solution)/shard_map/pallas_call | solution.py:728
  145.5 3.7 %all-to-all-start.5 = ((bf16[8,80,256]{2,1,0:T(8,128)(2,1)}), bf16[8,80,256]{2,1,0:T(8,128)(2,1)S(1)}, u32[]{:S(2)}, u32[]{:S(2)}) async-start(bf16[8,80,256]{2,1,0:T(8,128)(2,1)} %shard_map.75), calls=%async_computation.6 | async-start | bytes 655360 | tf_op jit(solution)/shard_map/all_to_all | solution.py:736
  149.2 7.4 %shard_map.74 = bf16[1,256,2048]{2,1,0:T(8,128)(2,1)} custom-call(s32[2]{0:T(128)} %pad_add_fusion.place_ref.places_ref, bf16[8,288,256]{2,1,0:T(8,128)(2,1)} %copy-done.5, bf16[2048,512]{1,0:T(8,128)(2,1)} %all-gather.3.cloned.1.call-done.refs_10_.refs_0_, bf16[2048,512]{1,0:T(8,128)(2,1)} %collective-permute-done.9.refs_1_, ...), custom_call_target="tpu_custom_call" | custom-call | flops 4831838208 | bytes 18874368 | tf_op jit(solution)/shard_map/pallas_call | solution.py:702
  157.3 1.9 %shard_map.76 = f32[64,2304]{1,0:T(8,128)} custom-call(bf16[8,80,256]{2,1,0:T(8,128)(2,1)} %copy-done.4), custom_call_target="tpu_custom_call" | custom-call | tf_op jit(solution)/shard_map/pallas_call | solution.py:738
  (92 shorter events, 27.0 us)
Async XLA Ops:
  7.2 51.8 %all-gather.3.cloned.1.call-start = ((), (), s32[]{:S(2)}) async-start(), calls=%async_computation.7 | async-start | bytes 2621440 | tf_op jit(solution)/shard_map/all_gather | solution.py:527
  9.4 28.7 %collective-permute-start = (bf16[256,2048]{1,0:T(8,128)(2,1)S(1)}, bf16[256,2048]{1,0:T(8,128)(2,1)}, u32[]{:S(2)}, u32[]{:S(2)}) collective-permute-start(bf16[256,2048]{1,0:T(8,128)(2,1)S(1)} %bitcast.21), channel_id=1, source_target_pairs={{0,4},{4,0},{8,12},{12,8},{16,20},{20,16},{24,28},{28,24},{1,5},{5... | collective-permute-start | bytes 3145736 | tf_op jit(solution)/shard_map/ppermute | solution.py:400
  9.9 28.2 %collective-permute-start.1 = (bf16[256,2048]{1,0:T(8,128)(2,1)S(1)}, bf16[256,2048]{1,0:T(8,128)(2,1)S(1)}, u32[]{:S(2)}, u32[]{:S(2)}) collective-permute-start(bf16[256,2048]{1,0:T(8,128)(2,1)S(1)} %bitcast.22), channel_id=1, source_target_pairs={{0,8},{4,12},{8,0},{12,4},{16,24},{20,28},{24,16},{28,20},{1,9},{5... | collective-permute-start | bytes 3145736 | tf_op jit(solution)/shard_map/ppermute | solution.py:400
  12.4 25.6 %collective-permute-start.2 = (bf16[256,2048]{1,0:T(8,128)(2,1)S(1)}, bf16[256,2048]{1,0:T(8,128)(2,1)S(1)}, u32[]{:S(2)}, u32[]{:S(2)}) collective-permute-start(bf16[256,2048]{1,0:T(8,128)(2,1)S(1)} %bitcast.23), channel_id=1, source_target_pairs={{0,16},{4,20},{8,24},{12,28},{16,0},{20,4},{24,8},{28,12},{1,17},{... | collective-permute-start | bytes 3145736 | tf_op jit(solution)/shard_map/ppermute | solution.py:400
  14.6 23.4 %all-to-all-start = ((f32[8,4,256]{2,1,0:T(4,128)}), f32[8,4,256]{2,1,0:T(4,128)S(1)}, u32[]{:S(2)}, u32[]{:S(2)}) async-start(f32[8,4,256]{2,1,0:T(4,128)} %all_to_all.29), calls=%async_computation | async-start | bytes 65536 | tf_op jit(solution)/shard_map/all_to_all | solution.py:530
  17.9 90.9 %all-gather.5.cloned.1.call-start = ((), (), s32[]{:S(2)}) async-start(), calls=%async_computation.8 | async-start | bytes 2621440 | tf_op jit(solution)/shard_map/all_gather | solution.py:574
  38.1 17.9 %collective-permute-start.3 = (bf16[256,2048]{1,0:T(8,128)(2,1)S(1)}, bf16[256,2048]{1,0:T(8,128)(2,1)S(1)}, u32[]{:S(2)}, u32[]{:S(2)}) collective-permute-start(bf16[256,2048]{1,0:T(8,128)(2,1)S(1)} %collective-permute-done.1.refs_2_), channel_id=1, source_target_pairs={{0,4},{4,0},{8,12},{12,8},{16,20},{20,16},{24,28},{28,24},{1,5},{5... | collective-permute-start | bytes 3145736 | tf_op jit(solution)/shard_map/ppermute | solution.py:400
  38.3 17.6 %collective-permute-start.4 = (bf16[256,2048]{1,0:T(8,128)(2,1)S(1)}, bf16[256,2048]{1,0:T(8,128)(2,1)}, u32[]{:S(2)}, u32[]{:S(2)}) collective-permute-start(bf16[256,2048]{1,0:T(8,128)(2,1)S(1)} %collective-permute-done.2.refs_4_), channel_id=1, source_target_pairs={{0,4},{4,0},{8,12},{12,8},{16,20},{20,16},{24,28},{28,24},{1,5},{5... | collective-permute-start | bytes 3145736 | tf_op jit(solution)/shard_map/ppermute | solution.py:400
  40.4 14.2 %collective-permute-start.5 = (bf16[128,2048]{1,0:T(8,128)(2,1)}, bf16[128,2048]{1,0:T(8,128)(2,1)S(1)}, u32[]{:S(2)}, u32[]{:S(2)}) collective-permute-start(bf16[128,2048]{1,0:T(8,128)(2,1)} %slice.20), channel_id=1, source_target_pairs={{0,16},{4,20},{8,24},{12,28},{16,0},{20,4},{24,8},{28,12},{1,17},{... | collective-permute-start | bytes 1572872 | tf_op jit(solution)/shard_map/ppermute | solution.py:400
  41.9 14.0 %collective-permute-start.6 = (bf16[128,2048]{1,0:T(8,128)(2,1)}, bf16[128,2048]{1,0:T(8,128)(2,1)}, u32[]{:S(2)}, u32[]{:S(2)}) collective-permute-start(bf16[128,2048]{1,0:T(8,128)(2,1)} %slice.21), channel_id=1, source_target_pairs={{0,8},{4,12},{8,0},{12,4},{16,24},{20,28},{24,16},{28,20},{1,9},{5... | collective-permute-start | bytes 1572872 | tf_op jit(solution)/shard_map/ppermute | solution.py:400
  59.0 19.9 %collective-permute-start.9 = (bf16[2048,512]{1,0:T(8,128)(2,1)}, bf16[2048,512]{1,0:T(8,128)(2,1)}, u32[]{:S(2)}, u32[]{:S(2)}) collective-permute-start(bf16[2048,512]{1,0:T(8,128)(2,1)} %all-gather.3.cloned.1.call-done.refs_10_.refs_0_), channel_id=1, source_target_pairs={{0,4},{4,0},{8,12},{12,8},{16,20},{20,16},{24,28},{28,24},{1,5},{5... | collective-permute-start | bytes 6291464 | tf_op jit(solution)/shard_map/ppermute | solution.py:400
  59.2 19.7 %all-to-all-start.1 = ((bf16[8,256,256]{2,1,0:T(8,128)(2,1)}), bf16[8,256,256]{2,1,0:T(8,128)(2,1)}, u32[]{:S(2)}, u32[]{:S(2)}) async-start(bf16[8,256,256]{2,1,0:T(8,128)(2,1)} %bitcast.16), calls=%async_computation.1 | async-start | bytes 2097152 | tf_op jit(solution)/shard_map/all_to_all | solution.py:578
  78.9 18.9 %all-to-all-start.2 = ((bf16[8,256,256]{2,1,0:T(8,128)(2,1)}), bf16[8,256,256]{2,1,0:T(8,128)(2,1)S(1)}, u32[]{:S(2)}, u32[]{:S(2)}) async-start(bf16[8,256,256]{2,1,0:T(8,128)(2,1)} %bitcast.27), calls=%async_computation.2 | async-start | bytes 2097152 | tf_op jit(solution)/shard_map/all_to_all | solution.py:605
  97.8 18.9 %all-to-all-start.3 = ((bf16[8,32,2048]{2,1,0:T(8,128)(2,1)}), bf16[8,32,2048]{2,1,0:T(8,128)(2,1)S(1)}, u32[]{:S(2)}, u32[]{:S(2)}) async-start(bf16[8,32,2048]{2,1,0:T(8,128)(2,1)} %bitcast.26), calls=%async_computation.3 | async-start | bytes 2097152 | tf_op jit(solution)/shard_map/all_to_all | solution.py:646
  101.4 42.1 %reduce-scatter.2.cloned.1.call-start = ((), (), s32[]{:S(2)}) async-start(), calls=%async_computation.9 | async-start | bytes 1310720 | tf_op jit(solution)/shard_map/reduce_scatter | solution.py:648
  116.7 26.8 %collective-permute-start.13 = (bf16[2048,512]{1,0:T(8,128)(2,1)}, bf16[2048,512]{1,0:T(8,128)(2,1)}, u32[]{:S(2)}, u32[]{:S(2)}) collective-permute-start(bf16[2048,512]{1,0:T(8,128)(2,1)} %all-gather.5.cloned.1.call-done.refs_2_), channel_id=1, source_target_pairs={{0,4},{4,0},{8,12},{12,8},{16,20},{20,16},{24,28},{28,24},{1,5},{5... | collective-permute-start | bytes 6291464 | tf_op jit(solution)/shard_map/ppermute | solution.py:400
  116.7 14.7 %collective-permute-start.16 = (bf16[2048,128]{1,0:T(8,128)(2,1)S(1)}, bf16[2048,128]{1,0:T(8,128)(2,1)S(1)}, u32[]{:S(2)}, u32[]{:S(2)}) collective-permute-start(bf16[2048,128]{1,0:T(8,128)(2,1)S(1)} %slice.23), channel_id=1, source_target_pairs={{0,16},{4,20},{8,24},{12,28},{16,0},{20,4},{24,8},{28,12},{1,17},{... | collective-permute-start | bytes 1572872 | tf_op jit(solution)/shard_map/ppermute | solution.py:400
  117.2 14.8 %collective-permute-start.14 = (bf16[2048,128]{1,0:T(8,128)(2,1)S(1)}, bf16[2048,128]{1,0:T(8,128)(2,1)S(1)}, u32[]{:S(2)}, u32[]{:S(2)}) collective-permute-start(bf16[2048,128]{1,0:T(8,128)(2,1)S(1)} %slice.23), channel_id=1, source_target_pairs={{0,8},{4,12},{8,0},{12,4},{16,24},{20,28},{24,16},{28,20},{1,9},{5... | collective-permute-start | bytes 1572872 | tf_op jit(solution)/shard_map/ppermute | solution.py:400
  120.7 24.8 %all-to-all-start.4 = ((bf16[8,288,256]{2,1,0:T(8,128)(2,1)}), bf16[8,288,256]{2,1,0:T(8,128)(2,1)S(1)}, u32[]{:S(2)}, u32[]{:S(2)}) async-start(bf16[8,288,256]{2,1,0:T(8,128)(2,1)} %get-tuple-element.162), calls=%async_computation.5 | async-start | bytes 2359296 | tf_op jit(solution)/shard_map/all_to_all | solution.py:667
  131.4 11.2 %collective-permute-start.17 = (bf16[2048,128]{1,0:T(8,128)(2,1)S(1)}, bf16[2048,128]{1,0:T(8,128)(2,1)S(1)}, u32[]{:S(2)}, u32[]{:S(2)}) collective-permute-start(bf16[2048,128]{1,0:T(8,128)(2,1)S(1)} %collective-permute-done.16.refs_4_), channel_id=1, source_target_pairs={{0,4},{4,0},{8,12},{12,8},{16,20},{20,16},{24,28},{28,24},{1,5},{5... | collective-permute-start | bytes 1572872 | tf_op jit(solution)/shard_map/ppermute | solution.py:400
  132.0 11.5 %collective-permute-start.15 = (bf16[2048,128]{1,0:T(8,128)(2,1)S(1)}, bf16[2048,128]{1,0:T(8,128)(2,1)S(1)}, u32[]{:S(2)}, u32[]{:S(2)}) collective-permute-start(bf16[2048,128]{1,0:T(8,128)(2,1)S(1)} %collective-permute-done.14.refs_3_), channel_id=1, source_target_pairs={{0,4},{4,0},{8,12},{12,8},{16,20},{20,16},{24,28},{28,24},{1,5},{5... | collective-permute-start | bytes 1572872 | tf_op jit(solution)/shard_map/ppermute | solution.py:400
  133.6 8.5 %collective-permute-start.11 = (bf16[8,16,128]{2,1,0:T(8,128)(2,1)}, bf16[8,16,128]{2,1,0:T(8,128)(2,1)S(1)}, u32[]{:S(2)}, u32[]{:S(2)}) collective-permute-start(bf16[8,16,128]{2,1,0:T(8,128)(2,1)} %get-tuple-element.155), channel_id=1, source_target_pairs={{0,2},{1,3},{2,0},{3,1},{4,6},{5,7},{6,4},{7,5},{8,10},{9,11},{10,... | collective-permute-start | bytes 98312 | tf_op jit(solution)/shard_map/ppermute | solution.py:400
  136.7 5.9 %collective-permute-start.12 = (bf16[8,16,128]{2,1,0:T(8,128)(2,1)}, bf16[8,16,128]{2,1,0:T(8,128)(2,1)S(1)}, u32[]{:S(2)}, u32[]{:S(2)}) collective-permute-start(bf16[8,16,128]{2,1,0:T(8,128)(2,1)} %get-tuple-element.156), channel_id=1, source_target_pairs={{0,3},{1,2},{2,1},{3,0},{4,7},{5,6},{6,5},{7,4},{8,11},{9,10},{10,... | collective-permute-start | bytes 98312 | tf_op jit(solution)/shard_map/ppermute | solution.py:400
  145.5 11.1 %all-to-all-start.5 = ((bf16[8,80,256]{2,1,0:T(8,128)(2,1)}), bf16[8,80,256]{2,1,0:T(8,128)(2,1)S(1)}, u32[]{:S(2)}, u32[]{:S(2)}) async-start(bf16[8,80,256]{2,1,0:T(8,128)(2,1)} %shard_map.75), calls=%async_computation.6 | async-start | bytes 655360 | tf_op jit(solution)/shard_map/all_to_all | solution.py:736
  (22 other events, 141.4 us)
Sparse Core Ops, SparseCore 0:
  9.6 48.4 all-gather.2
  59.6 45.7 all-gather.4
  109.0 28.7 reduce-scatter.1
